TPU v7x, 32 devices: a whole 2x2x4 slice. The times are simulated.
32 devices in a mesh: groups: 2 (over x), section: 16 (over z, y, core).
Axes of the slice: x: 2, y: 2, z: 4, core: 2. Of those that a mesh axis runs over, the one named last changes fastest.
Arguments:
- enc_rows: bfloat16 [2048, 6144], P('groups', 'section'), parts along dimension 0, may hold values from -6 to 6
- enc_gain: float32 [6144], replicated, may hold values from 0.5 to 1.5
- dec_input: bfloat16 [256, 6144], P('groups'), parts along dimension 0, may hold values from -6 to 6
- dec_gain: float32 [1, 6144], replicated, may hold values from 0.5 to 1.5
- w_query: bfloat16 [64, 6144, 128], P('section'), may hold values from -0.3125 to 0.3125
- w_keyval: bfloat16 [64, 6144, 256], P('section'), may hold values from -0.078125 to 0.078125
- w_out: bfloat16 [64, 128, 6144], P('section'), may hold values from -0.09375 to 0.09375
Outputs:
- decoded: bfloat16 [256, 6144], P('groups', 'section'), parts along dimension 0
There are 2 independent parts, one for each index of `groups`. A program takes and returns all parts, laid end to end along the dimension named above; an argument that names none is the same for every part. Nothing has to cross between parts.
All inputs are finite; a program needn't handle non-finite values.
Results may differ from a plain program's by a relative error of at most 0.012.
Values may be sent and summed in bfloat16 or wider, within the bound.
No kernel may reach another device: no remote copies, remote signals or barrier semaphores. Data moves between devices by JAX's collectives and lax.ppermute only.
A program may use at most 128 MiB of HBM per device.

v0:
```python
import math

import jax
import jax.numpy as jnp
from jax import lax
from jax.sharding import PartitionSpec as P

epsilon = 1e-06


def rms_scaled(values, gain):
    return values * lax.rsqrt(jnp.mean(values * values, axis=-1, keepdims=True) + epsilon) * gain


def body(enc_rows, enc_gain, dec_input, dec_gain, w_query, w_keyval, w_out):
    sections = lax.axis_size("section")
    position = lax.axis_index("section")
    layers = dec_gain.shape[0]
    target_rows = dec_input.shape[0]
    model_width = dec_input.shape[1]
    head_size = w_query.shape[2]
    score_scale = 1.0 / math.sqrt(head_size)
    my_layer = position // (sections // layers)
    whole_rows = lax.all_gather(enc_rows, "section", axis=1, tiled=True)
    encoded = rms_scaled(whole_rows.astype(jnp.float32), enc_gain).astype(jnp.bfloat16)
    keyvals = jnp.einsum(
        "rd,hdk->rhk", encoded, w_keyval, preferred_element_type=jnp.float32
    ).astype(jnp.bfloat16)
    key_rows = keyvals[:, :, :head_size]
    value_rows = keyvals[:, :, head_size:]

    def head_context(normed):
        queries = (
            jnp.einsum("td,hdk->htk", normed, w_query, preferred_element_type=jnp.float32)
            * score_scale
        ).astype(jnp.bfloat16)
        scores = jnp.einsum("htk,rhk->htr", queries, key_rows, preferred_element_type=jnp.float32)
        weights_bf = jax.nn.softmax(scores, axis=-1).astype(jnp.bfloat16)
        return jnp.einsum(
            "htr,rhk->htk", weights_bf, value_rows, preferred_element_type=jnp.float32
        ).astype(jnp.bfloat16)

    col_share = model_width // sections
    col_start = position * col_share
    state_share = lax.dynamic_slice_in_dim(dec_input, col_start, col_share, 1).astype(jnp.float32)
    for layer_idx in range(layers):
        squares = lax.psum(jnp.sum(state_share * state_share, axis=1), "section")
        gain_share = lax.dynamic_slice_in_dim(dec_gain[layer_idx], col_start, col_share, 0)
        inverse = lax.rsqrt(squares / model_width + epsilon)
        normed_share = (state_share * inverse[:, None] * gain_share).astype(jnp.bfloat16)
        normed = lax.all_gather(normed_share, "section", axis=1, tiled=True)

        def project(normed_in):
            return jnp.einsum(
                "htk,hkd->td", head_context(normed_in), w_out, preferred_element_type=jnp.float32
            )

        def skipped(normed_in):
            return jnp.zeros((target_rows, model_width), jnp.float32)

        state_share = state_share + lax.psum_scatter(
            lax.cond(my_layer == layer_idx, project, skipped, normed),
            "section",
            scatter_dimension=1,
            tiled=True,
        )
    decoded = state_share.astype(jnp.bfloat16)
    return decoded


def solution(mesh):
    in_specs = (
        P("groups", "section"),
        P(),
        P("groups", None),
        P(),
        P("section", None, None),
        P("section", None, None),
        P("section", None, None),
    )
    out_specs = P("groups", "section")
    return jax.shard_map(body, mesh=mesh, in_specs=in_specs, out_specs=out_specs, check_vma=False)
```

profile of v0, /device:TPU:0, one launch (start us, length us, event | category | flops | bytes accessed | tf_op | source)
XLA Modules:
  0.0 247.7 jit_solution(8770332978571581930)
XLA Ops:
  6.5 0.0 copy-start
  6.5 0.0 all-gather.5.cloned.1.call-start
  6.5 0.7 all-gather.5.cloned.1.call-update
  7.3 0.0 all-gather.3.cloned.1.call-start
  7.3 0.0 copy-done
  7.3 1.0 fusion.31
  8.4 35.7 %psum.7 = f32[128]{0:T(128)S(1)} all-reduce(f32[128]{0:T(128)S(1)} %fusion.31), channel_id=1, replica_groups=mesh['groups'=2,'section'=16] {'section'}, use_global_device_ids=true, to_apply=%region_1.2 | all-reduce | flops 128 | bytes 1024 | tf_op jit(solution)/shard_map/psum | solution.py:47
  44.0 1.6 fusion.33
  45.7 0.0 all-gather.3.cloned.1.call-update
  45.7 0.0 reduce-scatter.2.cloned.1.call-start
  45.7 0.0 copy-start.4
  45.8 70.7 %all-gather.5.cloned.1.call-done = bf16[1024,6144]{1,0:T(8,128)(2,1)} async-done(((bf16[1024,384]{1,0:T(8,128)(2,1)}), bf16[1024,6144]{1,0:T(8,128)(2,1)}) %all-gather.5.cloned.1.call-update) | async-done | bytes 12582928 | tf_op jit(solution)/shard_map/all_gather | solution.py:24
  116.5 7.1 %fusion.20 = f32[1024]{0:T(1024)S(1)} fusion(bf16[1024,6144]{1,0:T(8,128)(2,1)} %all-gather.5.cloned.1.call-done), kind=kLoop, calls=%fused_computation.17 | loop fusion | flops 18873344 | bytes 12587008 | tf_op jit(solution)/shard_map/reduce_sum | solution.py:12
  123.6 0.0 copy-done.4
  123.6 18.8 %fusion.28 = bf16[1024,4,256]{2,0,1:T(8,128)(2,1)} fusion(bf16[4,6144,256]{2,1,0:T(8,128)(2,1)} %param.14, bf16[1024,6144]{1,0:T(8,128)(2,1)} %all-gather.5.cloned.1.call-done, f32[6144]{0:T(1024)S(1)} %copy-done.4, f32[1024]{0:T(1024)S(1)} %add_rsqrt_fusion), kind=kOutput, calls=%fused_computation.24 | convolution fusion | flops 12911116288 | bytes 27291648 | tf_op jit(solution)/shard_map/rd,hdk->rhk/dot_general | solution.py:26
  142.4 13.4 %all-gather.3.cloned.1.call-done = bf16[128,6144]{1,0:T(8,128)(2,1)} async-done(((bf16[128,384]{1,0:T(8,128)(2,1)}), bf16[128,6144]{1,0:T(8,128)(2,1)}) %all-gather.3.cloned.1.call-update) | async-done | bytes 1572880 | tf_op jit(solution)/shard_map/all_gather | solution.py:51
  155.8 16.5 %conditional.1 = (f32[128,6144]{1,0:T(8,128)S(1)}) conditional(s32[]{:T(128)} %convert_element_type.32, () %tuple.11, (bf16[4,6144,128]{2,1,0:T(8,128)(2,1)}, bf16[128,6144]{1,0:T(8,128)(2,1)}, bf16[1024,4,256]{2,0,1:T(8,128)(2,1)}, bf16[1024,4,256]{2,0,1:T(8,128)(2,1)}, bf16[4,128,6144]{2,1,0:T(8,128)(2,1)}) %tuple.12), branch_computations={%region_3.4_spmd, %region_4.7_spmd} | conditional | flops 1881868800 | bytes 48762944 | solution.py:62
  155.8 4.8 %fusion.10 = f32[4,128,1024]{2,1,0:T(8,128)S(1)} fusion(bf16[4,6144,128]{2,1,0:T(8,128)(2,1)} %get-tuple-element.27, bf16[128,6144]{1,0:T(8,128)(2,1)} %get-tuple-element.19, bf16[1024,4,256]{2,0,1:T(8,128)(2,1)} %get-tuple-element.32), kind=kOutput, calls=%fused_computation.8 | convolution fusion | flops 939655168 | bytes 11010048 | tf_op jit(solution)/shard_map/cond/branch_1_fun/htk,rhk->htr/dot_general | solution.py:37
  160.7 0.0 copy-start.2
  160.7 0.0 copy-start.3
  160.7 0.5 fusion.35
  161.2 1.8 copy-done.3
  163.0 1.6 copy.10
  164.7 0.0 copy-done.2
  164.7 1.3 slice.10
  166.0 6.3 %convolution_bitcast_fusion = f32[128,6144]{1,0:T(8,128)S(1)} fusion(bf16[4,128,6144]{2,1,0:T(8,128)(2,1)} %get-tuple-element.28, bf16[1024,4,128]{2,1,0:T(4,128)(2,1)} %slice.10, f32[4,128]{1,0:T(4,128)S(1)} %fusion.35, f32[4,128,1024]{2,1,0:T(8,128)} %copy-done.2), kind=kOutput, calls=%fused_computation.1 | convolution fusion | flops 941164032 | bytes 12584960 | tf_op jit(solution)/shard_map/cond/branch_1_fun/htk,hkd->td/dot_general | solution.py:54
  172.4 0.0 copy-start.1
  172.4 1.7 copy-done.1
  174.0 0.0 reduce-scatter.2.cloned.1.call-update
  174.1 65.5 %reduce-scatter.2.cloned.1.call-done = f32[128,384]{1,0:T(8,128)} async-done(((f32[128,6144]{1,0:T(8,128)}), f32[128,384]{1,0:T(8,128)}) %reduce-scatter.2.cloned.1.call-update) | async-done | bytes 196624 | tf_op jit(solution)/shard_map/reduce_scatter | solution.py:61
  239.5 1.6 fusion.34
  (3 shorter events, 0.0 us)
Async XLA Ops:
  6.5 0.8 copy-start
  6.5 109.9 %all-gather.5.cloned.1.call-start = ((), (), s32[]{:S(2)}) async-start(), calls=%async_computation.2 | async-start | bytes 13369344 | tf_op jit(solution)/shard_map/all_gather | solution.py:24
  7.3 148.6 %all-gather.3.cloned.1.call-start = ((), (), s32[]{:S(2)}) async-start(), calls=%async_computation.1 | async-start | bytes 1671168 | tf_op jit(solution)/shard_map/all_gather | solution.py:51
  45.7 193.8 %reduce-scatter.2.cloned.1.call-start = ((), (), s32[]{:S(2)}) async-start(), calls=%async_computation.3 | async-start | bytes 3342336 | tf_op jit(solution)/shard_map/reduce_scatter | solution.py:61
  45.7 77.8 %copy-start.4 = (f32[6144]{0:T(1024)S(1)}, f32[6144]{0:T(1024)}, u32[]{:S(2)}) copy-start(f32[6144]{0:T(1024)} %param.10) | copy-start | bytes 73732
  160.7 4.0 %copy-start.2 = (f32[4,128,1024]{2,1,0:T(8,128)}, f32[4,128,1024]{2,1,0:T(8,128)S(1)}, u32[]{:S(2)}) copy-start(f32[4,128,1024]{2,1,0:T(8,128)S(1)} %fusion.10) | copy-start | bytes 6291460 | tf_op jit(solution)/shard_map/cond
  160.7 2.3 copy-start.3
  172.4 1.7 copy-start.1
Sparse Core Ops, SparseCore 0:
  9.5 106.8 all-gather.4
  118.6 37.1 all-gather.2
  174.2 65.3 reduce-scatter.1
where the time goes:
time: 248 us
  waiting for transfers between devices  150 us (60%)
  blocking collectives  35.7 us (14%)
  matrix products  30 us (12%)
  between operations  13.2 us (5%)
  other arithmetic  11.9 us (5%)
  local copies, waits for them, and re-layouts  6.5 us (3%)
    all_gather x1, waiting for transfers between devices, body(): whole_rows = lax.all_gather(enc_rows, 'section', axis=1, tiled=True)  70.7 us
    reduce_scatter x1, waiting for transfers between devices, body(): lax.psum_scatter(lax.cond(my_layer == layer_idx, project, skipped, normed...  65.5 us
    psum x1, blocking collectives, body(): squares = lax.psum(jnp.sum(state_share * state_share, axis=1), 'section')  35.7 us
    dot_general x1, matrix products, body(): jnp.einsum('rd,hdk->rhk', encoded, w_keyval, preferred_element_type=jnp.f...  18.8 us
    all_gather x1, waiting for transfers between devices, body(): normed = lax.all_gather(normed_share, 'section', axis=1, tiled=True)  13.4 us
    reduce_sum x1, other arithmetic, rms_scaled(): jnp.mean(values * values, axis=-1, keepdims=True) + epsilon  7.08 us
    dot_general x1, matrix products, project(): jnp.einsum('htk,hkd->td', head_context(normed_in), w_out, preferred_eleme...  6.34 us
  transfers between devices with their start and end apart: 3, of which 3 were waited for; matrix products, arithmetic and copies ran while one was open for 12% of the time, Pallas kernels for 0%

commit v1 on v0

--- a/solution.py
+++ b/solution.py
@@ -1,18 +1,402 @@
+import functools
 import math
 
 import jax
 import jax.numpy as jnp
+import numpy as np
 from jax import lax
+from jax.experimental import pallas as pl
+from jax.experimental.pallas import tpu as pltpu
 from jax.sharding import PartitionSpec as P
 
 epsilon = 1e-06
+MAX_RING = 8
+VMEM_MIB = 60
+STEP_MIB = 48
+TILE = 16
 
 
 def rms_scaled(values, gain):
     return values * lax.rsqrt(jnp.mean(values * values, axis=-1, keepdims=True) + epsilon) * gain
 
 
-def body(enc_rows, enc_gain, dec_input, dec_gain, w_query, w_keyval, w_out):
+def ring_order(chips):
+    return list(range(0, chips, 2)) + list(range(1, chips, 2))[::-1]
+
+
+def params(mib):
+    return pltpu.CompilerParams(vmem_limit_bytes=mib * 2**20)
+
+
+def anywhere(count):
+    return [pl.BlockSpec(memory_space=pl.ANY)] * count
+
+
+def prepare_kernel(rows_ref, gain_ref, *halves):
+    cols = rows_ref.shape[1]
+    for which, half_ref in enumerate(halves):
+        rows = half_ref.shape[0] - TILE
+        values = rows_ref[which * rows : (which + 1) * rows, :].astype(jnp.float32)
+        half_ref[:rows, :] = (values * gain_ref[...]).astype(jnp.bfloat16)
+        squares = values * values
+        high = squares.astype(jnp.bfloat16)
+        low = (squares - high.astype(jnp.float32)).astype(jnp.bfloat16)
+        ones = jnp.ones((8, cols), jnp.bfloat16)
+        sums = sum(
+            lax.dot_general(ones, part, (((1,), (1,)), ((), ())), preferred_element_type=jnp.float32)
+            for part in (high, low)
+        )[:1]
+        terms = []
+        for _ in range(3):
+            terms.append(sums.astype(jnp.bfloat16).astype(jnp.float32))
+            sums = sums - terms[-1]
+        per = -(-rows // cols)
+        lines = []
+        for term in terms:
+            for line in range(per):
+                part = term[:, line * cols : min(rows, (line + 1) * cols)]
+                if part.shape[1] < cols:
+                    part = jnp.concatenate([part, jnp.zeros((1, cols - part.shape[1]), jnp.float32)], axis=1)
+                lines.append(part)
+        lines.append(jnp.zeros((TILE - len(lines), cols), jnp.float32))
+        half_ref[rows:, :] = jnp.concatenate(lines, axis=0).astype(jnp.bfloat16)
+
+
+def prepare(enc_rows, gain_share):
+    rows, cols = enc_rows.shape
+    return pl.pallas_call(
+        prepare_kernel,
+        out_shape=[jax.ShapeDtypeStruct((rows // 2 + TILE, cols), jnp.bfloat16)] * 2,
+        compiler_params=params(VMEM_MIB),
+        name="prepare",
+    )(enc_rows, gain_share[None, :])
+
+
+def lane_sums(tile, rows):
+    cols = tile.shape[1]
+    per = -(-rows // cols)
+    lines = []
+    for line in range(per):
+        term = sum(tile[k * per + line : k * per + line + 1, :] for k in range(3))
+        lines.append(term[:, : min(cols, rows - line * cols)])
+    return jnp.concatenate(lines, axis=1)
+
+
+def start_blocks(index_ref, slots, pieces, w_ref, rows_at, tiles, weights, rows_sem, tiles_sem, weights_sem):
+    heads = weights.shape[0]
+    rows, features = rows_at.shape[0], tiles.shape[2]
+    row_copies, tile_copies, weight_copies = [], [], []
+    for slot in range(slots):
+        columns = pl.ds(slot * features, features)
+        at = 0
+        for piece in pieces[slot]:
+            size = min(piece.shape[0], rows - at)
+            source = piece.at[pl.ds(0, size), :]
+            target = rows_at.at[pl.ds(at, size), columns]
+            row_copies.append(pltpu.make_async_copy(source, target, rows_sem.at[len(row_copies)]))
+            at += size
+        source = pieces[slot][-1].at[pl.ds(pieces[slot][-1].shape[0] - TILE, TILE), :]
+        tile_copies.append(pltpu.make_async_copy(source, tiles.at[slot], tiles_sem.at[slot]))
+    for head in range(heads):
+        group = []
+        for slot in range(slots):
+            source = w_ref.at[head, pl.ds(pl.multiple_of(index_ref[slot] * features, features), features), :]
+            target = weights.at[head, pl.ds(slot * features, features), :]
+            group.append(pltpu.make_async_copy(source, target, weights_sem.at[head, slot]))
+        weight_copies.append(group)
+    return row_copies, tile_copies, weight_copies
+
+
+def block_scratch(slots, rows, features, heads, pair):
+    pieces = sum(slots)
+    return [
+        pltpu.VMEM((rows, features * len(slots)), jnp.bfloat16),
+        pltpu.VMEM((len(slots), TILE, features), jnp.bfloat16),
+        pltpu.VMEM((heads, features * len(slots), pair), jnp.bfloat16),
+        pltpu.SemaphoreType.DMA((pieces,)),
+        pltpu.SemaphoreType.DMA((len(slots),)),
+        pltpu.SemaphoreType.DMA((heads, len(slots))),
+    ]
+
+
+def start_all(copies):
+    for copy in copies:
+        copy.start()
+
+
+def wait_all(copies):
+    for copy in copies:
+        copy.wait()
+
+
+def sum_kernel(slots, first, index_ref, *refs):
+    refs = list(refs)
+    pieces = [[refs.pop(0) for _ in range(count)] for count in slots]
+    w_ref = refs.pop(0)
+    sum_in, tile_in = (None, None) if first else (refs.pop(0), refs.pop(0))
+    sum_out, tile_out, rows_at, tiles, weights, rows_sem, tiles_sem, weights_sem = refs
+    heads = weights.shape[0]
+    row_copies, tile_copies, weight_copies = start_blocks(
+        index_ref, len(slots), pieces, w_ref, rows_at, tiles, weights, rows_sem, tiles_sem, weights_sem
+    )
+    start_all(row_copies)
+    start_all(weight_copies[0])
+    start_all(tile_copies)
+    wait_all(row_copies)
+    for head in range(heads):
+        if head + 1 < heads:
+            start_all(weight_copies[head + 1])
+        wait_all(weight_copies[head])
+        term = jnp.dot(rows_at[...], weights[head], preferred_element_type=jnp.float32)
+        sum_out[head] = term if first else sum_in[head] + term
+    wait_all(tile_copies)
+    squares = sum(tiles[slot].astype(jnp.float32) for slot in range(len(slots)))
+    tile_out[...] = squares if first else tile_in[...] + squares
+
+
+def sum_step(index, slots, w_keyval, rows, carried=None):
+    heads, width, pair = w_keyval.shape
+    features = slots[0][0].shape[1]
+    counts = tuple(len(parts) for parts in slots)
+    pieces = [piece for parts in slots for piece in parts]
+    operands = pieces + [w_keyval] + list(carried or ())
+    whole = pl.BlockSpec(memory_space=pltpu.VMEM)
+    depth = features * len(slots)
+    aliases = {} if carried is None else {len(pieces) + 2: 0, len(pieces) + 3: 1}
+    return pl.pallas_call(
+        functools.partial(sum_kernel, counts, carried is None),
+        out_shape=[pltpu.VMEM((heads, rows, pair), jnp.float32), pltpu.VMEM((TILE, features), jnp.float32)],
+        grid_spec=pltpu.PrefetchScalarGridSpec(
+            num_scalar_prefetch=1,
+            grid=(),
+            in_specs=anywhere(len(pieces) + 1) + [whole] * (len(operands) - len(pieces) - 1),
+            out_specs=[whole] * 2,
+            scratch_shapes=block_scratch(counts, rows, features, heads, pair),
+        ),
+        input_output_aliases=aliases,
+        compiler_params=params(STEP_MIB),
+        cost_estimate=pl.CostEstimate(
+            flops=2 * rows * depth * heads * pair, bytes_accessed=2 * depth * heads * pair, transcendentals=0
+        ),
+        name="sum_step",
+    )(index, *operands)
+
+
+def attend_kernel(slots, merging, width, index_ref, *refs):
+    refs = list(refs)
+    pieces = [[refs.pop(0) for _ in range(count)] for count in slots]
+    w_ref, sum_in, tile_in, query_ref = [refs.pop(0) for _ in range(4)]
+    if merging:
+        context_in, top_in, total_in, w_out_ref = [refs.pop(0) for _ in range(4)]
+        theirs_ref, mine_ref = refs.pop(0), refs.pop(0)
+    else:
+        context_out, top_out, total_out = [refs.pop(0) for _ in range(3)]
+    rows_at, tiles, weights, rows_sem, tiles_sem, weights_sem = [refs.pop(0) for _ in range(6)]
+    heads, rows, pair = sum_in.shape
+    size = pair // 2
+    row_copies, tile_copies, weight_copies = start_blocks(
+        index_ref, len(slots), pieces, w_ref, rows_at, tiles, weights, rows_sem, tiles_sem, weights_sem
+    )
+    start_all(row_copies)
+    start_all(tile_copies)
+    for head in range(heads):
+        start_all(weight_copies[head])
+    if merging:
+        w_out_at, out_sem, merged = refs
+        out_copies = [
+            pltpu.make_async_copy(w_out_ref.at[head], w_out_at.at[head], out_sem.at[head]) for head in range(heads)
+        ]
+        start_all(out_copies)
+    wait_all(tile_copies)
+    squares = sum((tiles[slot].astype(jnp.float32) for slot in range(len(slots))), tile_in[...])
+    inverse = lax.rsqrt(lane_sums(squares, rows) / width + epsilon)
+    wait_all(row_copies)
+    for head in range(heads):
+        wait_all(weight_copies[head])
+        keyvals = (
+            sum_in[head] + jnp.dot(rows_at[...], weights[head], preferred_element_type=jnp.float32)
+        ).astype(jnp.bfloat16)
+        scores = inverse * lax.dot_general(
+            query_ref[head], keyvals[:, :size], (((1,), (1,)), ((), ())), preferred_element_type=jnp.float32
+        )
+        top = jnp.max(scores, axis=1, keepdims=True)
+        weight = jnp.exp(scores - top)
+        norm = jnp.sum(weight, axis=1, keepdims=True)
+        context = jnp.dot(
+            (weight * inverse).astype(jnp.bfloat16), keyvals[:, size:], preferred_element_type=jnp.float32
+        )
+        if not merging:
+            context_out[head] = context
+            top_out[head] = jnp.broadcast_to(top, top_out.shape[1:])
+            total_out[head] = jnp.broadcast_to(norm, total_out.shape[1:])
+            continue
+        other_top, other_norm = top_in[head][:, :1], total_in[head][:, :1]
+        highest = jnp.maximum(top, other_top)
+        left, right = jnp.exp(top - highest), jnp.exp(other_top - highest)
+        whole = left * norm + right * other_norm
+        joined = context * (left / whole) + context_in[head] * (right / whole)
+        merged[:, head * size : (head + 1) * size] = joined.astype(jnp.bfloat16)
+    if not merging:
+        return
+    wait_all(out_copies)
+    count, _, cols = mine_ref.shape
+    for part, target in enumerate((theirs_ref, mine_ref)):
+        @pl.loop(0, count)
+        def _(step):
+            block = index_ref[len(slots) + part * count + step]
+            columns = pl.ds(pl.multiple_of(block * cols, cols), cols)
+            out_part = w_out_at[:, :, columns].reshape(heads * size, cols)
+            value = jnp.dot(merged[...], out_part, preferred_element_type=jnp.float32)
+            target[step] = value.astype(target.dtype)
+
+
+def attend(index, slots, w_keyval, carried, queries, other=None, w_out=None, blocks=0, cols=0):
+    heads, width, pair = w_keyval.shape
+    rows = carried[0].shape[1]
+    features = slots[0][0].shape[1]
+    counts = tuple(len(parts) for parts in slots)
+    target, size = queries.shape[1:]
+    pieces = [piece for parts in slots for piece in parts]
+    operands = pieces + [w_keyval, *carried, queries]
+    whole = pl.BlockSpec(memory_space=pltpu.VMEM)
+    in_specs = anywhere(len(pieces) + 1) + [whole] * 3
+    depth = features * len(slots)
+    scratch = block_scratch(counts, rows, features, heads, pair)
+    merging = other is not None
+    if merging:
+        operands += list(other) + [w_out]
+        in_specs += [whole] * 3 + anywhere(1)
+        scratch += [
+            pltpu.VMEM(w_out.shape, w_out.dtype),
+            pltpu.SemaphoreType.DMA((heads,)),
+            pltpu.VMEM((target, heads * size), jnp.bfloat16),
+        ]
+        out_shape = [
+            jax.ShapeDtypeStruct((blocks, target, cols), jnp.bfloat16),
+            pltpu.VMEM((blocks, target, cols), jnp.float32),
+        ]
+    else:
+        out_shape = [pltpu.VMEM((heads, target, last), jnp.float32) for last in (size, 128, 128)]
+    return pl.pallas_call(
+        functools.partial(attend_kernel, counts, merging, width),
+        out_shape=out_shape,
+        grid_spec=pltpu.PrefetchScalarGridSpec(
+            num_scalar_prefetch=1,
+            grid=(),
+            in_specs=in_specs,
+            out_specs=[whole] * len(out_shape),
+            scratch_shapes=scratch,
+        ),
+        compiler_params=params(STEP_MIB),
+        cost_estimate=pl.CostEstimate(
+            flops=2 * rows * depth * heads * pair, bytes_accessed=2 * depth * heads * pair, transcendentals=0
+        ),
+        name="attend",
+    )(index, *operands)
+
+
+def add_kernel(mine_ref, other_ref, *outs):
+    for block, out in enumerate(outs):
+        out[...] = (mine_ref[block] + other_ref[block].astype(jnp.float32)).astype(out.dtype)
+
+
+def add_blocks(mine, other):
+    count, target, cols = mine.shape
+    return pl.pallas_call(
+        add_kernel,
+        out_shape=[
+            jax.ShapeDtypeStruct((target, cols), jnp.float32 if block == 0 else jnp.bfloat16)
+            for block in range(count)
+        ],
+        compiler_params=params(VMEM_MIB),
+        name="add_blocks",
+    )(mine, other)
+
+
+def ring_body(enc_rows, enc_gain, dec_input, dec_gain, w_query, w_keyval, w_out):
+    sections = lax.axis_size("section")
+    position = lax.axis_index("section")
+    chips = sections // 2
+    ring = ring_order(chips)
+    place = {chip: k for k, chip in enumerate(ring)}
+    width = dec_input.shape[1]
+    cols = width // sections
+    head_size = w_query.shape[2]
+    score_scale = 1.0 / math.sqrt(head_size)
+    far = chips // 2
+
+    def at(chip, offset):
+        return ring[(place[chip] + offset) % chips]
+
+    def hop(values, offset):
+        pairs = [(2 * chip + core, 2 * at(chip, offset) + core) for chip in range(chips) for core in range(2)]
+        return lax.ppermute(values, "section", pairs)
+
+    def swap(values):
+        return lax.ppermute(values, "section", [(s, s ^ 1) for s in range(sections)])
+
+    table = []
+    for s in range(sections):
+        chip, core = divmod(s, 2)
+        row = [s, s ^ 1]
+        for step in range(1, far):
+            for side in (core, 1 - core):
+                row += [2 * at(chip, -step) + side, 2 * at(chip, step) + side]
+        row += [2 * at(chip, far) + core, 2 * at(chip, far) + 1 - core]
+        for side in (1 - core, core):
+            row += [2 * at(chip, k) + side for k in range(chips)]
+        table.append(row)
+    row = lax.dynamic_slice_in_dim(jnp.asarray(np.array(table, np.int32)), position, 1, 0)[0]
+    first_slot = [0] + [2 + 4 * step for step in range(far)]
+
+    half_rows = enc_rows.shape[0] // 2
+    own = prepare(enc_rows, lax.dynamic_slice_in_dim(enc_gain, position * cols, cols, 0))
+    state = dec_input.astype(jnp.float32)
+    normed = rms_scaled(state, dec_gain[0]).astype(jnp.bfloat16)
+    queries = (
+        jnp.einsum("td,hdk->htk", normed, w_query, preferred_element_type=jnp.float32) * score_scale
+    ).astype(jnp.bfloat16)
+
+    carried = [None, None]
+    slots = [[(half,), (swap(half),)] for half in own]
+    held = [(half, half) for half in own]
+    flying = [(hop(half, 1), hop(half, -1)) for half in own]
+    token = queries
+    for phase in range(2 * far):
+        step, which = phase // 2 + 1, phase % 2
+        *arrived, token = lax.optimization_barrier((*flying[phase], token))
+        if step + 1 < far:
+            flying.append((hop(arrived[0], 1), hop(arrived[1], -1)))
+        elif step + 1 == far:
+            cut = half_rows // 2
+            flying.append((hop(arrived[0][:cut], 1), hop(arrived[1][cut:], -1)))
+        other = [swap(part) for part in arrived]
+        if step < far:
+            received = [(part,) for part in arrived + other]
+        else:
+            received = [tuple(arrived), tuple(other)]
+        slots.append(received)
+        if phase == 0:
+            todo, half, begin = slots[0], 0, 0
+        elif phase == 2:
+            todo, half, begin = slots[1] + slots[3], 1, 0
+        else:
+            todo, half, begin = slots[phase + 1], 1 - which, first_slot[(phase + 1) // 2]
+        if phase < 2 * far - 1:
+            carried[half] = sum_step(row[begin : begin + len(todo)], todo, w_keyval, half_rows, carried[half])
+            token = carried[half][1]
+    last = first_slot[far]
+    first = attend(row[last : last + 2], slots[2 * far], w_keyval, carried[0], queries)
+    theirs, mine = attend(row[last:], slots[2 * far + 1], w_keyval, carried[1], queries, first, w_out, chips, cols)
+    blocks = add_blocks(mine, swap(theirs))
+    share = lax.dynamic_slice_in_dim(dec_input, position * cols, cols, 1).astype(jnp.float32)
+    total = share + blocks[0]
+    for k in range(1, chips):
+        total = total + hop(blocks[k], k).astype(jnp.float32)
+    return total.astype(jnp.bfloat16)
+
+
+def general_body(enc_rows, enc_gain, dec_input, dec_gain, w_query, w_keyval, w_out):
     sections = lax.axis_size("section")
     position = lax.axis_index("section")
     layers = dec_gain.shape[0]
@@ -50,7 +434,7 @@
         normed_share = (state_share * inverse[:, None] * gain_share).astype(jnp.bfloat16)
         normed = lax.all_gather(normed_share, "section", axis=1, tiled=True)
 
-        def project(normed_in):
+        def project_out(normed_in):
             return jnp.einsum(
                 "htk,hkd->td", head_context(normed_in), w_out, preferred_element_type=jnp.float32
             )
@@ -59,13 +443,19 @@
             return jnp.zeros((target_rows, model_width), jnp.float32)
 
         state_share = state_share + lax.psum_scatter(
-            lax.cond(my_layer == layer_idx, project, skipped, normed),
+            lax.cond(my_layer == layer_idx, project_out, skipped, normed),
             "section",
             scatter_dimension=1,
             tiled=True,
         )
-    decoded = state_share.astype(jnp.bfloat16)
-    return decoded
+    return state_share.astype(jnp.bfloat16)
+
+
+def body(enc_rows, enc_gain, dec_input, dec_gain, w_query, w_keyval, w_out):
+    chips, odd = divmod(lax.axis_size("section"), 2)
+    ringed = not odd and 4 <= chips <= MAX_RING and chips & (chips - 1) == 0 and dec_gain.shape[0] == 1
+    chosen = ring_body if ringed else general_body
+    return chosen(enc_rows, enc_gain, dec_input, dec_gain, w_query, w_keyval, w_out)
 
 
 def solution(mesh):

time: 248 us -> 142 us (0.57)
  waiting for transfers between devices: 150 us -> 25.2 us
  Pallas kernels: 0 us -> 62.5 us
  starting transfers between devices: 0.08 us -> 40.8 us
  blocking collectives: 35.7 us -> 0 us
  matrix products: 30 us -> 4.34 us
  between operations: 13.2 us -> 0.33 us
  other arithmetic: 11.9 us -> 3.55 us
    all_gather x2 -> x0, waiting for transfers between devices: 84.1 us -> none  [the longest x1 70.7 us: body(): whole_rows = lax.all_gather(enc_rows, 'section', axis=1, tiled=True)]
    reduce_scatter x1 -> x0, waiting for transfers between devices: 65.5 us -> none  [body(): lax.psum_scatter(lax.cond(my_layer == layer_idx, project, skipped, normed...]
    pallas_call x0 -> x11, Pallas kernels: none -> 62.5 us  [the longest x7 42.3 us: sum_step(): pl.pallas_call(functools.partial(sum_kernel, counts, carried is None), ou...]
    ppermute x0 -> x42, starting transfers between devices: none -> 40.8 us  [the longest x23 36.7 us: hop(): return lax.ppermute(values, 'section', pairs)]
    psum x1 -> x0, blocking collectives: 35.7 us -> none  [body(): squares = lax.psum(jnp.sum(state_share * state_share, axis=1), 'section')]
    dot_general x3 -> x1, matrix products: 30 us -> 4.34 us  [ring_body(): jnp.einsum('td,hdk->htk', normed, w_query, preferred_element_type=jnp.flo...]
    ppermute x0 -> x42, waiting for transfers between devices: none -> 25.2 us  [the longest x23 23 us: hop(): return lax.ppermute(values, 'section', pairs)]
    reduce_sum x1, other arithmetic: 7.08 us -> 1.79 us  [rms_scaled(): jnp.mean(values * values, axis=-1, keepdims=True) + epsilon]
  transfers between devices with their start and end apart: 3 -> 42, of which waited for: 3 -> 8; matrix products, arithmetic and copies ran while one was open for 12% -> 5% of each run, Pallas kernels for 0% -> 34%
where the time goes in v1:
time: 142 us; the launch traced here: 141 us
  Pallas kernels  62.5 us (44%)
  starting transfers between devices  40.8 us (29%)
  waiting for transfers between devices  25.2 us (18%)
  local copies, waits for them, and re-layouts  4.4 us (3%)
  matrix products  4.34 us (3%)
  other arithmetic  3.55 us (2%)
    pallas_call x7, Pallas kernels, sum_step(): pl.pallas_call(functools.partial(sum_kernel, counts, carried is None), ou...  42.3 us
    ppermute x23, starting transfers between devices, hop(): return lax.ppermute(values, 'section', pairs)  36.7 us
    ppermute x23, waiting for transfers between devices, hop(): return lax.ppermute(values, 'section', pairs)  23 us
    pallas_call x2, Pallas kernels, attend(): pl.pallas_call(functools.partial(attend_kernel, counts, merging, width),...  15.1 us
    dot_general x1, matrix products, ring_body(): jnp.einsum('td,hdk->htk', normed, w_query, preferred_element_type=jnp.flo...  4.34 us
    ppermute x19, starting transfers between devices, swap(): lax.ppermute(values, 'section', [(s, s ^ 1) for s in range(sections)])  4.12 us
  transfers between devices with their start and end apart: 42, of which 8 were waited for; matrix products, arithmetic and copies ran while one was open for 5% of the time, Pallas kernels for 34%

profile of v1, /device:TPU:0, one launch (start us, length us, event | category | flops | bytes accessed | tf_op | source)
XLA Modules:
  0.0 141.1 jit_solution(15921150676317697548)
XLA Ops:
  0.0 0.8 dynamic_slice.11
  0.8 0.6 broadcast_in_dim.4.gain_ref
  1.3 2.5 %prepare.1 = (bf16[528,384]{1,0:T(8,128)(2,1)}, bf16[528,384]{1,0:T(8,128)(2,1)}) custom-call(bf16[1024,384]{1,0:T(8,128)(2,1)} %rows_ref.1, f32[1,384]{1,0:T(1,128)} %broadcast_in_dim.4.gain_ref), custom_call_target="tpu_custom_call" | custom-call | tf_op jit(solution)/shard_map/prepare/pallas_call | solution.py:67
  3.9 3.0 %collective-permute-start = (bf16[528,384]{1,0:T(8,128)(2,1)}, bf16[528,384]{1,0:T(8,128)(2,1)S(1)}, u32[]{:S(2)}, u32[]{:S(2)}) collective-permute-start(bf16[528,384]{1,0:T(8,128)(2,1)} %get-tuple-element.50.refs_0_), channel_id=1, source_target_pairs={{0,4},{1,5},{2,0},{3,1},{4,8},{5,9},{6,2},{7,3},{8,12},{9,13},{10,... | collective-permute-start | bytes 1216520 | tf_op jit(solution)/shard_map/ppermute | solution.py:333
  6.9 2.0 %collective-permute-start.18 = (bf16[528,384]{1,0:T(8,128)(2,1)}, bf16[528,384]{1,0:T(8,128)(2,1)S(1)}, u32[]{:S(2)}, u32[]{:S(2)}) collective-permute-start(bf16[528,384]{1,0:T(8,128)(2,1)} %get-tuple-element.51.refs_0_), channel_id=1, source_target_pairs={{0,4},{1,5},{2,0},{3,1},{4,8},{5,9},{6,2},{7,3},{8,12},{9,13},{10,... | collective-permute-start | bytes 1216520 | tf_op jit(solution)/shard_map/ppermute | solution.py:333
  8.9 1.8 %fusion = f32[128]{0:T(128)S(1)} fusion(bf16[128,6144]{1,0:T(8,128)(2,1)} %param.10), kind=kLoop, calls=%fused_computation.2 | loop fusion | flops 2359168 | bytes 1573376 | tf_op jit(solution)/shard_map/reduce_sum | solution.py:20
  10.8 4.3 %fusion.14.refs_7_ = bf16[4,128,128]{2,1,0:T(8,128)(2,1)S(1)} fusion(bf16[4,6144,128]{2,1,0:T(8,128)(2,1)} %param.12, bf16[128,6144]{1,0:T(8,128)(2,1)} %param.10, f32[6144]{0:T(1024)S(1)} %bitcast.27, f32[128]{0:T(128)S(1)} %add_rsqrt_fusion), kind=kOutput, calls=%fused_computation.11 | convolution fusion | flops 808583168 | bytes 8020480 | tf_op jit(solution)/shard_map/td,hdk->htk/dot_general | solution.py:357
  15.1 10.0 %collective-permute-done.18.refs_0_ = bf16[528,384]{1,0:T(8,128)(2,1)S(1)} collective-permute-done((bf16[528,384]{1,0:T(8,128)(2,1)}, bf16[528,384]{1,0:T(8,128)(2,1)S(1)}, u32[]{:S(2)}, u32[]{:S(2)}) %collective-permute-start.18) | collective-permute-done | bytes 405536 | tf_op jit(solution)/shard_map/ppermute | solution.py:333
  25.1 1.5 %collective-permute-done.19.refs_1_ = bf16[528,384]{1,0:T(8,128)(2,1)S(1)} collective-permute-done((bf16[528,384]{1,0:T(8,128)(2,1)}, bf16[528,384]{1,0:T(8,128)(2,1)S(1)}, u32[]{:S(2)}, u32[]{:S(2)}) %collective-permute-start.19) | collective-permute-done | bytes 405536 | tf_op jit(solution)/shard_map/ppermute | solution.py:333
  26.6 0.5 collective-permute-start.23
  27.1 0.7 constant_dynamic-slice_fusion
  27.9 1.6 %collective-permute-start.20 = (bf16[528,384]{1,0:T(8,128)(2,1)S(1)}, bf16[528,384]{1,0:T(8,128)(2,1)S(1)}, u32[]{:S(2)}, u32[]{:S(2)}) collective-permute-start(bf16[528,384]{1,0:T(8,128)(2,1)S(1)} %collective-permute-done.18.refs_0_), channel_id=1, source_target_pairs={{0,4},{1,5},{2,0},{3,1},{4,8},{5,9},{6,2},{7,3},{8,12},{9,13},{10,... | collective-permute-start | bytes 1216520 | tf_op jit(solution)/shard_map/ppermute | solution.py:333
  29.5 4.1 %sum_step.7 = (f32[4,512,256]{2,1,0:T(8,128)S(1)}, f32[16,384]{1,0:T(8,128)S(1)}) custom-call(s32[2]{0:T(128)S(1)} %get-tuple-element.99.index_ref, bf16[528,384]{1,0:T(8,128)(2,1)S(1)} %copy-done.1, bf16[528,384]{1,0:T(8,128)(2,1)S(1)} %collective-permute-done.2.refs_1_, bf16[4,6144,256]{2,1,0:T(8,128)(2,1)} %refs_4_.13), custom_call_target="tpu_custom_call" | custom-call | flops 805306368 | bytes 1572864 | tf_op jit(solution)/shard_map/sum_step/pallas_call | solution.py:166
  33.6 0.5 collective-permute-start.21
  34.1 0.5 collective-permute-start.6
  34.8 6.1 %sum_step.11 = (f32[4,512,256]{2,1,0:T(8,128)S(1)}, f32[16,384]{1,0:T(8,128)S(1)}) custom-call(s32[4]{0:T(128)S(1)} %get-tuple-element.95.index_ref, bf16[528,384]{1,0:T(8,128)(2,1)S(1)} %collective-permute-done.18.refs_0_, bf16[528,384]{1,0:T(8,128)(2,1)S(1)} %collective-permute-done.19.refs_1_, ...), custom_call_target="tpu_custom_call", output_to_operand_aliasing={{0}: (6, {}), {1}: (7, {})} | custom-call | flops 1610612736 | bytes 3145728 | tf_op jit(solution)/shard_map/sum_step/pallas_call | solution.py:166
  40.9 1.6 %collective-permute-start.3 = (bf16[528,384]{1,0:T(8,128)(2,1)S(1)}, bf16[528,384]{1,0:T(8,128)(2,1)S(1)}, u32[]{:S(2)}, u32[]{:S(2)}) collective-permute-start(bf16[528,384]{1,0:T(8,128)(2,1)S(1)} %collective-permute-done.refs_2_), channel_id=1, source_target_pairs={{0,4},{1,5},{2,0},{3,1},{4,8},{5,9},{6,2},{7,3},{8,12},{9,13},{10,... | collective-permute-start | bytes 1216520 | tf_op jit(solution)/shard_map/ppermute | solution.py:333
  42.5 2.2 %collective-permute-done.21.refs_1_ = bf16[528,384]{1,0:T(8,128)(2,1)S(1)} collective-permute-done((bf16[528,384]{1,0:T(8,128)(2,1)S(1)}, bf16[528,384]{1,0:T(8,128)(2,1)S(1)}, u32[]{:S(2)}, u32[]{:S(2)}) %collective-permute-start.21) | collective-permute-done | bytes 405536 | tf_op jit(solution)/shard_map/ppermute | solution.py:333
  45.1 1.6 %collective-permute-start.24 = (bf16[528,384]{1,0:T(8,128)(2,1)S(1)}, bf16[528,384]{1,0:T(8,128)(2,1)S(1)}, u32[]{:S(2)}, u32[]{:S(2)}) collective-permute-start(bf16[528,384]{1,0:T(8,128)(2,1)S(1)} %collective-permute-done.20.refs_0_), channel_id=1, source_target_pairs={{0,4},{1,5},{2,0},{3,1},{4,8},{5,9},{6,2},{7,3},{8,12},{9,13},{10,... | collective-permute-start | bytes 1216520 | tf_op jit(solution)/shard_map/ppermute | solution.py:333
  46.9 7.9 %sum_step.8 = (f32[4,512,256]{2,1,0:T(8,128)S(1)}, f32[16,384]{1,0:T(8,128)S(1)}) custom-call(s32[6]{0:T(128)S(1)} %slice_bitcast_fusion.4.index_ref, bf16[528,384]{1,0:T(8,128)(2,1)S(1)} %copy-done.2, bf16[528,384]{1,0:T(8,128)(2,1)S(1)} %collective-permute-done.5.refs_1_, bf16[528,384]{1,0:T(8,128)(2,1)S(1)} %collective-permute-done.refs_2_, ...), custom_call_target="tpu_custom_call" | custom-call | flops 2415919104 | bytes 4718592 | tf_op jit(solution)/shard_map/sum_step/pallas_call | solution.py:166
  54.9 0.5 collective-permute-start.25
  55.9 1.6 %collective-permute-start.8 = (bf16[528,384]{1,0:T(8,128)(2,1)S(1)}, bf16[528,384]{1,0:T(8,128)(2,1)S(1)}, u32[]{:S(2)}, u32[]{:S(2)}) collective-permute-start(bf16[528,384]{1,0:T(8,128)(2,1)S(1)} %collective-permute-done.3.refs_0_), channel_id=1, source_target_pairs={{0,4},{1,5},{2,0},{3,1},{4,8},{5,9},{6,2},{7,3},{8,12},{9,13},{10,... | collective-permute-start | bytes 1216520 | tf_op jit(solution)/shard_map/ppermute | solution.py:333
  57.5 4.3 %collective-permute-done.24.refs_0_ = bf16[528,384]{1,0:T(8,128)(2,1)S(1)} collective-permute-done((bf16[528,384]{1,0:T(8,128)(2,1)S(1)}, bf16[528,384]{1,0:T(8,128)(2,1)S(1)}, u32[]{:S(2)}, u32[]{:S(2)}) %collective-permute-start.24) | collective-permute-done | bytes 405536 | tf_op jit(solution)/shard_map/ppermute | solution.py:333
  62.1 6.1 %sum_step.12 = (f32[4,512,256]{2,1,0:T(8,128)S(1)}, f32[16,384]{1,0:T(8,128)S(1)}) custom-call(s32[4]{0:T(128)S(1)} %get-tuple-element.97.index_ref, bf16[528,384]{1,0:T(8,128)(2,1)S(1)} %collective-permute-done.20.refs_0_, bf16[528,384]{1,0:T(8,128)(2,1)S(1)} %collective-permute-done.21.refs_1_, ...), custom_call_target="tpu_custom_call", output_to_operand_aliasing={{0}: (6, {}), {1}: (7, {})} | custom-call | flops 1610612736 | bytes 3145728 | tf_op jit(solution)/shard_map/sum_step/pallas_call | solution.py:166
  68.3 0.5 collective-permute-start.31
  68.8 1.9 %collective-permute-start.28 = (bf16[256,384]{1,0:T(8,128)(2,1)S(1)}, bf16[256,384]{1,0:T(8,128)(2,1)S(1)}, u32[]{:S(2)}, u32[]{:S(2)}) collective-permute-start(bf16[256,384]{1,0:T(8,128)(2,1)S(1)} %slice.72), channel_id=1, source_target_pairs={{0,4},{1,5},{2,0},{3,1},{4,8},{5,9},{6,2},{7,3},{8,12},{9,13},{10,... | collective-permute-start | bytes 589832 | tf_op jit(solution)/shard_map/ppermute | solution.py:333
  70.7 6.1 %sum_step.9 = (f32[4,512,256]{2,1,0:T(8,128)S(1)}, f32[16,384]{1,0:T(8,128)S(1)}) custom-call(s32[4]{0:T(128)S(1)} %get-tuple-element.97.index_ref, bf16[528,384]{1,0:T(8,128)(2,1)S(1)} %collective-permute-done.3.refs_0_, bf16[528,384]{1,0:T(8,128)(2,1)S(1)} %collective-permute-done.4.refs_1_, ...), custom_call_target="tpu_custom_call", output_to_operand_aliasing={{0}: (6, {}), {1}: (7, {})} | custom-call | flops 1610612736 | bytes 3145728 | tf_op jit(solution)/shard_map/sum_step/pallas_call | solution.py:166
  76.9 0.5 collective-permute-start.15
  77.9 1.7 %collective-permute-start.13 = (bf16[272,384]{1,0:T(8,128)(2,1)S(1)}, bf16[272,384]{1,0:T(8,128)(2,1)S(1)}, u32[]{:S(2)}, u32[]{:S(2)}) collective-permute-start(bf16[272,384]{1,0:T(8,128)(2,1)S(1)} %slice.65), channel_id=1, source_target_pairs={{0,2},{1,3},{2,6},{3,7},{4,0},{5,1},{6,10},{7,11},{8,4},{9,5},{10,... | collective-permute-start | bytes 626696 | tf_op jit(solution)/shard_map/ppermute | solution.py:333
  80.0 6.1 %sum_step.13 = (f32[4,512,256]{2,1,0:T(8,128)S(1)}, f32[16,384]{1,0:T(8,128)S(1)}) custom-call(s32[4]{0:T(128)S(1)} %get-tuple-element.96.index_ref, bf16[528,384]{1,0:T(8,128)(2,1)S(1)} %collective-permute-done.24.refs_0_, bf16[528,384]{1,0:T(8,128)(2,1)S(1)} %collective-permute-done.25.refs_1_, ...), custom_call_target="tpu_custom_call", output_to_operand_aliasing={{0}: (6, {}), {1}: (7, {})} | custom-call | flops 1610612736 | bytes 3145728 | tf_op jit(solution)/shard_map/sum_step/pallas_call | solution.py:166
  86.1 0.5 collective-permute-start.32
  86.6 6.1 %sum_step.10 = (f32[4,512,256]{2,1,0:T(8,128)S(1)}, f32[16,384]{1,0:T(8,128)S(1)}) custom-call(s32[4]{0:T(128)S(1)} %get-tuple-element.96.index_ref, bf16[528,384]{1,0:T(8,128)(2,1)S(1)} %collective-permute-done.8.refs_0_, bf16[528,384]{1,0:T(8,128)(2,1)S(1)} %collective-permute-done.9.refs_1_, ...), custom_call_target="tpu_custom_call", output_to_operand_aliasing={{0}: (6, {}), {1}: (7, {})} | custom-call | flops 1610612736 | bytes 3145728 | tf_op jit(solution)/shard_map/sum_step/pallas_call | solution.py:166
  93.4 5.6 %attend.2 = (f32[4,128,128]{2,1,0:T(8,128)S(1)}, f32[4,128,128]{2,1,0:T(8,128)S(1)}, f32[4,128,128]{2,1,0:T(8,128)S(1)}) custom-call(s32[2]{0:T(128)S(1)} %get-tuple-element.98.index_ref, bf16[256,384]{1,0:T(8,128)(2,1)S(1)} %collective-permute-done.28.refs_0_, bf16[272,384]{1,0:T(8,128)(2,1)S(1)} %collective-permute-done.29.refs_1_, ...), custom_call_target="tpu_custom_call" | custom-call | flops 805306368 | bytes 1572864 | tf_op jit(solution)/shard_map/attend/pallas_call | solution.py:280
  99.0 9.4 %attend.3 = (bf16[8,128,384]{2,1,0:T(8,128)(2,1)S(1)}, f32[8,128,384]{2,1,0:T(8,128)S(1)}) custom-call(s32[18]{0:T(128)S(1)} %slice_bitcast_fusion.6.index_ref, bf16[256,384]{1,0:T(8,128)(2,1)S(1)} %collective-permute-done.12.refs_0_, bf16[272,384]{1,0:T(8,128)(2,1)S(1)} %collective-permute-done.13.refs_1_, ...), custom_call_target="tpu_custom_call" | custom-call | flops 805306368 | bytes 1572864 | tf_op jit(solution)/shard_map/attend/pallas_call | solution.py:280
  108.5 1.2 copy-done
  109.7 2.2 %collective-permute-done.34.other_ref = bf16[8,128,384]{2,1,0:T(8,128)(2,1)S(1)} collective-permute-done((bf16[8,128,384]{2,1,0:T(8,128)(2,1)S(1)}, bf16[8,128,384]{2,1,0:T(8,128)(2,1)S(1)}, u32[]{:S(2)}, u32[]{:S(2)}) %collective-permute-start.34) | collective-permute-done | bytes 786464 | tf_op jit(solution)/shard_map/ppermute | solution.py:336
  111.9 0.9 copy-done.3
  112.8 2.5 %add_blocks.1 = (f32[128,384]{1,0:T(8,128)}, bf16[128,384]{1,0:T(8,128)(2,1)}, bf16[128,384]{1,0:T(8,128)(2,1)}, bf16[128,384]{1,0:T(8,128)(2,1)}, bf16[128,384]...) custom-call(f32[8,128,384]{2,1,0:T(8,128)} %copy-done, ...), custom_call_target="tpu_custom_call" | custom-call | tf_op jit(solution)/shard_map/add_blocks/pallas_call | solution.py:305
  115.3 1.7 %collective-permute-start.35 = (bf16[128,384]{1,0:T(8,128)(2,1)}, bf16[128,384]{1,0:T(8,128)(2,1)S(1)}, u32[]{:S(2)}, u32[]{:S(2)}) collective-permute-start(bf16[128,384]{1,0:T(8,128)(2,1)} %get-tuple-element.88), channel_id=1, source_target_pairs={{0,4},{1,5},{2,0},{3,1},{4,8},{5,9},{6,2},{7,3},{8,12},{9,13},{10,... | collective-permute-start | bytes 294920 | tf_op jit(solution)/shard_map/ppermute | solution.py:333
  117.1 2.6 %collective-permute-start.36 = (bf16[128,384]{1,0:T(8,128)(2,1)}, bf16[128,384]{1,0:T(8,128)(2,1)S(1)}, u32[]{:S(2)}, u32[]{:S(2)}) collective-permute-start(bf16[128,384]{1,0:T(8,128)(2,1)} %get-tuple-element.89), channel_id=1, source_target_pairs={{0,8},{1,9},{2,4},{3,5},{4,12},{5,13},{6,0},{7,1},{8,14},{9,15},{1... | collective-permute-start | bytes 294920 | tf_op jit(solution)/shard_map/ppermute | solution.py:333
  119.7 1.3 collective-permute-start.37
  120.9 2.4 %collective-permute-start.38 = (bf16[128,384]{1,0:T(8,128)(2,1)}, bf16[128,384]{1,0:T(8,128)(2,1)S(1)}, u32[]{:S(2)}, u32[]{:S(2)}) collective-permute-start(bf16[128,384]{1,0:T(8,128)(2,1)} %get-tuple-element.91), channel_id=1, source_target_pairs={{0,14},{1,15},{2,12},{3,13},{4,10},{5,11},{6,8},{7,9},{8,6},{9,7},... | collective-permute-start | bytes 294920 | tf_op jit(solution)/shard_map/ppermute | solution.py:333
  123.7 3.5 %collective-permute-start.40 = (bf16[128,384]{1,0:T(8,128)(2,1)}, bf16[128,384]{1,0:T(8,128)(2,1)S(1)}, u32[]{:S(2)}, u32[]{:S(2)}) collective-permute-start(bf16[128,384]{1,0:T(8,128)(2,1)} %get-tuple-element.93), channel_id=1, source_target_pairs={{0,6},{1,7},{2,10},{3,11},{4,2},{5,3},{6,14},{7,15},{8,0},{9,1},{1... | collective-permute-start | bytes 294920 | tf_op jit(solution)/shard_map/ppermute | solution.py:333
  127.2 7.1 %collective-permute-start.41 = (bf16[128,384]{1,0:T(8,128)(2,1)}, bf16[128,384]{1,0:T(8,128)(2,1)S(1)}, u32[]{:S(2)}, u32[]{:S(2)}) collective-permute-start(bf16[128,384]{1,0:T(8,128)(2,1)} %get-tuple-element.94), channel_id=1, source_target_pairs={{0,2},{1,3},{2,6},{3,7},{4,0},{5,1},{6,10},{7,11},{8,4},{9,5},{10,... | collective-permute-start | bytes 294920 | tf_op jit(solution)/shard_map/ppermute | solution.py:333
  134.4 1.5 %collective-permute-done.37 = bf16[128,384]{1,0:T(8,128)(2,1)S(1)} collective-permute-done((bf16[128,384]{1,0:T(8,128)(2,1)}, bf16[128,384]{1,0:T(8,128)(2,1)S(1)}, u32[]{:S(2)}, u32[]{:S(2)}) %collective-permute-start.37) | collective-permute-done | bytes 98336 | tf_op jit(solution)/shard_map/ppermute | solution.py:333
  135.9 2.8 %collective-permute-done.40 = bf16[128,384]{1,0:T(8,128)(2,1)S(1)} collective-permute-done((bf16[128,384]{1,0:T(8,128)(2,1)}, bf16[128,384]{1,0:T(8,128)(2,1)S(1)}, u32[]{:S(2)}, u32[]{:S(2)}) %collective-permute-start.40) | collective-permute-done | bytes 98336 | tf_op jit(solution)/shard_map/ppermute | solution.py:333
  138.7 0.6 collective-permute-done.41
  139.3 1.7 %add_convert_fusion = bf16[128,384]{1,0:T(8,128)(2,1)} fusion(bf16[128,384]{1,0:T(8,128)(2,1)S(1)} %collective-permute-done.41, bf16[128,384]{1,0:T(8,128)(2,1)S(1)} %collective-permute-done.40, bf16[128,384]{1,0:T(8,128)(2,1)S(1)} %collective-permute-done.39, bf16[128,384]{1,0:T(8,128)(2,1)S(1)} %collective-permute-done.38, ...), kind=kLoop, calls=%fused_computation.12 | loop fusion | flops 835584 | bytes 1081348 | tf_op jit(solution)/shard_map/convert_element_type | solution.py:396
  (72 shorter events, 3.9 us)
Async XLA Ops:
  0.0 10.7 %copy-start.4 = (f32[1,6144]{1,0:T(1,128)S(1)}, f32[1,6144]{1,0:T(1,128)}, u32[]{:S(2)}) copy-start(f32[1,6144]{1,0:T(1,128)} %param.11) | copy-start | bytes 73732
  3.9 29.7 %collective-permute-start = (bf16[528,384]{1,0:T(8,128)(2,1)}, bf16[528,384]{1,0:T(8,128)(2,1)S(1)}, u32[]{:S(2)}, u32[]{:S(2)}) collective-permute-start(bf16[528,384]{1,0:T(8,128)(2,1)} %get-tuple-element.50.refs_0_), channel_id=1, source_target_pairs={{0,4},{1,5},{2,0},{3,1},{4,8},{5,9},{6,2},{7,3},{8,12},{9,13},{10,... | collective-permute-start | bytes 1216520 | tf_op jit(solution)/shard_map/ppermute | solution.py:333
  6.9 27.2 %collective-permute-start.1 = (bf16[528,384]{1,0:T(8,128)(2,1)}, bf16[528,384]{1,0:T(8,128)(2,1)S(1)}, u32[]{:S(2)}, u32[]{:S(2)}) collective-permute-start(bf16[528,384]{1,0:T(8,128)(2,1)} %get-tuple-element.50.refs_0_), channel_id=1, source_target_pairs={{0,2},{1,3},{2,6},{3,7},{4,0},{5,1},{6,10},{7,11},{8,4},{9,5},{10,... | collective-permute-start | bytes 1216520 | tf_op jit(solution)/shard_map/ppermute | solution.py:333
  6.9 21.0 %collective-permute-start.2 = (bf16[528,384]{1,0:T(8,128)(2,1)}, bf16[528,384]{1,0:T(8,128)(2,1)S(1)}, u32[]{:S(2)}, u32[]{:S(2)}) collective-permute-start(bf16[528,384]{1,0:T(8,128)(2,1)} %get-tuple-element.51.refs_0_), channel_id=1, source_target_pairs={{0,1},{1,0},{2,3},{3,2},{4,5},{5,4},{6,7},{7,6},{8,9},{9,8},{10,11... | collective-permute-start | bytes 1216520 | tf_op jit(solution)/shard_map/ppermute | solution.py:336
  6.9 18.2 %collective-permute-start.18 = (bf16[528,384]{1,0:T(8,128)(2,1)}, bf16[528,384]{1,0:T(8,128)(2,1)S(1)}, u32[]{:S(2)}, u32[]{:S(2)}) collective-permute-start(bf16[528,384]{1,0:T(8,128)(2,1)} %get-tuple-element.51.refs_0_), channel_id=1, source_target_pairs={{0,4},{1,5},{2,0},{3,1},{4,8},{5,9},{6,2},{7,3},{8,12},{9,13},{10,... | collective-permute-start | bytes 1216520 | tf_op jit(solution)/shard_map/ppermute | solution.py:333
  8.9 17.7 %collective-permute-start.19 = (bf16[528,384]{1,0:T(8,128)(2,1)}, bf16[528,384]{1,0:T(8,128)(2,1)S(1)}, u32[]{:S(2)}, u32[]{:S(2)}) collective-permute-start(bf16[528,384]{1,0:T(8,128)(2,1)} %get-tuple-element.51.refs_0_), channel_id=1, source_target_pairs={{0,2},{1,3},{2,6},{3,7},{4,0},{5,1},{6,10},{7,11},{8,4},{9,5},{10,... | collective-permute-start | bytes 1216520 | tf_op jit(solution)/shard_map/ppermute | solution.py:333
  10.7 18.8 %copy-start.1 = (bf16[528,384]{1,0:T(8,128)(2,1)S(1)}, bf16[528,384]{1,0:T(8,128)(2,1)}, u32[]{:S(2)}) copy-start(bf16[528,384]{1,0:T(8,128)(2,1)} %get-tuple-element.51.refs_0_) | copy-start | bytes 1216516
  26.6 7.5 %collective-permute-start.22 = (bf16[528,384]{1,0:T(8,128)(2,1)S(1)}, bf16[528,384]{1,0:T(8,128)(2,1)S(1)}, u32[]{:S(2)}, u32[]{:S(2)}) collective-permute-start(bf16[528,384]{1,0:T(8,128)(2,1)S(1)} %collective-permute-done.18.refs_0_), channel_id=1, source_target_pairs={{0,1},{1,0},{2,3},{3,2},{4,5},{5,4},{6,7},{7,6},{8,9},{9,8},{10,11... | collective-permute-start | bytes 1216520 | tf_op jit(solution)/shard_map/ppermute | solution.py:336
  26.6 8.0 %collective-permute-start.23 = (bf16[528,384]{1,0:T(8,128)(2,1)S(1)}, bf16[528,384]{1,0:T(8,128)(2,1)S(1)}, u32[]{:S(2)}, u32[]{:S(2)}) collective-permute-start(bf16[528,384]{1,0:T(8,128)(2,1)S(1)} %collective-permute-done.19.refs_1_), channel_id=1, source_target_pairs={{0,1},{1,0},{2,3},{3,2},{4,5},{5,4},{6,7},{7,6},{8,9},{9,8},{10,11... | collective-permute-start | bytes 1216520 | tf_op jit(solution)/shard_map/ppermute | solution.py:336
  27.9 12.9 %collective-permute-start.20 = (bf16[528,384]{1,0:T(8,128)(2,1)S(1)}, bf16[528,384]{1,0:T(8,128)(2,1)S(1)}, u32[]{:S(2)}, u32[]{:S(2)}) collective-permute-start(bf16[528,384]{1,0:T(8,128)(2,1)S(1)} %collective-permute-done.18.refs_0_), channel_id=1, source_target_pairs={{0,4},{1,5},{2,0},{3,1},{4,8},{5,9},{6,2},{7,3},{8,12},{9,13},{10,... | collective-permute-start | bytes 1216520 | tf_op jit(solution)/shard_map/ppermute | solution.py:333
  29.5 4.6 %copy-start.2 = (bf16[528,384]{1,0:T(8,128)(2,1)S(1)}, bf16[528,384]{1,0:T(8,128)(2,1)}, u32[]{:S(2)}) copy-start(bf16[528,384]{1,0:T(8,128)(2,1)} %get-tuple-element.50.refs_0_) | copy-start | bytes 1216516
  33.6 11.1 %collective-permute-start.21 = (bf16[528,384]{1,0:T(8,128)(2,1)S(1)}, bf16[528,384]{1,0:T(8,128)(2,1)S(1)}, u32[]{:S(2)}, u32[]{:S(2)}) collective-permute-start(bf16[528,384]{1,0:T(8,128)(2,1)S(1)} %collective-permute-done.19.refs_1_), channel_id=1, source_target_pairs={{0,2},{1,3},{2,6},{3,7},{4,0},{5,1},{6,10},{7,11},{8,4},{9,5},{10,... | collective-permute-start | bytes 1216520 | tf_op jit(solution)/shard_map/ppermute | solution.py:333
  34.1 11.0 %collective-permute-start.5 = (bf16[528,384]{1,0:T(8,128)(2,1)S(1)}, bf16[528,384]{1,0:T(8,128)(2,1)S(1)}, u32[]{:S(2)}, u32[]{:S(2)}) collective-permute-start(bf16[528,384]{1,0:T(8,128)(2,1)S(1)} %copy-done.2), channel_id=1, source_target_pairs={{0,1},{1,0},{2,3},{3,2},{4,5},{5,4},{6,7},{7,6},{8,9},{9,8},{10,11... | collective-permute-start | bytes 1216520 | tf_op jit(solution)/shard_map/ppermute | solution.py:336
  34.1 11.0 %collective-permute-start.6 = (bf16[528,384]{1,0:T(8,128)(2,1)S(1)}, bf16[528,384]{1,0:T(8,128)(2,1)S(1)}, u32[]{:S(2)}, u32[]{:S(2)}) collective-permute-start(bf16[528,384]{1,0:T(8,128)(2,1)S(1)} %collective-permute-done.refs_2_), channel_id=1, source_target_pairs={{0,1},{1,0},{2,3},{3,2},{4,5},{5,4},{6,7},{7,6},{8,9},{9,8},{10,11... | collective-permute-start | bytes 1216520 | tf_op jit(solution)/shard_map/ppermute | solution.py:336
  34.6 12.1 %collective-permute-start.7 = (bf16[528,384]{1,0:T(8,128)(2,1)S(1)}, bf16[528,384]{1,0:T(8,128)(2,1)S(1)}, u32[]{:S(2)}, u32[]{:S(2)}) collective-permute-start(bf16[528,384]{1,0:T(8,128)(2,1)S(1)} %collective-permute-done.1.refs_3_), channel_id=1, source_target_pairs={{0,1},{1,0},{2,3},{3,2},{4,5},{5,4},{6,7},{7,6},{8,9},{9,8},{10,11... | collective-permute-start | bytes 1216520 | tf_op jit(solution)/shard_map/ppermute | solution.py:336
  40.9 14.0 %collective-permute-start.3 = (bf16[528,384]{1,0:T(8,128)(2,1)S(1)}, bf16[528,384]{1,0:T(8,128)(2,1)S(1)}, u32[]{:S(2)}, u32[]{:S(2)}) collective-permute-start(bf16[528,384]{1,0:T(8,128)(2,1)S(1)} %collective-permute-done.refs_2_), channel_id=1, source_target_pairs={{0,4},{1,5},{2,0},{3,1},{4,8},{5,9},{6,2},{7,3},{8,12},{9,13},{10,... | collective-permute-start | bytes 1216520 | tf_op jit(solution)/shard_map/ppermute | solution.py:333
  44.7 10.7 %collective-permute-start.4 = (bf16[528,384]{1,0:T(8,128)(2,1)S(1)}, bf16[528,384]{1,0:T(8,128)(2,1)S(1)}, u32[]{:S(2)}, u32[]{:S(2)}) collective-permute-start(bf16[528,384]{1,0:T(8,128)(2,1)S(1)} %collective-permute-done.1.refs_3_), channel_id=1, source_target_pairs={{0,2},{1,3},{2,6},{3,7},{4,0},{5,1},{6,10},{7,11},{8,4},{9,5},{10,... | collective-permute-start | bytes 1216520 | tf_op jit(solution)/shard_map/ppermute | solution.py:333
  45.1 10.3 %collective-permute-start.26 = (bf16[528,384]{1,0:T(8,128)(2,1)S(1)}, bf16[528,384]{1,0:T(8,128)(2,1)S(1)}, u32[]{:S(2)}, u32[]{:S(2)}) collective-permute-start(bf16[528,384]{1,0:T(8,128)(2,1)S(1)} %collective-permute-done.20.refs_0_), channel_id=1, source_target_pairs={{0,1},{1,0},{2,3},{3,2},{4,5},{5,4},{6,7},{7,6},{8,9},{9,8},{10,11... | collective-permute-start | bytes 1216520 | tf_op jit(solution)/shard_map/ppermute | solution.py:336
  45.1 16.7 %collective-permute-start.24 = (bf16[528,384]{1,0:T(8,128)(2,1)S(1)}, bf16[528,384]{1,0:T(8,128)(2,1)S(1)}, u32[]{:S(2)}, u32[]{:S(2)}) collective-permute-start(bf16[528,384]{1,0:T(8,128)(2,1)S(1)} %collective-permute-done.20.refs_0_), channel_id=1, source_target_pairs={{0,4},{1,5},{2,0},{3,1},{4,8},{5,9},{6,2},{7,3},{8,12},{9,13},{10,... | collective-permute-start | bytes 1216520 | tf_op jit(solution)/shard_map/ppermute | solution.py:333
  46.8 9.2 %collective-permute-start.27 = (bf16[528,384]{1,0:T(8,128)(2,1)S(1)}, bf16[528,384]{1,0:T(8,128)(2,1)S(1)}, u32[]{:S(2)}, u32[]{:S(2)}) collective-permute-start(bf16[528,384]{1,0:T(8,128)(2,1)S(1)} %collective-permute-done.21.refs_1_), channel_id=1, source_target_pairs={{0,1},{1,0},{2,3},{3,2},{4,5},{5,4},{6,7},{7,6},{8,9},{9,8},{10,11... | collective-permute-start | bytes 1216520 | tf_op jit(solution)/shard_map/ppermute | solution.py:336
  54.9 13.3 %collective-permute-start.25 = (bf16[528,384]{1,0:T(8,128)(2,1)S(1)}, bf16[528,384]{1,0:T(8,128)(2,1)S(1)}, u32[]{:S(2)}, u32[]{:S(2)}) collective-permute-start(bf16[528,384]{1,0:T(8,128)(2,1)S(1)} %collective-permute-done.21.refs_1_), channel_id=1, source_target_pairs={{0,2},{1,3},{2,6},{3,7},{4,0},{5,1},{6,10},{7,11},{8,4},{9,5},{10,... | collective-permute-start | bytes 1216520 | tf_op jit(solution)/shard_map/ppermute | solution.py:333
  55.4 12.9 %collective-permute-start.10 = (bf16[528,384]{1,0:T(8,128)(2,1)S(1)}, bf16[528,384]{1,0:T(8,128)(2,1)S(1)}, u32[]{:S(2)}, u32[]{:S(2)}) collective-permute-start(bf16[528,384]{1,0:T(8,128)(2,1)S(1)} %collective-permute-done.3.refs_0_), channel_id=1, source_target_pairs={{0,1},{1,0},{2,3},{3,2},{4,5},{5,4},{6,7},{7,6},{8,9},{9,8},{10,11... | collective-permute-start | bytes 1216520 | tf_op jit(solution)/shard_map/ppermute | solution.py:336
  55.5 13.3 %collective-permute-start.11 = (bf16[528,384]{1,0:T(8,128)(2,1)S(1)}, bf16[528,384]{1,0:T(8,128)(2,1)S(1)}, u32[]{:S(2)}, u32[]{:S(2)}) collective-permute-start(bf16[528,384]{1,0:T(8,128)(2,1)S(1)} %collective-permute-done.4.refs_1_), channel_id=1, source_target_pairs={{0,1},{1,0},{2,3},{3,2},{4,5},{5,4},{6,7},{7,6},{8,9},{9,8},{10,11... | collective-permute-start | bytes 1216520 | tf_op jit(solution)/shard_map/ppermute | solution.py:336
  55.9 20.9 %collective-permute-start.8 = (bf16[528,384]{1,0:T(8,128)(2,1)S(1)}, bf16[528,384]{1,0:T(8,128)(2,1)S(1)}, u32[]{:S(2)}, u32[]{:S(2)}) collective-permute-start(bf16[528,384]{1,0:T(8,128)(2,1)S(1)} %collective-permute-done.3.refs_0_), channel_id=1, source_target_pairs={{0,4},{1,5},{2,0},{3,1},{4,8},{5,9},{6,2},{7,3},{8,12},{9,13},{10,... | collective-permute-start | bytes 1216520 | tf_op jit(solution)/shard_map/ppermute | solution.py:333
  61.8 15.0 %collective-permute-start.9 = (bf16[528,384]{1,0:T(8,128)(2,1)S(1)}, bf16[528,384]{1,0:T(8,128)(2,1)S(1)}, u32[]{:S(2)}, u32[]{:S(2)}) collective-permute-start(bf16[528,384]{1,0:T(8,128)(2,1)S(1)} %collective-permute-done.4.refs_1_), channel_id=1, source_target_pairs={{0,2},{1,3},{2,6},{3,7},{4,0},{5,1},{6,10},{7,11},{8,4},{9,5},{10,... | collective-permute-start | bytes 1216520 | tf_op jit(solution)/shard_map/ppermute | solution.py:333
  68.2 9.7 %collective-permute-start.30 = (bf16[528,384]{1,0:T(8,128)(2,1)S(1)}, bf16[528,384]{1,0:T(8,128)(2,1)S(1)}, u32[]{:S(2)}, u32[]{:S(2)}) collective-permute-start(bf16[528,384]{1,0:T(8,128)(2,1)S(1)} %collective-permute-done.24.refs_0_), channel_id=1, source_target_pairs={{0,1},{1,0},{2,3},{3,2},{4,5},{5,4},{6,7},{7,6},{8,9},{9,8},{10,11... | collective-permute-start | bytes 1216520 | tf_op jit(solution)/shard_map/ppermute | solution.py:336
  68.3 11.3 %collective-permute-start.31 = (bf16[528,384]{1,0:T(8,128)(2,1)S(1)}, bf16[528,384]{1,0:T(8,128)(2,1)S(1)}, u32[]{:S(2)}, u32[]{:S(2)}) collective-permute-start(bf16[528,384]{1,0:T(8,128)(2,1)S(1)} %collective-permute-done.25.refs_1_), channel_id=1, source_target_pairs={{0,1},{1,0},{2,3},{3,2},{4,5},{5,4},{6,7},{7,6},{8,9},{9,8},{10,11... | collective-permute-start | bytes 1216520 | tf_op jit(solution)/shard_map/ppermute | solution.py:336
  68.8 8.6 %collective-permute-start.28 = (bf16[256,384]{1,0:T(8,128)(2,1)S(1)}, bf16[256,384]{1,0:T(8,128)(2,1)S(1)}, u32[]{:S(2)}, u32[]{:S(2)}) collective-permute-start(bf16[256,384]{1,0:T(8,128)(2,1)S(1)} %slice.72), channel_id=1, source_target_pairs={{0,4},{1,5},{2,0},{3,1},{4,8},{5,9},{6,2},{7,3},{8,12},{9,13},{10,... | collective-permute-start | bytes 589832 | tf_op jit(solution)/shard_map/ppermute | solution.py:333
  76.8 9.3 %collective-permute-start.14 = (bf16[528,384]{1,0:T(8,128)(2,1)S(1)}, bf16[528,384]{1,0:T(8,128)(2,1)S(1)}, u32[]{:S(2)}, u32[]{:S(2)}) collective-permute-start(bf16[528,384]{1,0:T(8,128)(2,1)S(1)} %collective-permute-done.8.refs_0_), channel_id=1, source_target_pairs={{0,1},{1,0},{2,3},{3,2},{4,5},{5,4},{6,7},{7,6},{8,9},{9,8},{10,11... | collective-permute-start | bytes 1216520 | tf_op jit(solution)/shard_map/ppermute | solution.py:336
  76.9 9.7 %collective-permute-start.15 = (bf16[528,384]{1,0:T(8,128)(2,1)S(1)}, bf16[528,384]{1,0:T(8,128)(2,1)S(1)}, u32[]{:S(2)}, u32[]{:S(2)}) collective-permute-start(bf16[528,384]{1,0:T(8,128)(2,1)S(1)} %collective-permute-done.9.refs_1_), channel_id=1, source_target_pairs={{0,1},{1,0},{2,3},{3,2},{4,5},{5,4},{6,7},{7,6},{8,9},{9,8},{10,11... | collective-permute-start | bytes 1216520 | tf_op jit(solution)/shard_map/ppermute | solution.py:336
  77.4 8.6 %collective-permute-start.29 = (bf16[272,384]{1,0:T(8,128)(2,1)S(1)}, bf16[272,384]{1,0:T(8,128)(2,1)S(1)}, u32[]{:S(2)}, u32[]{:S(2)}) collective-permute-start(bf16[272,384]{1,0:T(8,128)(2,1)S(1)} %slice.73), channel_id=1, source_target_pairs={{0,2},{1,3},{2,6},{3,7},{4,0},{5,1},{6,10},{7,11},{8,4},{9,5},{10,... | collective-permute-start | bytes 626696 | tf_op jit(solution)/shard_map/ppermute | solution.py:333
  77.9 14.8 %collective-permute-start.13 = (bf16[272,384]{1,0:T(8,128)(2,1)S(1)}, bf16[272,384]{1,0:T(8,128)(2,1)S(1)}, u32[]{:S(2)}, u32[]{:S(2)}) collective-permute-start(bf16[272,384]{1,0:T(8,128)(2,1)S(1)} %slice.65), channel_id=1, source_target_pairs={{0,2},{1,3},{2,6},{3,7},{4,0},{5,1},{6,10},{7,11},{8,4},{9,5},{10,... | collective-permute-start | bytes 626696 | tf_op jit(solution)/shard_map/ppermute | solution.py:333
  79.6 13.1 %collective-permute-start.12 = (bf16[256,384]{1,0:T(8,128)(2,1)S(1)}, bf16[256,384]{1,0:T(8,128)(2,1)S(1)}, u32[]{:S(2)}, u32[]{:S(2)}) collective-permute-start(bf16[256,384]{1,0:T(8,128)(2,1)S(1)} %slice.64), channel_id=1, source_target_pairs={{0,4},{1,5},{2,0},{3,1},{4,8},{5,9},{6,2},{7,3},{8,12},{9,13},{10,... | collective-permute-start | bytes 589832 | tf_op jit(solution)/shard_map/ppermute | solution.py:333
  86.0 7.3 %collective-permute-start.33 = (bf16[272,384]{1,0:T(8,128)(2,1)S(1)}, bf16[272,384]{1,0:T(8,128)(2,1)S(1)}, u32[]{:S(2)}, u32[]{:S(2)}) collective-permute-start(bf16[272,384]{1,0:T(8,128)(2,1)S(1)} %collective-permute-done.29.refs_1_), channel_id=1, source_target_pairs={{0,1},{1,0},{2,3},{3,2},{4,5},{5,4},{6,7},{7,6},{8,9},{9,8},{10,11... | collective-permute-start | bytes 626696 | tf_op jit(solution)/shard_map/ppermute | solution.py:336
  86.1 7.2 %collective-permute-start.32 = (bf16[256,384]{1,0:T(8,128)(2,1)S(1)}, bf16[256,384]{1,0:T(8,128)(2,1)S(1)}, u32[]{:S(2)}, u32[]{:S(2)}) collective-permute-start(bf16[256,384]{1,0:T(8,128)(2,1)S(1)} %collective-permute-done.28.refs_0_), channel_id=1, source_target_pairs={{0,1},{1,0},{2,3},{3,2},{4,5},{5,4},{6,7},{7,6},{8,9},{9,8},{10,11... | collective-permute-start | bytes 589832 | tf_op jit(solution)/shard_map/ppermute | solution.py:336
  92.7 6.3 %collective-permute-start.17 = (bf16[272,384]{1,0:T(8,128)(2,1)S(1)}, bf16[272,384]{1,0:T(8,128)(2,1)S(1)}, u32[]{:S(2)}, u32[]{:S(2)}) collective-permute-start(bf16[272,384]{1,0:T(8,128)(2,1)S(1)} %collective-permute-done.13.refs_1_), channel_id=1, source_target_pairs={{0,1},{1,0},{2,3},{3,2},{4,5},{5,4},{6,7},{7,6},{8,9},{9,8},{10,11... | collective-permute-start | bytes 626696 | tf_op jit(solution)/shard_map/ppermute | solution.py:336
  92.9 6.2 %collective-permute-start.16 = (bf16[256,384]{1,0:T(8,128)(2,1)S(1)}, bf16[256,384]{1,0:T(8,128)(2,1)S(1)}, u32[]{:S(2)}, u32[]{:S(2)}) collective-permute-start(bf16[256,384]{1,0:T(8,128)(2,1)S(1)} %collective-permute-done.12.refs_0_), channel_id=1, source_target_pairs={{0,1},{1,0},{2,3},{3,2},{4,5},{5,4},{6,7},{7,6},{8,9},{9,8},{10,11... | collective-permute-start | bytes 589832 | tf_op jit(solution)/shard_map/ppermute | solution.py:336
  108.5 1.2 copy-start
  109.6 2.3 %collective-permute-start.34 = (bf16[8,128,384]{2,1,0:T(8,128)(2,1)S(1)}, bf16[8,128,384]{2,1,0:T(8,128)(2,1)S(1)}, u32[]{:S(2)}, u32[]{:S(2)}) collective-permute-start(bf16[8,128,384]{2,1,0:T(8,128)(2,1)S(1)} %get-tuple-element.86), channel_id=1, source_target_pairs={{0,1},{1,0},{2,3},{3,2},{4,5},{5,4},{6,7},{7,6},{8,9},{9,8},{10,11... | collective-permute-start | bytes 2359304 | tf_op jit(solution)/shard_map/ppermute | solution.py:336
  111.9 0.9 copy-start.3
  115.3 8.4 %collective-permute-start.35 = (bf16[128,384]{1,0:T(8,128)(2,1)}, bf16[128,384]{1,0:T(8,128)(2,1)S(1)}, u32[]{:S(2)}, u32[]{:S(2)}) collective-permute-start(bf16[128,384]{1,0:T(8,128)(2,1)} %get-tuple-element.88), channel_id=1, source_target_pairs={{0,4},{1,5},{2,0},{3,1},{4,8},{5,9},{6,2},{7,3},{8,12},{9,13},{10,... | collective-permute-start | bytes 294920 | tf_op jit(solution)/shard_map/ppermute | solution.py:333
  117.1 10.2 %collective-permute-start.36 = (bf16[128,384]{1,0:T(8,128)(2,1)}, bf16[128,384]{1,0:T(8,128)(2,1)S(1)}, u32[]{:S(2)}, u32[]{:S(2)}) collective-permute-start(bf16[128,384]{1,0:T(8,128)(2,1)} %get-tuple-element.89), channel_id=1, source_target_pairs={{0,8},{1,9},{2,4},{3,5},{4,12},{5,13},{6,0},{7,1},{8,14},{9,15},{1... | collective-permute-start | bytes 294920 | tf_op jit(solution)/shard_map/ppermute | solution.py:333
  119.7 16.3 %collective-permute-start.37 = (bf16[128,384]{1,0:T(8,128)(2,1)}, bf16[128,384]{1,0:T(8,128)(2,1)S(1)}, u32[]{:S(2)}, u32[]{:S(2)}) collective-permute-start(bf16[128,384]{1,0:T(8,128)(2,1)} %get-tuple-element.90), channel_id=1, source_target_pairs={{0,12},{1,13},{2,8},{3,9},{4,14},{5,15},{6,4},{7,5},{8,10},{9,11},... | collective-permute-start | bytes 294920 | tf_op jit(solution)/shard_map/ppermute | solution.py:333
  120.9 15.0 %collective-permute-start.38 = (bf16[128,384]{1,0:T(8,128)(2,1)}, bf16[128,384]{1,0:T(8,128)(2,1)S(1)}, u32[]{:S(2)}, u32[]{:S(2)}) collective-permute-start(bf16[128,384]{1,0:T(8,128)(2,1)} %get-tuple-element.91), channel_id=1, source_target_pairs={{0,14},{1,15},{2,12},{3,13},{4,10},{5,11},{6,8},{7,9},{8,6},{9,7},... | collective-permute-start | bytes 294920 | tf_op jit(solution)/shard_map/ppermute | solution.py:333
  123.4 12.6 %collective-permute-start.39 = (bf16[128,384]{1,0:T(8,128)(2,1)}, bf16[128,384]{1,0:T(8,128)(2,1)S(1)}, u32[]{:S(2)}, u32[]{:S(2)}) collective-permute-start(bf16[128,384]{1,0:T(8,128)(2,1)} %get-tuple-element.92), channel_id=1, source_target_pairs={{0,10},{1,11},{2,14},{3,15},{4,6},{5,7},{6,12},{7,13},{8,2},{9,3},... | collective-permute-start | bytes 294920 | tf_op jit(solution)/shard_map/ppermute | solution.py:333
  123.7 15.0 %collective-permute-start.40 = (bf16[128,384]{1,0:T(8,128)(2,1)}, bf16[128,384]{1,0:T(8,128)(2,1)S(1)}, u32[]{:S(2)}, u32[]{:S(2)}) collective-permute-start(bf16[128,384]{1,0:T(8,128)(2,1)} %get-tuple-element.93), channel_id=1, source_target_pairs={{0,6},{1,7},{2,10},{3,11},{4,2},{5,3},{6,14},{7,15},{8,0},{9,1},{1... | collective-permute-start | bytes 294920 | tf_op jit(solution)/shard_map/ppermute | solution.py:333
  127.2 12.1 %collective-permute-start.41 = (bf16[128,384]{1,0:T(8,128)(2,1)}, bf16[128,384]{1,0:T(8,128)(2,1)S(1)}, u32[]{:S(2)}, u32[]{:S(2)}) collective-permute-start(bf16[128,384]{1,0:T(8,128)(2,1)} %get-tuple-element.94), channel_id=1, source_target_pairs={{0,2},{1,3},{2,6},{3,7},{4,0},{5,1},{6,10},{7,11},{8,4},{9,5},{10,... | collective-permute-start | bytes 294920 | tf_op jit(solution)/shard_map/ppermute | solution.py:333

commit v2 on v1

--- a/solution.py
+++ b/solution.py
@@ -11,7 +11,8 @@
 
 epsilon = 1e-06
 MAX_RING = 8
-VMEM_MIB = 60
+SMALL_MIB = 16
+PARTS = 2
 STEP_MIB = 48
 TILE = 16
 
@@ -32,44 +33,52 @@
     return [pl.BlockSpec(memory_space=pl.ANY)] * count
 
 
-def prepare_kernel(rows_ref, gain_ref, *halves):
-    cols = rows_ref.shape[1]
-    for which, half_ref in enumerate(halves):
-        rows = half_ref.shape[0] - TILE
-        values = rows_ref[which * rows : (which + 1) * rows, :].astype(jnp.float32)
-        half_ref[:rows, :] = (values * gain_ref[...]).astype(jnp.bfloat16)
-        squares = values * values
-        high = squares.astype(jnp.bfloat16)
-        low = (squares - high.astype(jnp.float32)).astype(jnp.bfloat16)
-        ones = jnp.ones((8, cols), jnp.bfloat16)
-        sums = sum(
-            lax.dot_general(ones, part, (((1,), (1,)), ((), ())), preferred_element_type=jnp.float32)
-            for part in (high, low)
-        )[:1]
-        terms = []
-        for _ in range(3):
-            terms.append(sums.astype(jnp.bfloat16).astype(jnp.float32))
-            sums = sums - terms[-1]
-        per = -(-rows // cols)
-        lines = []
-        for term in terms:
-            for line in range(per):
-                part = term[:, line * cols : min(rows, (line + 1) * cols)]
-                if part.shape[1] < cols:
-                    part = jnp.concatenate([part, jnp.zeros((1, cols - part.shape[1]), jnp.float32)], axis=1)
-                lines.append(part)
-        lines.append(jnp.zeros((TILE - len(lines), cols), jnp.float32))
-        half_ref[rows:, :] = jnp.concatenate(lines, axis=0).astype(jnp.bfloat16)
-
-
-def prepare(enc_rows, gain_share):
-    rows, cols = enc_rows.shape
+def prepare_kernel(index_ref, rows_ref, gain_ref, *refs):
+    half_ref = refs[-1]
+    rows, cols = rows_ref.shape
+    values = rows_ref[...].astype(jnp.float32)
+    half_ref[:rows, :] = (values * gain_ref[...]).astype(jnp.bfloat16)
+    squares = values * values
+    high = squares.astype(jnp.bfloat16)
+    low = (squares - high.astype(jnp.float32)).astype(jnp.bfloat16)
+    ones = jnp.ones((8, cols), jnp.bfloat16)
+    sums = sum(
+        lax.dot_general(ones, part, (((1,), (1,)), ((), ())), preferred_element_type=jnp.float32)
+        for part in (high, low)
+    )[:1]
+    terms = []
+    for _ in range(3):
+        terms.append(sums.astype(jnp.bfloat16).astype(jnp.float32))
+        sums = sums - terms[-1]
+    lines = []
+    for term in terms:
+        for line in range(-(-rows // cols)):
+            part = term[:, line * cols : min(rows, (line + 1) * cols)]
+            if part.shape[1] < cols:
+                part = jnp.concatenate([part, jnp.zeros((1, cols - part.shape[1]), jnp.float32)], axis=1)
+            lines.append(part)
+    lines.append(jnp.zeros((TILE - len(lines), cols), jnp.float32))
+    half_ref[rows:, :] = jnp.concatenate(lines, axis=0).astype(jnp.bfloat16)
+
+
+def prepare(position, enc_rows, enc_gain, which, before=()):
+    rows, cols = enc_rows.shape[0] // 2, enc_rows.shape[1]
     return pl.pallas_call(
         prepare_kernel,
-        out_shape=[jax.ShapeDtypeStruct((rows // 2 + TILE, cols), jnp.bfloat16)] * 2,
-        compiler_params=params(VMEM_MIB),
+        out_shape=jax.ShapeDtypeStruct((rows + TILE, cols), jnp.bfloat16),
+        grid_spec=pltpu.PrefetchScalarGridSpec(
+            num_scalar_prefetch=1,
+            grid=(1,),
+            in_specs=[
+                pl.BlockSpec((rows, cols), lambda g, i: (which, 0)),
+                pl.BlockSpec((1, cols), lambda g, i: (0, i[0])),
+            ]
+            + anywhere(len(before)),
+            out_specs=pl.BlockSpec((rows + TILE, cols), lambda g, i: (0, 0)),
+        ),
+        compiler_params=params(SMALL_MIB),
         name="prepare",
-    )(enc_rows, gain_share[None, :])
+    )(position[None], enc_rows, enc_gain[None, :], *before)
 
 
 def lane_sums(tile, rows):
@@ -140,15 +149,17 @@
         index_ref, len(slots), pieces, w_ref, rows_at, tiles, weights, rows_sem, tiles_sem, weights_sem
     )
     start_all(row_copies)
-    start_all(weight_copies[0])
+    for copies in weight_copies:
+        start_all(copies)
     start_all(tile_copies)
     wait_all(row_copies)
-    for head in range(heads):
-        if head + 1 < heads:
-            start_all(weight_copies[head + 1])
-        wait_all(weight_copies[head])
-        term = jnp.dot(rows_at[...], weights[head], preferred_element_type=jnp.float32)
-        sum_out[head] = term if first else sum_in[head] + term
+    for pair in range(0, heads, 2):
+        both = range(pair, min(pair + 2, heads))
+        for head in both:
+            wait_all(weight_copies[head])
+        for head in both:
+            term = jnp.dot(rows_at[...], weights[head], preferred_element_type=jnp.float32)
+            sum_out[head] = term if first else sum_in[head] + term
     wait_all(tile_copies)
     squares = sum(tiles[slot].astype(jnp.float32) for slot in range(len(slots)))
     tile_out[...] = squares if first else tile_in[...] + squares
@@ -176,7 +187,7 @@
         input_output_aliases=aliases,
         compiler_params=params(STEP_MIB),
         cost_estimate=pl.CostEstimate(
-            flops=2 * rows * depth * heads * pair, bytes_accessed=2 * depth * heads * pair, transcendentals=0
+            flops=rows * depth * heads * pair // 2, bytes_accessed=depth * heads * pair // 2, transcendentals=0
         ),
         name="sum_step",
     )(index, *operands)
@@ -211,8 +222,9 @@
     squares = sum((tiles[slot].astype(jnp.float32) for slot in range(len(slots))), tile_in[...])
     inverse = lax.rsqrt(lane_sums(squares, rows) / width + epsilon)
     wait_all(row_copies)
+    for copies in weight_copies:
+        wait_all(copies)
     for head in range(heads):
-        wait_all(weight_copies[head])
         keyvals = (
             sum_in[head] + jnp.dot(rows_at[...], weights[head], preferred_element_type=jnp.float32)
         ).astype(jnp.bfloat16)
@@ -241,7 +253,7 @@
     wait_all(out_copies)
     count, _, cols = mine_ref.shape
     for part, target in enumerate((theirs_ref, mine_ref)):
-        @pl.loop(0, count)
+        @pl.loop(0, count, unroll=min(count, 4))
         def _(step):
             block = index_ref[len(slots) + part * count + step]
             columns = pl.ds(pl.multiple_of(block * cols, cols), cols)
@@ -289,28 +301,81 @@
         ),
         compiler_params=params(STEP_MIB),
         cost_estimate=pl.CostEstimate(
-            flops=2 * rows * depth * heads * pair, bytes_accessed=2 * depth * heads * pair, transcendentals=0
+            flops=rows * depth * heads * pair // 2, bytes_accessed=depth * heads * pair // 2, transcendentals=0
         ),
         name="attend",
     )(index, *operands)
 
 
-def add_kernel(mine_ref, other_ref, *outs):
-    for block, out in enumerate(outs):
-        out[...] = (mine_ref[block] + other_ref[block].astype(jnp.float32)).astype(out.dtype)
-
-
-def add_blocks(mine, other):
+def split_kernel(mine_ref, other_ref, keep_ref, *sends):
+    lines, rows = keep_ref.shape[0], keep_ref.shape[1]
+    part = rows // len(sends)
+    for line in range(lines):
+        keep_ref[line] = mine_ref[2 * line] + other_ref[2 * line].astype(jnp.float32)
+        total = mine_ref[2 * line + 1] + other_ref[2 * line + 1].astype(jnp.float32)
+        for which, send in enumerate(sends):
+            send[line] = total[which * part : (which + 1) * part].astype(send.dtype)
+
+
+def split_blocks(mine, other, parts):
     count, target, cols = mine.shape
+    sends = [jax.ShapeDtypeStruct((count // 2, target // parts, cols), jnp.bfloat16)] * parts
     return pl.pallas_call(
-        add_kernel,
+        split_kernel,
+        out_shape=[pltpu.VMEM((count // 2, target, cols), jnp.float32)] + sends,
+        compiler_params=params(SMALL_MIB),
+        name="split_blocks",
+    )(mine, other)
+
+
+def fold_kernel(which, keep_ref, other_ref, *outs):
+    part = other_ref.shape[1]
+    for line, out in enumerate(outs):
+        kept = keep_ref[line, which * part : (which + 1) * part, :]
+        out[...] = (kept + other_ref[line].astype(jnp.float32)).astype(out.dtype)
+
+
+def fold_blocks(which, keep, other):
+    lines, part, cols = other.shape
+    return pl.pallas_call(
+        functools.partial(fold_kernel, which),
         out_shape=[
-            jax.ShapeDtypeStruct((target, cols), jnp.float32 if block == 0 else jnp.bfloat16)
-            for block in range(count)
+            jax.ShapeDtypeStruct((part, cols), jnp.float32 if line == 0 else jnp.bfloat16) for line in range(lines)
         ],
-        compiler_params=params(VMEM_MIB),
-        name="add_blocks",
-    )(mine, other)
+        compiler_params=params(SMALL_MIB),
+        name="fold_blocks",
+    )(keep, other)
+
+
+def finish_kernel(lines, index_ref, share_ref, *refs):
+    *terms, out_ref = refs
+    at = 0
+    for first in range(0, len(terms), lines):
+        part = terms[first].shape[0]
+        total = share_ref[at : at + part, :].astype(jnp.float32)
+        for term in terms[first : first + lines]:
+            total = total + term[...].astype(jnp.float32)
+        out_ref[at : at + part, :] = total.astype(out_ref.dtype)
+        at += part
+
+
+def finish(position, dec_input, parts):
+    cols = parts[0][0].shape[1]
+    target = dec_input.shape[0]
+    terms = [term for part in parts for term in part]
+    block = pl.BlockSpec((target, cols), lambda g, i: (0, i[0]))
+    return pl.pallas_call(
+        functools.partial(finish_kernel, len(parts[0])),
+        out_shape=jax.ShapeDtypeStruct((target, cols), jnp.bfloat16),
+        grid_spec=pltpu.PrefetchScalarGridSpec(
+            num_scalar_prefetch=1,
+            grid=(1,),
+            in_specs=[block] + [pl.BlockSpec(memory_space=pltpu.VMEM)] * len(terms),
+            out_specs=pl.BlockSpec((target, cols), lambda g, i: (0, 0)),
+        ),
+        compiler_params=params(SMALL_MIB),
+        name="finish",
+    )(position[None], dec_input, *terms)
 
 
 def ring_body(enc_rows, enc_gain, dec_input, dec_gain, w_query, w_keyval, w_out):
@@ -332,8 +397,11 @@
         pairs = [(2 * chip + core, 2 * at(chip, offset) + core) for chip in range(chips) for core in range(2)]
         return lax.ppermute(values, "section", pairs)
 
+    def exchange(values, bits):
+        return lax.ppermute(values, "section", [(s, s ^ bits) for s in range(sections)])
+
     def swap(values):
-        return lax.ppermute(values, "section", [(s, s ^ 1) for s in range(sections)])
+        return exchange(values, 1)
 
     table = []
     for s in range(sections):
@@ -344,18 +412,20 @@
                 row += [2 * at(chip, -step) + side, 2 * at(chip, step) + side]
         row += [2 * at(chip, far) + core, 2 * at(chip, far) + 1 - core]
         for side in (1 - core, core):
-            row += [2 * at(chip, k) + side for k in range(chips)]
+            row += [2 * (chip ^ k) + side for k in range(chips)]
         table.append(row)
     row = lax.dynamic_slice_in_dim(jnp.asarray(np.array(table, np.int32)), position, 1, 0)[0]
     first_slot = [0] + [2 + 4 * step for step in range(far)]
 
     half_rows = enc_rows.shape[0] // 2
-    own = prepare(enc_rows, lax.dynamic_slice_in_dim(enc_gain, position * cols, cols, 0))
     state = dec_input.astype(jnp.float32)
     normed = rms_scaled(state, dec_gain[0]).astype(jnp.bfloat16)
     queries = (
         jnp.einsum("td,hdk->htk", normed, w_query, preferred_element_type=jnp.float32) * score_scale
     ).astype(jnp.bfloat16)
+
+    own = [prepare(position, enc_rows, enc_gain, 0)]
+    own.append(prepare(position, enc_rows, enc_gain, 1, [queries]))
 
     carried = [None, None]
     slots = [[(half,), (swap(half),)] for half in own]
@@ -388,12 +458,13 @@
     last = first_slot[far]
     first = attend(row[last : last + 2], slots[2 * far], w_keyval, carried[0], queries)
     theirs, mine = attend(row[last:], slots[2 * far + 1], w_keyval, carried[1], queries, first, w_out, chips, cols)
-    blocks = add_blocks(mine, swap(theirs))
-    share = lax.dynamic_slice_in_dim(dec_input, position * cols, cols, 1).astype(jnp.float32)
-    total = share + blocks[0]
-    for k in range(1, chips):
-        total = total + hop(blocks[k], k).astype(jnp.float32)
-    return total.astype(jnp.bfloat16)
+    keep, *sends = split_blocks(mine, swap(theirs), PARTS)
+    sends = [exchange(send, 2) for send in sends]
+    parts = []
+    for which, send in enumerate(sends):
+        first, *others = fold_blocks(which, keep, send)
+        parts.append([first] + [exchange(term, 4 * (line + 1)) for line, term in enumerate(others)])
+    return finish(position, dec_input, parts)
 
 
 def general_body(enc_rows, enc_gain, dec_input, dec_gain, w_query, w_keyval, w_out):

time: 142 us -> 121 us (0.85)
  Pallas kernels: 62.5 us -> 47.6 us
  starting transfers between devices: 40.8 us -> 36 us
  waiting for transfers between devices: 25.2 us -> 27.7 us
  other arithmetic: 3.55 us -> 1.8 us
    ppermute x23 -> x16, starting transfers between devices: 36.7 us -> 20.1 us  [hop(): return lax.ppermute(values, 'section', pairs)]
    ppermute x19 -> x27, starting transfers between devices: 4.12 us -> 15.9 us  [exchange(): lax.ppermute(values, 'section', [(s, s ^ bits) for s in range(sections)])]
    pallas_call x7, Pallas kernels: 42.3 us -> 31.3 us  [sum_step(): pl.pallas_call(functools.partial(sum_kernel, counts, carried is None), ou...]
    ppermute x19 -> x27, waiting for transfers between devices: 2.25 us -> 11.9 us  [exchange(): lax.ppermute(values, 'section', [(s, s ^ bits) for s in range(sections)])]
    ppermute x23 -> x16, waiting for transfers between devices: 23 us -> 15.8 us  [hop(): return lax.ppermute(values, 'section', pairs)]
    pallas_call x2 -> x6, Pallas kernels: 5.05 us -> 1.75 us  [the longest x2 0.8 us: prepare(): pl.pallas_call(prepare_kernel, out_shape=jax.ShapeDtypeStruct((rows + TIL...]
    convert_element_type x1 -> x0, other arithmetic: 1.75 us -> none  [ring_body(): return total.astype(jnp.bfloat16)]
  transfers between devices with their start and end apart: 42 -> 43, of which waited for: 8 -> 13; matrix products, arithmetic and copies ran while one was open for 5% -> 6% of each run, Pallas kernels for 34% -> 31%
where the time goes in v2:
time: 121 us; the launch traced here: 120 us
  Pallas kernels  47.6 us (39%)
  starting transfers between devices  36 us (30%)
  waiting for transfers between devices  27.7 us (23%)
  matrix products  3.89 us (3%)
  local copies, waits for them, and re-layouts  3 us (2%)
  other arithmetic  1.8 us (1%)
    pallas_call x7, Pallas kernels, sum_step(): pl.pallas_call(functools.partial(sum_kernel, counts, carried is None), ou...  31.3 us
    ppermute x16, starting transfers between devices, hop(): return lax.ppermute(values, 'section', pairs)  20.1 us
    ppermute x27, starting transfers between devices, exchange(): lax.ppermute(values, 'section', [(s, s ^ bits) for s in range(sections)])  15.9 us
    ppermute x16, waiting for transfers between devices, hop(): return lax.ppermute(values, 'section', pairs)  15.8 us
    pallas_call x2, Pallas kernels, attend(): pl.pallas_call(functools.partial(attend_kernel, counts, merging, width),...  14.5 us
    ppermute x27, waiting for transfers between devices, exchange(): lax.ppermute(values, 'section', [(s, s ^ bits) for s in range(sections)])  11.9 us
    dot_general x1, matrix products, ring_body(): jnp.einsum('td,hdk->htk', normed, w_query, preferred_element_type=jnp.flo...  3.89 us
  transfers between devices with their start and end apart: 43, of which 13 were waited for; matrix products, arithmetic and copies ran while one was open for 6% of the time, Pallas kernels for 31%

profile of v2, /device:TPU:0, one launch (start us, length us, event | category | flops | bytes accessed | tf_op | source)
XLA Modules:
  0.0 120.3 jit_solution(4483844551246853533)
XLA Ops:
  0.0 1.3 %copy-done.1 = bf16[1024,384]{1,0:T(8,128)(2,1)S(1)} copy-done((bf16[1024,384]{1,0:T(8,128)(2,1)S(1)}, bf16[1024,384]{1,0:T(8,128)(2,1)}, u32[]{:S(2)}) %copy-start.1) | copy-done | bytes 786456
  1.3 0.7 copy-done.3
  2.4 0.5 collective-permute-start.2
  2.9 2.6 %collective-permute-start.18 = (bf16[528,384]{1,0:T(8,128)(2,1)S(1)}, bf16[528,384]{1,0:T(8,128)(2,1)}, u32[]{:S(2)}, u32[]{:S(2)}) collective-permute-start(bf16[528,384]{1,0:T(8,128)(2,1)S(1)} %prepare.3.refs_0_), channel_id=1, source_target_pairs={{0,4},{1,5},{2,0},{3,1},{4,8},{5,9},{6,2},{7,3},{8,12},{9,13},{10,... | collective-permute-start | bytes 1216520 | tf_op jit(solution)/shard_map/ppermute | solution.py:398
  5.6 1.8 %fusion = f32[128]{0:T(128)S(1)} fusion(bf16[128,6144]{1,0:T(8,128)(2,1)} %share_ref.1), kind=kLoop, calls=%fused_computation.2 | loop fusion | flops 2359168 | bytes 1573376 | tf_op jit(solution)/shard_map/reduce_sum | solution.py:21
  7.4 3.9 %fusion.14.refs_0_.refs_7_ = bf16[4,128,128]{2,1,0:T(8,128)(2,1)S(1)} fusion(bf16[4,6144,128]{2,1,0:T(8,128)(2,1)} %param.12, bf16[128,6144]{1,0:T(8,128)(2,1)S(1)} %copy-done, f32[6144]{0:T(1024)S(1)} %bitcast.31, f32[128]{0:T(128)S(1)} %add_rsqrt_fusion), kind=kOutput, calls=%fused_computation.11 | convolution fusion | flops 808583168 | bytes 8020480 | tf_op jit(solution)/shard_map/td,hdk->htk/dot_general | solution.py:424
  11.8 2.0 %collective-permute-start = (bf16[528,384]{1,0:T(8,128)(2,1)S(1)}, bf16[528,384]{1,0:T(8,128)(2,1)}, u32[]{:S(2)}, u32[]{:S(2)}) collective-permute-start(bf16[528,384]{1,0:T(8,128)(2,1)S(1)} %prepare.2.refs_0_), channel_id=1, source_target_pairs={{0,4},{1,5},{2,0},{3,1},{4,8},{5,9},{6,2},{7,3},{8,12},{9,13},{10,... | collective-permute-start | bytes 1216520 | tf_op jit(solution)/shard_map/ppermute | solution.py:398
  13.8 2.0 %collective-permute-done.18.refs_0_ = bf16[528,384]{1,0:T(8,128)(2,1)} collective-permute-done((bf16[528,384]{1,0:T(8,128)(2,1)S(1)}, bf16[528,384]{1,0:T(8,128)(2,1)}, u32[]{:S(2)}, u32[]{:S(2)}) %collective-permute-start.18) | collective-permute-done | bytes 405536 | tf_op jit(solution)/shard_map/ppermute | solution.py:398
  15.8 2.0 %collective-permute-done.19.refs_1_ = bf16[528,384]{1,0:T(8,128)(2,1)} collective-permute-done((bf16[528,384]{1,0:T(8,128)(2,1)S(1)}, bf16[528,384]{1,0:T(8,128)(2,1)}, u32[]{:S(2)}, u32[]{:S(2)}) %collective-permute-start.19) | collective-permute-done | bytes 405536 | tf_op jit(solution)/shard_map/ppermute | solution.py:398
  17.9 0.5 collective-permute-start.23
  18.4 1.6 %collective-permute-start.20 = (bf16[528,384]{1,0:T(8,128)(2,1)}, bf16[528,384]{1,0:T(8,128)(2,1)S(1)}, u32[]{:S(2)}, u32[]{:S(2)}) collective-permute-start(bf16[528,384]{1,0:T(8,128)(2,1)} %collective-permute-done.18.refs_0_), channel_id=1, source_target_pairs={{0,4},{1,5},{2,0},{3,1},{4,8},{5,9},{6,2},{7,3},{8,12},{9,13},{10,... | collective-permute-start | bytes 1216520 | tf_op jit(solution)/shard_map/ppermute | solution.py:398
  20.0 4.6 %collective-permute-done.refs_2_ = bf16[528,384]{1,0:T(8,128)(2,1)} collective-permute-done((bf16[528,384]{1,0:T(8,128)(2,1)S(1)}, bf16[528,384]{1,0:T(8,128)(2,1)}, u32[]{:S(2)}, u32[]{:S(2)}) %collective-permute-start) | collective-permute-done | bytes 405536 | tf_op jit(solution)/shard_map/ppermute | solution.py:398
  24.5 1.9 %collective-permute-start.21 = (bf16[528,384]{1,0:T(8,128)(2,1)}, bf16[528,384]{1,0:T(8,128)(2,1)S(1)}, u32[]{:S(2)}, u32[]{:S(2)}) collective-permute-start(bf16[528,384]{1,0:T(8,128)(2,1)} %collective-permute-done.19.refs_1_), channel_id=1, source_target_pairs={{0,2},{1,3},{2,6},{3,7},{4,0},{5,1},{6,10},{7,11},{8,4},{9,5},{10,... | collective-permute-start | bytes 1216520 | tf_op jit(solution)/shard_map/ppermute | solution.py:398
  26.5 0.7 constant_dynamic-slice_fusion
  27.3 3.1 %sum_step.7 = (f32[4,512,256]{2,1,0:T(8,128)S(1)}, f32[16,384]{1,0:T(8,128)S(1)}) custom-call(s32[2]{0:T(128)S(1)} %get-tuple-element.101.index_ref, bf16[528,384]{1,0:T(8,128)(2,1)S(1)} %prepare.3.refs_0_, bf16[528,384]{1,0:T(8,128)(2,1)S(1)} %collective-permute-done.2.refs_1_, bf16[4,6144,256]{2,1,0:T(8,128)(2,1)} %refs_4_.13), custom_call_target="tpu_custom_call" | custom-call | flops 201326592 | bytes 393216 | tf_op jit(solution)/shard_map/sum_step/pallas_call | solution.py:177
  30.4 0.6 collective-permute-start.6
  31.0 1.8 %collective-permute-done.20.refs_0_ = bf16[528,384]{1,0:T(8,128)(2,1)S(1)} collective-permute-done((bf16[528,384]{1,0:T(8,128)(2,1)}, bf16[528,384]{1,0:T(8,128)(2,1)S(1)}, u32[]{:S(2)}, u32[]{:S(2)}) %collective-permute-start.20) | collective-permute-done | bytes 405536 | tf_op jit(solution)/shard_map/ppermute | solution.py:398
  32.9 1.8 %collective-permute-start.3 = (bf16[528,384]{1,0:T(8,128)(2,1)}, bf16[528,384]{1,0:T(8,128)(2,1)S(1)}, u32[]{:S(2)}, u32[]{:S(2)}) collective-permute-start(bf16[528,384]{1,0:T(8,128)(2,1)} %collective-permute-done.refs_2_), channel_id=1, source_target_pairs={{0,4},{1,5},{2,0},{3,1},{4,8},{5,9},{6,2},{7,3},{8,12},{9,13},{10,... | collective-permute-start | bytes 1216520 | tf_op jit(solution)/shard_map/ppermute | solution.py:398
  34.7 1.0 collective-permute-done.21.refs_1_
  35.6 1.5 %collective-permute-start.4 = (bf16[528,384]{1,0:T(8,128)(2,1)S(1)}, bf16[528,384]{1,0:T(8,128)(2,1)S(1)}, u32[]{:S(2)}, u32[]{:S(2)}) collective-permute-start(bf16[528,384]{1,0:T(8,128)(2,1)S(1)} %collective-permute-done.1.refs_3_), channel_id=1, source_target_pairs={{0,2},{1,3},{2,6},{3,7},{4,0},{5,1},{6,10},{7,11},{8,4},{9,5},{10,... | collective-permute-start | bytes 1216520 | tf_op jit(solution)/shard_map/ppermute | solution.py:398
  37.3 5.1 %sum_step.11 = (f32[4,512,256]{2,1,0:T(8,128)S(1)}, f32[16,384]{1,0:T(8,128)S(1)}) custom-call(s32[4]{0:T(128)S(1)} %get-tuple-element.97.index_ref, bf16[528,384]{1,0:T(8,128)(2,1)} %collective-permute-done.18.refs_0_, bf16[528,384]{1,0:T(8,128)(2,1)} %collective-permute-done.19.refs_1_, ...), custom_call_target="tpu_custom_call", output_to_operand_aliasing={{0}: (6, {}), {1}: (7, {})} | custom-call | flops 402653184 | bytes 786432 | tf_op jit(solution)/shard_map/sum_step/pallas_call | solution.py:177
  42.5 0.5 collective-permute-start.24
  43.2 1.0 collective-permute-done.3.refs_0_
  44.2 1.5 %collective-permute-start.25 = (bf16[528,384]{1,0:T(8,128)(2,1)S(1)}, bf16[528,384]{1,0:T(8,128)(2,1)S(1)}, u32[]{:S(2)}, u32[]{:S(2)}) collective-permute-start(bf16[528,384]{1,0:T(8,128)(2,1)S(1)} %collective-permute-done.21.refs_1_), channel_id=1, source_target_pairs={{0,2},{1,3},{2,6},{3,7},{4,0},{5,1},{6,10},{7,11},{8,4},{9,5},{10,... | collective-permute-start | bytes 1216520 | tf_op jit(solution)/shard_map/ppermute | solution.py:398
  45.8 5.5 %sum_step.8 = (f32[4,512,256]{2,1,0:T(8,128)S(1)}, f32[16,384]{1,0:T(8,128)S(1)}) custom-call(s32[6]{0:T(128)S(1)} %slice_bitcast_fusion.4.index_ref, bf16[528,384]{1,0:T(8,128)(2,1)S(1)} %prepare.2.refs_0_, bf16[528,384]{1,0:T(8,128)(2,1)S(1)} %collective-permute-done.5.refs_1_, bf16[528,384]{1,0:T(8,128)(2,1)} %collective-permute-done.refs_2_, ...), custom_call_target="tpu_custom_call" | custom-call | flops 603979776 | bytes 1179648 | tf_op jit(solution)/shard_map/sum_step/pallas_call | solution.py:177
  52.4 1.9 %collective-permute-done.24.refs_0_ = bf16[528,384]{1,0:T(8,128)(2,1)S(1)} collective-permute-done((bf16[528,384]{1,0:T(8,128)(2,1)S(1)}, bf16[528,384]{1,0:T(8,128)(2,1)S(1)}, u32[]{:S(2)}, u32[]{:S(2)}) %collective-permute-start.24) | collective-permute-done | bytes 405536 | tf_op jit(solution)/shard_map/ppermute | solution.py:398
  54.3 1.6 %collective-permute-start.9 = (bf16[528,384]{1,0:T(8,128)(2,1)S(1)}, bf16[528,384]{1,0:T(8,128)(2,1)S(1)}, u32[]{:S(2)}, u32[]{:S(2)}) collective-permute-start(bf16[528,384]{1,0:T(8,128)(2,1)S(1)} %collective-permute-done.4.refs_1_), channel_id=1, source_target_pairs={{0,2},{1,3},{2,6},{3,7},{4,0},{5,1},{6,10},{7,11},{8,4},{9,5},{10,... | collective-permute-start | bytes 1216520 | tf_op jit(solution)/shard_map/ppermute | solution.py:398
  55.9 4.4 %sum_step.12 = (f32[4,512,256]{2,1,0:T(8,128)S(1)}, f32[16,384]{1,0:T(8,128)S(1)}) custom-call(s32[4]{0:T(128)S(1)} %get-tuple-element.99.index_ref, bf16[528,384]{1,0:T(8,128)(2,1)S(1)} %collective-permute-done.20.refs_0_, bf16[528,384]{1,0:T(8,128)(2,1)S(1)} %collective-permute-done.21.refs_1_, ...), custom_call_target="tpu_custom_call", output_to_operand_aliasing={{0}: (6, {}), {1}: (7, {})} | custom-call | flops 402653184 | bytes 786432 | tf_op jit(solution)/shard_map/sum_step/pallas_call | solution.py:177
  61.4 4.4 %sum_step.9 = (f32[4,512,256]{2,1,0:T(8,128)S(1)}, f32[16,384]{1,0:T(8,128)S(1)}) custom-call(s32[4]{0:T(128)S(1)} %get-tuple-element.99.index_ref, bf16[528,384]{1,0:T(8,128)(2,1)S(1)} %collective-permute-done.3.refs_0_, bf16[528,384]{1,0:T(8,128)(2,1)S(1)} %collective-permute-done.4.refs_1_, ...), custom_call_target="tpu_custom_call", output_to_operand_aliasing={{0}: (6, {}), {1}: (7, {})} | custom-call | flops 402653184 | bytes 786432 | tf_op jit(solution)/shard_map/sum_step/pallas_call | solution.py:177
  66.4 1.4 %collective-permute-done.28.refs_0_ = bf16[256,384]{1,0:T(8,128)(2,1)S(1)} collective-permute-done((bf16[256,384]{1,0:T(8,128)(2,1)S(1)}, bf16[256,384]{1,0:T(8,128)(2,1)S(1)}, u32[]{:S(2)}, u32[]{:S(2)}) %collective-permute-start.28) | collective-permute-done | bytes 196640 | tf_op jit(solution)/shard_map/ppermute | solution.py:398
  67.8 1.6 %collective-permute-start.29 = (bf16[272,384]{1,0:T(8,128)(2,1)S(1)}, bf16[272,384]{1,0:T(8,128)(2,1)S(1)}, u32[]{:S(2)}, u32[]{:S(2)}) collective-permute-start(bf16[272,384]{1,0:T(8,128)(2,1)S(1)} %slice.73), channel_id=1, source_target_pairs={{0,2},{1,3},{2,6},{3,7},{4,0},{5,1},{6,10},{7,11},{8,4},{9,5},{10,... | collective-permute-start | bytes 626696 | tf_op jit(solution)/shard_map/ppermute | solution.py:398
  69.4 1.6 %collective-permute-start.13 = (bf16[272,384]{1,0:T(8,128)(2,1)S(1)}, bf16[272,384]{1,0:T(8,128)(2,1)S(1)}, u32[]{:S(2)}, u32[]{:S(2)}) collective-permute-start(bf16[272,384]{1,0:T(8,128)(2,1)S(1)} %slice.65), channel_id=1, source_target_pairs={{0,2},{1,3},{2,6},{3,7},{4,0},{5,1},{6,10},{7,11},{8,4},{9,5},{10,... | collective-permute-start | bytes 626696 | tf_op jit(solution)/shard_map/ppermute | solution.py:398
  71.1 0.7 collective-permute-start.12
  71.8 4.4 %sum_step.13 = (f32[4,512,256]{2,1,0:T(8,128)S(1)}, f32[16,384]{1,0:T(8,128)S(1)}) custom-call(s32[4]{0:T(128)S(1)} %get-tuple-element.98.index_ref, bf16[528,384]{1,0:T(8,128)(2,1)S(1)} %collective-permute-done.24.refs_0_, bf16[528,384]{1,0:T(8,128)(2,1)S(1)} %collective-permute-done.25.refs_1_, ...), custom_call_target="tpu_custom_call", output_to_operand_aliasing={{0}: (6, {}), {1}: (7, {})} | custom-call | flops 402653184 | bytes 786432 | tf_op jit(solution)/shard_map/sum_step/pallas_call | solution.py:177
  76.8 4.4 %sum_step.10 = (f32[4,512,256]{2,1,0:T(8,128)S(1)}, f32[16,384]{1,0:T(8,128)S(1)}) custom-call(s32[4]{0:T(128)S(1)} %get-tuple-element.98.index_ref, bf16[528,384]{1,0:T(8,128)(2,1)S(1)} %collective-permute-done.8.refs_0_, bf16[528,384]{1,0:T(8,128)(2,1)S(1)} %collective-permute-done.9.refs_1_, ...), custom_call_target="tpu_custom_call", output_to_operand_aliasing={{0}: (6, {}), {1}: (7, {})} | custom-call | flops 402653184 | bytes 786432 | tf_op jit(solution)/shard_map/sum_step/pallas_call | solution.py:177
  81.8 5.6 %attend.2 = (f32[4,128,128]{2,1,0:T(8,128)S(1)}, f32[4,128,128]{2,1,0:T(8,128)S(1)}, f32[4,128,128]{2,1,0:T(8,128)S(1)}) custom-call(s32[2]{0:T(128)S(1)} %get-tuple-element.100.index_ref, bf16[256,384]{1,0:T(8,128)(2,1)S(1)} %collective-permute-done.28.refs_0_, bf16[272,384]{1,0:T(8,128)(2,1)S(1)} %collective-permute-done.29.refs_1_, ...), custom_call_target="tpu_custom_call" | custom-call | flops 201326592 | bytes 393216 | tf_op jit(solution)/shard_map/attend/pallas_call | solution.py:292
  87.5 8.9 %attend.3 = (bf16[8,128,384]{2,1,0:T(8,128)(2,1)S(1)}, f32[8,128,384]{2,1,0:T(8,128)S(1)}) custom-call(s32[18]{0:T(128)S(1)} %slice_bitcast_fusion.6.index_ref, bf16[256,384]{1,0:T(8,128)(2,1)S(1)} %collective-permute-done.12.refs_0_, bf16[272,384]{1,0:T(8,128)(2,1)S(1)} %collective-permute-done.13.refs_1_, ...), custom_call_target="tpu_custom_call" | custom-call | flops 201326592 | bytes 393216 | tf_op jit(solution)/shard_map/attend/pallas_call | solution.py:292
  96.5 2.2 %collective-permute-done.34.other_ref = bf16[8,128,384]{2,1,0:T(8,128)(2,1)S(1)} collective-permute-done((bf16[8,128,384]{2,1,0:T(8,128)(2,1)S(1)}, bf16[8,128,384]{2,1,0:T(8,128)(2,1)S(1)}, u32[]{:S(2)}, u32[]{:S(2)}) %collective-permute-start.34) | collective-permute-done | bytes 786464 | tf_op jit(solution)/shard_map/ppermute | solution.py:401
  98.9 1.6 %collective-permute-start.39 = (bf16[4,64,384]{2,1,0:T(8,128)(2,1)S(1)}, bf16[4,64,384]{2,1,0:T(8,128)(2,1)S(1)}, u32[]{:S(2)}, u32[]{:S(2)}) collective-permute-start(bf16[4,64,384]{2,1,0:T(8,128)(2,1)S(1)} %get-tuple-element.92), channel_id=1, source_target_pairs={{0,2},{1,3},{2,0},{3,1},{4,6},{5,7},{6,4},{7,5},{8,10},{9,11},{10,... | collective-permute-start | bytes 589832 | tf_op jit(solution)/shard_map/ppermute | solution.py:401
  101.0 5.7 %collective-permute-done.39.other_ref = bf16[4,64,384]{2,1,0:T(8,128)(2,1)S(1)} collective-permute-done((bf16[4,64,384]{2,1,0:T(8,128)(2,1)S(1)}, bf16[4,64,384]{2,1,0:T(8,128)(2,1)S(1)}, u32[]{:S(2)}, u32[]{:S(2)}) %collective-permute-start.39) | collective-permute-done | bytes 196640 | tf_op jit(solution)/shard_map/ppermute | solution.py:401
  106.7 0.8 collective-permute-start.40
  107.6 1.7 %collective-permute-start.41 = (bf16[64,384]{1,0:T(8,128)(2,1)S(1)}, bf16[64,384]{1,0:T(8,128)(2,1)S(1)}, u32[]{:S(2)}, u32[]{:S(2)}) collective-permute-start(bf16[64,384]{1,0:T(8,128)(2,1)S(1)} %get-tuple-element.95), channel_id=1, source_target_pairs={{0,8},{1,9},{2,10},{3,11},{4,12},{5,13},{6,14},{7,15},{8,0},{9,1},... | collective-permute-start | bytes 147464 | tf_op jit(solution)/shard_map/ppermute | solution.py:401
  109.2 2.0 %collective-permute-start.42 = (bf16[64,384]{1,0:T(8,128)(2,1)S(1)}, bf16[64,384]{1,0:T(8,128)(2,1)S(1)}, u32[]{:S(2)}, u32[]{:S(2)}) collective-permute-start(bf16[64,384]{1,0:T(8,128)(2,1)S(1)} %get-tuple-element.96), channel_id=1, source_target_pairs={{0,12},{1,13},{2,14},{3,15},{4,8},{5,9},{6,10},{7,11},{8,4},{9,5},... | collective-permute-start | bytes 147464 | tf_op jit(solution)/shard_map/ppermute | solution.py:401
  111.3 2.4 %collective-permute-start.37 = (bf16[64,384]{1,0:T(8,128)(2,1)S(1)}, bf16[64,384]{1,0:T(8,128)(2,1)S(1)}, u32[]{:S(2)}, u32[]{:S(2)}) collective-permute-start(bf16[64,384]{1,0:T(8,128)(2,1)S(1)} %get-tuple-element.90), channel_id=1, source_target_pairs={{0,8},{1,9},{2,10},{3,11},{4,12},{5,13},{6,14},{7,15},{8,0},{9,1},... | collective-permute-start | bytes 147464 | tf_op jit(solution)/shard_map/ppermute | solution.py:401
  113.7 2.0 %collective-permute-start.38 = (bf16[64,384]{1,0:T(8,128)(2,1)S(1)}, bf16[64,384]{1,0:T(8,128)(2,1)S(1)}, u32[]{:S(2)}, u32[]{:S(2)}) collective-permute-start(bf16[64,384]{1,0:T(8,128)(2,1)S(1)} %get-tuple-element.91), channel_id=1, source_target_pairs={{0,12},{1,13},{2,14},{3,15},{4,8},{5,9},{6,10},{7,11},{8,4},{9,5},... | collective-permute-start | bytes 147464 | tf_op jit(solution)/shard_map/ppermute | solution.py:401
  115.7 1.2 %collective-permute-done.36.refs_1_ = bf16[64,384]{1,0:T(8,128)(2,1)S(1)} collective-permute-done((bf16[64,384]{1,0:T(8,128)(2,1)S(1)}, bf16[64,384]{1,0:T(8,128)(2,1)S(1)}, u32[]{:S(2)}, u32[]{:S(2)}) %collective-permute-start.36) | collective-permute-done | bytes 49184 | tf_op jit(solution)/shard_map/ppermute | solution.py:401
  117.3 2.3 %collective-permute-done.38.refs_3_ = bf16[64,384]{1,0:T(8,128)(2,1)S(1)} collective-permute-done((bf16[64,384]{1,0:T(8,128)(2,1)S(1)}, bf16[64,384]{1,0:T(8,128)(2,1)S(1)}, u32[]{:S(2)}, u32[]{:S(2)}) %collective-permute-start.38) | collective-permute-done | bytes 49184 | tf_op jit(solution)/shard_map/ppermute | solution.py:401
  119.6 0.7 finish.1
  (77 shorter events, 6.7 us)
Async XLA Ops:
  0.0 7.4 %copy-start = (bf16[128,6144]{1,0:T(8,128)(2,1)S(1)}, bf16[128,6144]{1,0:T(8,128)(2,1)}, u32[]{:S(2)}) copy-start(bf16[128,6144]{1,0:T(8,128)(2,1)} %share_ref.1) | copy-start | bytes 4718596
  0.0 1.3 %copy-start.1 = (bf16[1024,384]{1,0:T(8,128)(2,1)S(1)}, bf16[1024,384]{1,0:T(8,128)(2,1)}, u32[]{:S(2)}) copy-start(bf16[1024,384]{1,0:T(8,128)(2,1)} %rows_ref.3) | copy-start | bytes 2359300
  2.0 5.4 %copy-start.5 = (f32[1,6144]{1,0:T(1,128)S(1)}, f32[1,6144]{1,0:T(1,128)}, u32[]{:S(2)}) copy-start(f32[1,6144]{1,0:T(1,128)} %param.11) | copy-start | bytes 73732
  2.4 16.0 %collective-permute-start.2 = (bf16[528,384]{1,0:T(8,128)(2,1)S(1)}, bf16[528,384]{1,0:T(8,128)(2,1)S(1)}, u32[]{:S(2)}, u32[]{:S(2)}) collective-permute-start(bf16[528,384]{1,0:T(8,128)(2,1)S(1)} %prepare.3.refs_0_), channel_id=1, source_target_pairs={{0,1},{1,0},{2,3},{3,2},{4,5},{5,4},{6,7},{7,6},{8,9},{9,8},{10,11... | collective-permute-start | bytes 1216520 | tf_op jit(solution)/shard_map/ppermute | solution.py:401
  2.9 12.9 %collective-permute-start.18 = (bf16[528,384]{1,0:T(8,128)(2,1)S(1)}, bf16[528,384]{1,0:T(8,128)(2,1)}, u32[]{:S(2)}, u32[]{:S(2)}) collective-permute-start(bf16[528,384]{1,0:T(8,128)(2,1)S(1)} %prepare.3.refs_0_), channel_id=1, source_target_pairs={{0,4},{1,5},{2,0},{3,1},{4,8},{5,9},{6,2},{7,3},{8,12},{9,13},{10,... | collective-permute-start | bytes 1216520 | tf_op jit(solution)/shard_map/ppermute | solution.py:398
  5.6 12.3 %collective-permute-start.19 = (bf16[528,384]{1,0:T(8,128)(2,1)S(1)}, bf16[528,384]{1,0:T(8,128)(2,1)}, u32[]{:S(2)}, u32[]{:S(2)}) collective-permute-start(bf16[528,384]{1,0:T(8,128)(2,1)S(1)} %prepare.3.refs_0_), channel_id=1, source_target_pairs={{0,2},{1,3},{2,6},{3,7},{4,0},{5,1},{6,10},{7,11},{8,4},{9,5},{10,... | collective-permute-start | bytes 1216520 | tf_op jit(solution)/shard_map/ppermute | solution.py:398
  7.4 3.9 %copy-start.2 = (bf16[1024,384]{1,0:T(8,128)(2,1)S(1)}, bf16[1024,384]{1,0:T(8,128)(2,1)}, u32[]{:S(2)}) copy-start(bf16[1024,384]{1,0:T(8,128)(2,1)} %rows_ref.3) | copy-start | bytes 2359300
  7.4 3.9 %copy-start.4 = (f32[6144]{0:T(1024)S(1)}, f32[6144]{0:T(1024)}, u32[]{:S(2)}) copy-start(f32[6144]{0:T(1024)} %param.9) | copy-start | bytes 73732
  11.8 12.8 %collective-permute-start = (bf16[528,384]{1,0:T(8,128)(2,1)S(1)}, bf16[528,384]{1,0:T(8,128)(2,1)}, u32[]{:S(2)}, u32[]{:S(2)}) collective-permute-start(bf16[528,384]{1,0:T(8,128)(2,1)S(1)} %prepare.2.refs_0_), channel_id=1, source_target_pairs={{0,4},{1,5},{2,0},{3,1},{4,8},{5,9},{6,2},{7,3},{8,12},{9,13},{10,... | collective-permute-start | bytes 1216520 | tf_op jit(solution)/shard_map/ppermute | solution.py:398
  13.8 13.4 %collective-permute-start.1 = (bf16[528,384]{1,0:T(8,128)(2,1)S(1)}, bf16[528,384]{1,0:T(8,128)(2,1)S(1)}, u32[]{:S(2)}, u32[]{:S(2)}) collective-permute-start(bf16[528,384]{1,0:T(8,128)(2,1)S(1)} %prepare.2.refs_0_), channel_id=1, source_target_pairs={{0,2},{1,3},{2,6},{3,7},{4,0},{5,1},{6,10},{7,11},{8,4},{9,5},{10,... | collective-permute-start | bytes 1216520 | tf_op jit(solution)/shard_map/ppermute | solution.py:398
  17.9 12.5 %collective-permute-start.22 = (bf16[528,384]{1,0:T(8,128)(2,1)}, bf16[528,384]{1,0:T(8,128)(2,1)}, u32[]{:S(2)}, u32[]{:S(2)}) collective-permute-start(bf16[528,384]{1,0:T(8,128)(2,1)} %collective-permute-done.18.refs_0_), channel_id=1, source_target_pairs={{0,1},{1,0},{2,3},{3,2},{4,5},{5,4},{6,7},{7,6},{8,9},{9,8},{10,11... | collective-permute-start | bytes 1216520 | tf_op jit(solution)/shard_map/ppermute | solution.py:401
  17.9 13.1 %collective-permute-start.23 = (bf16[528,384]{1,0:T(8,128)(2,1)}, bf16[528,384]{1,0:T(8,128)(2,1)}, u32[]{:S(2)}, u32[]{:S(2)}) collective-permute-start(bf16[528,384]{1,0:T(8,128)(2,1)} %collective-permute-done.19.refs_1_), channel_id=1, source_target_pairs={{0,1},{1,0},{2,3},{3,2},{4,5},{5,4},{6,7},{7,6},{8,9},{9,8},{10,11... | collective-permute-start | bytes 1216520 | tf_op jit(solution)/shard_map/ppermute | solution.py:401
  18.4 14.5 %collective-permute-start.20 = (bf16[528,384]{1,0:T(8,128)(2,1)}, bf16[528,384]{1,0:T(8,128)(2,1)S(1)}, u32[]{:S(2)}, u32[]{:S(2)}) collective-permute-start(bf16[528,384]{1,0:T(8,128)(2,1)} %collective-permute-done.18.refs_0_), channel_id=1, source_target_pairs={{0,4},{1,5},{2,0},{3,1},{4,8},{5,9},{6,2},{7,3},{8,12},{9,13},{10,... | collective-permute-start | bytes 1216520 | tf_op jit(solution)/shard_map/ppermute | solution.py:398
  24.5 11.1 %collective-permute-start.21 = (bf16[528,384]{1,0:T(8,128)(2,1)}, bf16[528,384]{1,0:T(8,128)(2,1)S(1)}, u32[]{:S(2)}, u32[]{:S(2)}) collective-permute-start(bf16[528,384]{1,0:T(8,128)(2,1)} %collective-permute-done.19.refs_1_), channel_id=1, source_target_pairs={{0,2},{1,3},{2,6},{3,7},{4,0},{5,1},{6,10},{7,11},{8,4},{9,5},{10,... | collective-permute-start | bytes 1216520 | tf_op jit(solution)/shard_map/ppermute | solution.py:398
  27.2 15.2 %collective-permute-start.5 = (bf16[528,384]{1,0:T(8,128)(2,1)S(1)}, bf16[528,384]{1,0:T(8,128)(2,1)S(1)}, u32[]{:S(2)}, u32[]{:S(2)}) collective-permute-start(bf16[528,384]{1,0:T(8,128)(2,1)S(1)} %prepare.2.refs_0_), channel_id=1, source_target_pairs={{0,1},{1,0},{2,3},{3,2},{4,5},{5,4},{6,7},{7,6},{8,9},{9,8},{10,11... | collective-permute-start | bytes 1216520 | tf_op jit(solution)/shard_map/ppermute | solution.py:401
  30.4 12.1 %collective-permute-start.6 = (bf16[528,384]{1,0:T(8,128)(2,1)}, bf16[528,384]{1,0:T(8,128)(2,1)S(1)}, u32[]{:S(2)}, u32[]{:S(2)}) collective-permute-start(bf16[528,384]{1,0:T(8,128)(2,1)} %collective-permute-done.refs_2_), channel_id=1, source_target_pairs={{0,1},{1,0},{2,3},{3,2},{4,5},{5,4},{6,7},{7,6},{8,9},{9,8},{10,11... | collective-permute-start | bytes 1216520 | tf_op jit(solution)/shard_map/ppermute | solution.py:401
  31.0 12.1 %collective-permute-start.7 = (bf16[528,384]{1,0:T(8,128)(2,1)S(1)}, bf16[528,384]{1,0:T(8,128)(2,1)S(1)}, u32[]{:S(2)}, u32[]{:S(2)}) collective-permute-start(bf16[528,384]{1,0:T(8,128)(2,1)S(1)} %collective-permute-done.1.refs_3_), channel_id=1, source_target_pairs={{0,1},{1,0},{2,3},{3,2},{4,5},{5,4},{6,7},{7,6},{8,9},{9,8},{10,11... | collective-permute-start | bytes 1216520 | tf_op jit(solution)/shard_map/ppermute | solution.py:401
  32.9 11.4 %collective-permute-start.3 = (bf16[528,384]{1,0:T(8,128)(2,1)}, bf16[528,384]{1,0:T(8,128)(2,1)S(1)}, u32[]{:S(2)}, u32[]{:S(2)}) collective-permute-start(bf16[528,384]{1,0:T(8,128)(2,1)} %collective-permute-done.refs_2_), channel_id=1, source_target_pairs={{0,4},{1,5},{2,0},{3,1},{4,8},{5,9},{6,2},{7,3},{8,12},{9,13},{10,... | collective-permute-start | bytes 1216520 | tf_op jit(solution)/shard_map/ppermute | solution.py:398
  35.6 15.7 %collective-permute-start.4 = (bf16[528,384]{1,0:T(8,128)(2,1)S(1)}, bf16[528,384]{1,0:T(8,128)(2,1)S(1)}, u32[]{:S(2)}, u32[]{:S(2)}) collective-permute-start(bf16[528,384]{1,0:T(8,128)(2,1)S(1)} %collective-permute-done.1.refs_3_), channel_id=1, source_target_pairs={{0,2},{1,3},{2,6},{3,7},{4,0},{5,1},{6,10},{7,11},{8,4},{9,5},{10,... | collective-permute-start | bytes 1216520 | tf_op jit(solution)/shard_map/ppermute | solution.py:398
  42.4 9.0 %collective-permute-start.26 = (bf16[528,384]{1,0:T(8,128)(2,1)S(1)}, bf16[528,384]{1,0:T(8,128)(2,1)S(1)}, u32[]{:S(2)}, u32[]{:S(2)}) collective-permute-start(bf16[528,384]{1,0:T(8,128)(2,1)S(1)} %collective-permute-done.20.refs_0_), channel_id=1, source_target_pairs={{0,1},{1,0},{2,3},{3,2},{4,5},{5,4},{6,7},{7,6},{8,9},{9,8},{10,11... | collective-permute-start | bytes 1216520 | tf_op jit(solution)/shard_map/ppermute | solution.py:401
  42.5 11.8 %collective-permute-start.24 = (bf16[528,384]{1,0:T(8,128)(2,1)S(1)}, bf16[528,384]{1,0:T(8,128)(2,1)S(1)}, u32[]{:S(2)}, u32[]{:S(2)}) collective-permute-start(bf16[528,384]{1,0:T(8,128)(2,1)S(1)} %collective-permute-done.20.refs_0_), channel_id=1, source_target_pairs={{0,4},{1,5},{2,0},{3,1},{4,8},{5,9},{6,2},{7,3},{8,12},{9,13},{10,... | collective-permute-start | bytes 1216520 | tf_op jit(solution)/shard_map/ppermute | solution.py:398
  43.0 8.8 %collective-permute-start.27 = (bf16[528,384]{1,0:T(8,128)(2,1)S(1)}, bf16[528,384]{1,0:T(8,128)(2,1)S(1)}, u32[]{:S(2)}, u32[]{:S(2)}) collective-permute-start(bf16[528,384]{1,0:T(8,128)(2,1)S(1)} %collective-permute-done.21.refs_1_), channel_id=1, source_target_pairs={{0,1},{1,0},{2,3},{3,2},{4,5},{5,4},{6,7},{7,6},{8,9},{9,8},{10,11... | collective-permute-start | bytes 1216520 | tf_op jit(solution)/shard_map/ppermute | solution.py:401
  44.2 16.0 %collective-permute-start.25 = (bf16[528,384]{1,0:T(8,128)(2,1)S(1)}, bf16[528,384]{1,0:T(8,128)(2,1)S(1)}, u32[]{:S(2)}, u32[]{:S(2)}) collective-permute-start(bf16[528,384]{1,0:T(8,128)(2,1)S(1)} %collective-permute-done.21.refs_1_), channel_id=1, source_target_pairs={{0,2},{1,3},{2,6},{3,7},{4,0},{5,1},{6,10},{7,11},{8,4},{9,5},{10,... | collective-permute-start | bytes 1216520 | tf_op jit(solution)/shard_map/ppermute | solution.py:398
  51.3 9.0 %collective-permute-start.10 = (bf16[528,384]{1,0:T(8,128)(2,1)S(1)}, bf16[528,384]{1,0:T(8,128)(2,1)S(1)}, u32[]{:S(2)}, u32[]{:S(2)}) collective-permute-start(bf16[528,384]{1,0:T(8,128)(2,1)S(1)} %collective-permute-done.3.refs_0_), channel_id=1, source_target_pairs={{0,1},{1,0},{2,3},{3,2},{4,5},{5,4},{6,7},{7,6},{8,9},{9,8},{10,11... | collective-permute-start | bytes 1216520 | tf_op jit(solution)/shard_map/ppermute | solution.py:401
  51.4 9.5 %collective-permute-start.11 = (bf16[528,384]{1,0:T(8,128)(2,1)S(1)}, bf16[528,384]{1,0:T(8,128)(2,1)S(1)}, u32[]{:S(2)}, u32[]{:S(2)}) collective-permute-start(bf16[528,384]{1,0:T(8,128)(2,1)S(1)} %collective-permute-done.4.refs_1_), channel_id=1, source_target_pairs={{0,1},{1,0},{2,3},{3,2},{4,5},{5,4},{6,7},{7,6},{8,9},{9,8},{10,11... | collective-permute-start | bytes 1216520 | tf_op jit(solution)/shard_map/ppermute | solution.py:401
  51.9 13.9 %collective-permute-start.8 = (bf16[528,384]{1,0:T(8,128)(2,1)S(1)}, bf16[528,384]{1,0:T(8,128)(2,1)S(1)}, u32[]{:S(2)}, u32[]{:S(2)}) collective-permute-start(bf16[528,384]{1,0:T(8,128)(2,1)S(1)} %collective-permute-done.3.refs_0_), channel_id=1, source_target_pairs={{0,4},{1,5},{2,0},{3,1},{4,8},{5,9},{6,2},{7,3},{8,12},{9,13},{10,... | collective-permute-start | bytes 1216520 | tf_op jit(solution)/shard_map/ppermute | solution.py:398
  54.3 11.5 %collective-permute-start.9 = (bf16[528,384]{1,0:T(8,128)(2,1)S(1)}, bf16[528,384]{1,0:T(8,128)(2,1)S(1)}, u32[]{:S(2)}, u32[]{:S(2)}) collective-permute-start(bf16[528,384]{1,0:T(8,128)(2,1)S(1)} %collective-permute-done.4.refs_1_), channel_id=1, source_target_pairs={{0,2},{1,3},{2,6},{3,7},{4,0},{5,1},{6,10},{7,11},{8,4},{9,5},{10,... | collective-permute-start | bytes 1216520 | tf_op jit(solution)/shard_map/ppermute | solution.py:398
  60.3 9.2 %collective-permute-start.30 = (bf16[528,384]{1,0:T(8,128)(2,1)S(1)}, bf16[528,384]{1,0:T(8,128)(2,1)S(1)}, u32[]{:S(2)}, u32[]{:S(2)}) collective-permute-start(bf16[528,384]{1,0:T(8,128)(2,1)S(1)} %collective-permute-done.24.refs_0_), channel_id=1, source_target_pairs={{0,1},{1,0},{2,3},{3,2},{4,5},{5,4},{6,7},{7,6},{8,9},{9,8},{10,11... | collective-permute-start | bytes 1216520 | tf_op jit(solution)/shard_map/ppermute | solution.py:401
  60.4 10.7 %collective-permute-start.31 = (bf16[528,384]{1,0:T(8,128)(2,1)S(1)}, bf16[528,384]{1,0:T(8,128)(2,1)S(1)}, u32[]{:S(2)}, u32[]{:S(2)}) collective-permute-start(bf16[528,384]{1,0:T(8,128)(2,1)S(1)} %collective-permute-done.25.refs_1_), channel_id=1, source_target_pairs={{0,1},{1,0},{2,3},{3,2},{4,5},{5,4},{6,7},{7,6},{8,9},{9,8},{10,11... | collective-permute-start | bytes 1216520 | tf_op jit(solution)/shard_map/ppermute | solution.py:401
  60.9 6.9 %collective-permute-start.28 = (bf16[256,384]{1,0:T(8,128)(2,1)S(1)}, bf16[256,384]{1,0:T(8,128)(2,1)S(1)}, u32[]{:S(2)}, u32[]{:S(2)}) collective-permute-start(bf16[256,384]{1,0:T(8,128)(2,1)S(1)} %slice.72), channel_id=1, source_target_pairs={{0,4},{1,5},{2,0},{3,1},{4,8},{5,9},{6,2},{7,3},{8,12},{9,13},{10,... | collective-permute-start | bytes 589832 | tf_op jit(solution)/shard_map/ppermute | solution.py:398
  65.8 10.5 %collective-permute-start.14 = (bf16[528,384]{1,0:T(8,128)(2,1)S(1)}, bf16[528,384]{1,0:T(8,128)(2,1)S(1)}, u32[]{:S(2)}, u32[]{:S(2)}) collective-permute-start(bf16[528,384]{1,0:T(8,128)(2,1)S(1)} %collective-permute-done.8.refs_0_), channel_id=1, source_target_pairs={{0,1},{1,0},{2,3},{3,2},{4,5},{5,4},{6,7},{7,6},{8,9},{9,8},{10,11... | collective-permute-start | bytes 1216520 | tf_op jit(solution)/shard_map/ppermute | solution.py:401
  65.9 10.9 %collective-permute-start.15 = (bf16[528,384]{1,0:T(8,128)(2,1)S(1)}, bf16[528,384]{1,0:T(8,128)(2,1)S(1)}, u32[]{:S(2)}, u32[]{:S(2)}) collective-permute-start(bf16[528,384]{1,0:T(8,128)(2,1)S(1)} %collective-permute-done.9.refs_1_), channel_id=1, source_target_pairs={{0,1},{1,0},{2,3},{3,2},{4,5},{5,4},{6,7},{7,6},{8,9},{9,8},{10,11... | collective-permute-start | bytes 1216520 | tf_op jit(solution)/shard_map/ppermute | solution.py:401
  67.8 8.4 %collective-permute-start.29 = (bf16[272,384]{1,0:T(8,128)(2,1)S(1)}, bf16[272,384]{1,0:T(8,128)(2,1)S(1)}, u32[]{:S(2)}, u32[]{:S(2)}) collective-permute-start(bf16[272,384]{1,0:T(8,128)(2,1)S(1)} %slice.73), channel_id=1, source_target_pairs={{0,2},{1,3},{2,6},{3,7},{4,0},{5,1},{6,10},{7,11},{8,4},{9,5},{10,... | collective-permute-start | bytes 626696 | tf_op jit(solution)/shard_map/ppermute | solution.py:398
  69.4 11.7 %collective-permute-start.13 = (bf16[272,384]{1,0:T(8,128)(2,1)S(1)}, bf16[272,384]{1,0:T(8,128)(2,1)S(1)}, u32[]{:S(2)}, u32[]{:S(2)}) collective-permute-start(bf16[272,384]{1,0:T(8,128)(2,1)S(1)} %slice.65), channel_id=1, source_target_pairs={{0,2},{1,3},{2,6},{3,7},{4,0},{5,1},{6,10},{7,11},{8,4},{9,5},{10,... | collective-permute-start | bytes 626696 | tf_op jit(solution)/shard_map/ppermute | solution.py:398
  71.1 10.1 %collective-permute-start.12 = (bf16[256,384]{1,0:T(8,128)(2,1)S(1)}, bf16[256,384]{1,0:T(8,128)(2,1)S(1)}, u32[]{:S(2)}, u32[]{:S(2)}) collective-permute-start(bf16[256,384]{1,0:T(8,128)(2,1)S(1)} %slice.64), channel_id=1, source_target_pairs={{0,4},{1,5},{2,0},{3,1},{4,8},{5,9},{6,2},{7,3},{8,12},{9,13},{10,... | collective-permute-start | bytes 589832 | tf_op jit(solution)/shard_map/ppermute | solution.py:398
  76.2 5.7 %collective-permute-start.33 = (bf16[272,384]{1,0:T(8,128)(2,1)S(1)}, bf16[272,384]{1,0:T(8,128)(2,1)S(1)}, u32[]{:S(2)}, u32[]{:S(2)}) collective-permute-start(bf16[272,384]{1,0:T(8,128)(2,1)S(1)} %collective-permute-done.29.refs_1_), channel_id=1, source_target_pairs={{0,1},{1,0},{2,3},{3,2},{4,5},{5,4},{6,7},{7,6},{8,9},{9,8},{10,11... | collective-permute-start | bytes 626696 | tf_op jit(solution)/shard_map/ppermute | solution.py:401
  76.3 5.6 %collective-permute-start.32 = (bf16[256,384]{1,0:T(8,128)(2,1)S(1)}, bf16[256,384]{1,0:T(8,128)(2,1)S(1)}, u32[]{:S(2)}, u32[]{:S(2)}) collective-permute-start(bf16[256,384]{1,0:T(8,128)(2,1)S(1)} %collective-permute-done.28.refs_0_), channel_id=1, source_target_pairs={{0,1},{1,0},{2,3},{3,2},{4,5},{5,4},{6,7},{7,6},{8,9},{9,8},{10,11... | collective-permute-start | bytes 589832 | tf_op jit(solution)/shard_map/ppermute | solution.py:401
  81.2 6.3 %collective-permute-start.17 = (bf16[272,384]{1,0:T(8,128)(2,1)S(1)}, bf16[272,384]{1,0:T(8,128)(2,1)S(1)}, u32[]{:S(2)}, u32[]{:S(2)}) collective-permute-start(bf16[272,384]{1,0:T(8,128)(2,1)S(1)} %collective-permute-done.13.refs_1_), channel_id=1, source_target_pairs={{0,1},{1,0},{2,3},{3,2},{4,5},{5,4},{6,7},{7,6},{8,9},{9,8},{10,11... | collective-permute-start | bytes 626696 | tf_op jit(solution)/shard_map/ppermute | solution.py:401
  81.3 6.1 %collective-permute-start.16 = (bf16[256,384]{1,0:T(8,128)(2,1)S(1)}, bf16[256,384]{1,0:T(8,128)(2,1)S(1)}, u32[]{:S(2)}, u32[]{:S(2)}) collective-permute-start(bf16[256,384]{1,0:T(8,128)(2,1)S(1)} %collective-permute-done.12.refs_0_), channel_id=1, source_target_pairs={{0,1},{1,0},{2,3},{3,2},{4,5},{5,4},{6,7},{7,6},{8,9},{9,8},{10,11... | collective-permute-start | bytes 589832 | tf_op jit(solution)/shard_map/ppermute | solution.py:401
  96.4 2.4 %collective-permute-start.34 = (bf16[8,128,384]{2,1,0:T(8,128)(2,1)S(1)}, bf16[8,128,384]{2,1,0:T(8,128)(2,1)S(1)}, u32[]{:S(2)}, u32[]{:S(2)}) collective-permute-start(bf16[8,128,384]{2,1,0:T(8,128)(2,1)S(1)} %get-tuple-element.85), channel_id=1, source_target_pairs={{0,1},{1,0},{2,3},{3,2},{4,5},{5,4},{6,7},{7,6},{8,9},{9,8},{10,11... | collective-permute-start | bytes 2359304 | tf_op jit(solution)/shard_map/ppermute | solution.py:401
  98.9 7.8 %collective-permute-start.39 = (bf16[4,64,384]{2,1,0:T(8,128)(2,1)S(1)}, bf16[4,64,384]{2,1,0:T(8,128)(2,1)S(1)}, u32[]{:S(2)}, u32[]{:S(2)}) collective-permute-start(bf16[4,64,384]{2,1,0:T(8,128)(2,1)S(1)} %get-tuple-element.92), channel_id=1, source_target_pairs={{0,2},{1,3},{2,0},{3,1},{4,6},{5,7},{6,4},{7,5},{8,10},{9,11},{10,... | collective-permute-start | bytes 589832 | tf_op jit(solution)/shard_map/ppermute | solution.py:401
  100.5 10.7 %collective-permute-start.35 = (bf16[4,64,384]{2,1,0:T(8,128)(2,1)S(1)}, bf16[4,64,384]{2,1,0:T(8,128)(2,1)S(1)}, u32[]{:S(2)}, u32[]{:S(2)}) collective-permute-start(bf16[4,64,384]{2,1,0:T(8,128)(2,1)S(1)} %get-tuple-element.87), channel_id=1, source_target_pairs={{0,2},{1,3},{2,0},{3,1},{4,6},{5,7},{6,4},{7,5},{8,10},{9,11},{10,... | collective-permute-start | bytes 589832 | tf_op jit(solution)/shard_map/ppermute | solution.py:401
  106.7 7.0 %collective-permute-start.40 = (bf16[64,384]{1,0:T(8,128)(2,1)S(1)}, bf16[64,384]{1,0:T(8,128)(2,1)S(1)}, u32[]{:S(2)}, u32[]{:S(2)}) collective-permute-start(bf16[64,384]{1,0:T(8,128)(2,1)S(1)} %get-tuple-element.94), channel_id=1, source_target_pairs={{0,4},{1,5},{2,6},{3,7},{4,0},{5,1},{6,2},{7,3},{8,12},{9,13},{10,... | collective-permute-start | bytes 147464 | tf_op jit(solution)/shard_map/ppermute | solution.py:401
  107.6 8.1 %collective-permute-start.41 = (bf16[64,384]{1,0:T(8,128)(2,1)S(1)}, bf16[64,384]{1,0:T(8,128)(2,1)S(1)}, u32[]{:S(2)}, u32[]{:S(2)}) collective-permute-start(bf16[64,384]{1,0:T(8,128)(2,1)S(1)} %get-tuple-element.95), channel_id=1, source_target_pairs={{0,8},{1,9},{2,10},{3,11},{4,12},{5,13},{6,14},{7,15},{8,0},{9,1},... | collective-permute-start | bytes 147464 | tf_op jit(solution)/shard_map/ppermute | solution.py:401
  109.2 6.5 %collective-permute-start.42 = (bf16[64,384]{1,0:T(8,128)(2,1)S(1)}, bf16[64,384]{1,0:T(8,128)(2,1)S(1)}, u32[]{:S(2)}, u32[]{:S(2)}) collective-permute-start(bf16[64,384]{1,0:T(8,128)(2,1)S(1)} %get-tuple-element.96), channel_id=1, source_target_pairs={{0,12},{1,13},{2,14},{3,15},{4,8},{5,9},{6,10},{7,11},{8,4},{9,5},... | collective-permute-start | bytes 147464 | tf_op jit(solution)/shard_map/ppermute | solution.py:401
  111.2 5.7 %collective-permute-start.36 = (bf16[64,384]{1,0:T(8,128)(2,1)S(1)}, bf16[64,384]{1,0:T(8,128)(2,1)S(1)}, u32[]{:S(2)}, u32[]{:S(2)}) collective-permute-start(bf16[64,384]{1,0:T(8,128)(2,1)S(1)} %get-tuple-element.89), channel_id=1, source_target_pairs={{0,4},{1,5},{2,6},{3,7},{4,0},{5,1},{6,2},{7,3},{8,12},{9,13},{10,... | collective-permute-start | bytes 147464 | tf_op jit(solution)/shard_map/ppermute | solution.py:401
  111.3 6.0 %collective-permute-start.37 = (bf16[64,384]{1,0:T(8,128)(2,1)S(1)}, bf16[64,384]{1,0:T(8,128)(2,1)S(1)}, u32[]{:S(2)}, u32[]{:S(2)}) collective-permute-start(bf16[64,384]{1,0:T(8,128)(2,1)S(1)} %get-tuple-element.90), channel_id=1, source_target_pairs={{0,8},{1,9},{2,10},{3,11},{4,12},{5,13},{6,14},{7,15},{8,0},{9,1},... | collective-permute-start | bytes 147464 | tf_op jit(solution)/shard_map/ppermute | solution.py:401
  113.7 5.9 %collective-permute-start.38 = (bf16[64,384]{1,0:T(8,128)(2,1)S(1)}, bf16[64,384]{1,0:T(8,128)(2,1)S(1)}, u32[]{:S(2)}, u32[]{:S(2)}) collective-permute-start(bf16[64,384]{1,0:T(8,128)(2,1)S(1)} %get-tuple-element.91), channel_id=1, source_target_pairs={{0,12},{1,13},{2,14},{3,15},{4,8},{5,9},{6,10},{7,11},{8,4},{9,5},... | collective-permute-start | bytes 147464 | tf_op jit(solution)/shard_map/ppermute | solution.py:401
  (1 other events, 0.7 us)

commit v3 on v2

--- a/solution.py
+++ b/solution.py
@@ -13,7 +13,7 @@
 MAX_RING = 8
 SMALL_MIB = 16
 PARTS = 2
-STEP_MIB = 48
+STEP_MIB = 20
 TILE = 16
 
 
@@ -91,98 +91,63 @@
     return jnp.concatenate(lines, axis=1)
 
 
-def start_blocks(index_ref, slots, pieces, w_ref, rows_at, tiles, weights, rows_sem, tiles_sem, weights_sem):
-    heads = weights.shape[0]
-    rows, features = rows_at.shape[0], tiles.shape[2]
-    row_copies, tile_copies, weight_copies = [], [], []
-    for slot in range(slots):
-        columns = pl.ds(slot * features, features)
-        at = 0
-        for piece in pieces[slot]:
-            size = min(piece.shape[0], rows - at)
-            source = piece.at[pl.ds(0, size), :]
-            target = rows_at.at[pl.ds(at, size), columns]
-            row_copies.append(pltpu.make_async_copy(source, target, rows_sem.at[len(row_copies)]))
-            at += size
-        source = pieces[slot][-1].at[pl.ds(pieces[slot][-1].shape[0] - TILE, TILE), :]
-        tile_copies.append(pltpu.make_async_copy(source, tiles.at[slot], tiles_sem.at[slot]))
-    for head in range(heads):
-        group = []
-        for slot in range(slots):
-            source = w_ref.at[head, pl.ds(pl.multiple_of(index_ref[slot] * features, features), features), :]
-            target = weights.at[head, pl.ds(slot * features, features), :]
-            group.append(pltpu.make_async_copy(source, target, weights_sem.at[head, slot]))
-        weight_copies.append(group)
-    return row_copies, tile_copies, weight_copies
-
-
-def block_scratch(slots, rows, features, heads, pair):
-    pieces = sum(slots)
-    return [
-        pltpu.VMEM((rows, features * len(slots)), jnp.bfloat16),
-        pltpu.VMEM((len(slots), TILE, features), jnp.bfloat16),
-        pltpu.VMEM((heads, features * len(slots), pair), jnp.bfloat16),
-        pltpu.SemaphoreType.DMA((pieces,)),
-        pltpu.SemaphoreType.DMA((len(slots),)),
-        pltpu.SemaphoreType.DMA((heads, len(slots))),
-    ]
-
-
-def start_all(copies):
-    for copy in copies:
-        copy.start()
-
-
-def wait_all(copies):
-    for copy in copies:
-        copy.wait()
-
-
-def sum_kernel(slots, first, index_ref, *refs):
+def slot_weights(index_ref, w_ref, head, slot, features):
+    return w_ref[head, pl.ds(pl.multiple_of(index_ref[slot] * features, features), features), :]
+
+
+def slot_squares(arrays, slots):
+    ends = [(which, at + length) for which, at, length in (parts[-1] for parts in slots)]
+    return sum(arrays[which][end : end + TILE, :].astype(jnp.float32) for which, end in ends)
+
+
+def gather_slots(slots):
+    arrays, placed = [], []
+    for parts in slots:
+        line = []
+        for array, at, length in parts:
+            found = [k for k, known in enumerate(arrays) if known is array]
+            if not found:
+                arrays.append(array)
+            line.append((found[0] if found else len(arrays) - 1, at, length))
+        placed.append(tuple(line))
+    return arrays, tuple(placed)
+
+
+def sum_kernel(slots, count, first, index_ref, *refs):
     refs = list(refs)
-    pieces = [[refs.pop(0) for _ in range(count)] for count in slots]
+    arrays = [refs.pop(0) for _ in range(count)]
     w_ref = refs.pop(0)
     sum_in, tile_in = (None, None) if first else (refs.pop(0), refs.pop(0))
-    sum_out, tile_out, rows_at, tiles, weights, rows_sem, tiles_sem, weights_sem = refs
-    heads = weights.shape[0]
-    row_copies, tile_copies, weight_copies = start_blocks(
-        index_ref, len(slots), pieces, w_ref, rows_at, tiles, weights, rows_sem, tiles_sem, weights_sem
-    )
-    start_all(row_copies)
-    for copies in weight_copies:
-        start_all(copies)
-    start_all(tile_copies)
-    wait_all(row_copies)
-    for pair in range(0, heads, 2):
-        both = range(pair, min(pair + 2, heads))
-        for head in both:
-            wait_all(weight_copies[head])
-        for head in both:
-            term = jnp.dot(rows_at[...], weights[head], preferred_element_type=jnp.float32)
-            sum_out[head] = term if first else sum_in[head] + term
-    wait_all(tile_copies)
-    squares = sum(tiles[slot].astype(jnp.float32) for slot in range(len(slots)))
+    sum_out, tile_out = refs
+    heads = sum_out.shape[0]
+    features = tile_out.shape[1]
+    for head in range(heads):
+        total = None if first else sum_in[head]
+        for slot, ((which, at, length),) in enumerate(slots):
+            term = jnp.dot(
+                arrays[which][at : at + length, :],
+                slot_weights(index_ref, w_ref, head, slot, features),
+                preferred_element_type=jnp.float32,
+            )
+            total = term if total is None else total + term
+        sum_out[head] = total
+    squares = slot_squares(arrays, slots)
     tile_out[...] = squares if first else tile_in[...] + squares
 
 
 def sum_step(index, slots, w_keyval, rows, carried=None):
     heads, width, pair = w_keyval.shape
-    features = slots[0][0].shape[1]
-    counts = tuple(len(parts) for parts in slots)
-    pieces = [piece for parts in slots for piece in parts]
-    operands = pieces + [w_keyval] + list(carried or ())
+    arrays, placed = gather_slots(slots)
+    features = arrays[0].shape[1]
+    operands = arrays + [w_keyval] + list(carried or ())
     whole = pl.BlockSpec(memory_space=pltpu.VMEM)
     depth = features * len(slots)
-    aliases = {} if carried is None else {len(pieces) + 2: 0, len(pieces) + 3: 1}
+    aliases = {} if carried is None else {len(arrays) + 2: 0, len(arrays) + 3: 1}
     return pl.pallas_call(
-        functools.partial(sum_kernel, counts, carried is None),
+        functools.partial(sum_kernel, placed, len(arrays), carried is None),
         out_shape=[pltpu.VMEM((heads, rows, pair), jnp.float32), pltpu.VMEM((TILE, features), jnp.float32)],
         grid_spec=pltpu.PrefetchScalarGridSpec(
-            num_scalar_prefetch=1,
-            grid=(),
-            in_specs=anywhere(len(pieces) + 1) + [whole] * (len(operands) - len(pieces) - 1),
-            out_specs=[whole] * 2,
-            scratch_shapes=block_scratch(counts, rows, features, heads, pair),
+            num_scalar_prefetch=1, grid=(), in_specs=[whole] * len(operands), out_specs=[whole] * 2
         ),
         input_output_aliases=aliases,
         compiler_params=params(STEP_MIB),
@@ -193,41 +158,40 @@
     )(index, *operands)
 
 
-def attend_kernel(slots, merging, width, index_ref, *refs):
+def attend_kernel(slots, count, merging, width, index_ref, *refs):
     refs = list(refs)
-    pieces = [[refs.pop(0) for _ in range(count)] for count in slots]
+    arrays = [refs.pop(0) for _ in range(count)]
     w_ref, sum_in, tile_in, query_ref = [refs.pop(0) for _ in range(4)]
     if merging:
-        context_in, top_in, total_in, w_out_ref = [refs.pop(0) for _ in range(4)]
-        theirs_ref, mine_ref = refs.pop(0), refs.pop(0)
+        context_in, top_in, total_in, w_out_ref, theirs_ref, mine_ref, w_out_at, out_sem, merged = refs
+        out_copies = [
+            pltpu.make_async_copy(w_out_ref.at[head], w_out_at.at[head], out_sem.at[head])
+            for head in range(w_out_at.shape[0])
+        ]
+        for copy in out_copies:
+            copy.start()
     else:
-        context_out, top_out, total_out = [refs.pop(0) for _ in range(3)]
-    rows_at, tiles, weights, rows_sem, tiles_sem, weights_sem = [refs.pop(0) for _ in range(6)]
+        context_out, top_out, total_out = refs
     heads, rows, pair = sum_in.shape
+    features = tile_in.shape[1]
     size = pair // 2
-    row_copies, tile_copies, weight_copies = start_blocks(
-        index_ref, len(slots), pieces, w_ref, rows_at, tiles, weights, rows_sem, tiles_sem, weights_sem
-    )
-    start_all(row_copies)
-    start_all(tile_copies)
+    squares = tile_in[...] + slot_squares(arrays, slots)
+    inverse = lax.rsqrt(lane_sums(squares, rows) / width + epsilon)
     for head in range(heads):
-        start_all(weight_copies[head])
-    if merging:
-        w_out_at, out_sem, merged = refs
-        out_copies = [
-            pltpu.make_async_copy(w_out_ref.at[head], w_out_at.at[head], out_sem.at[head]) for head in range(heads)
-        ]
-        start_all(out_copies)
-    wait_all(tile_copies)
-    squares = sum((tiles[slot].astype(jnp.float32) for slot in range(len(slots))), tile_in[...])
-    inverse = lax.rsqrt(lane_sums(squares, rows) / width + epsilon)
-    wait_all(row_copies)
-    for copies in weight_copies:
-        wait_all(copies)
-    for head in range(heads):
-        keyvals = (
-            sum_in[head] + jnp.dot(rows_at[...], weights[head], preferred_element_type=jnp.float32)
-        ).astype(jnp.bfloat16)
+        parts, first = [], 0
+        for part in range(len(slots[0])):
+            length = slots[0][part][2]
+            total = sum_in[head, first : first + length, :]
+            for slot in range(len(slots)):
+                which, at, _ = slots[slot][part]
+                total = total + jnp.dot(
+                    arrays[which][at : at + length, :],
+                    slot_weights(index_ref, w_ref, head, slot, features),
+                    preferred_element_type=jnp.float32,
+                )
+            parts.append(total.astype(jnp.bfloat16))
+            first += length
+        keyvals = jnp.concatenate(parts, axis=0)
         scores = inverse * lax.dot_general(
             query_ref[head], keyvals[:, :size], (((1,), (1,)), ((), ())), preferred_element_type=jnp.float32
         )
@@ -250,7 +214,8 @@
         merged[:, head * size : (head + 1) * size] = joined.astype(jnp.bfloat16)
     if not merging:
         return
-    wait_all(out_copies)
+    for copy in out_copies:
+        copy.wait()
     count, _, cols = mine_ref.shape
     for part, target in enumerate((theirs_ref, mine_ref)):
         @pl.loop(0, count, unroll=min(count, 4))
@@ -265,20 +230,18 @@
 def attend(index, slots, w_keyval, carried, queries, other=None, w_out=None, blocks=0, cols=0):
     heads, width, pair = w_keyval.shape
     rows = carried[0].shape[1]
-    features = slots[0][0].shape[1]
-    counts = tuple(len(parts) for parts in slots)
+    arrays, placed = gather_slots(slots)
+    features = arrays[0].shape[1]
     target, size = queries.shape[1:]
-    pieces = [piece for parts in slots for piece in parts]
-    operands = pieces + [w_keyval, *carried, queries]
+    operands = arrays + [w_keyval, *carried, queries]
     whole = pl.BlockSpec(memory_space=pltpu.VMEM)
-    in_specs = anywhere(len(pieces) + 1) + [whole] * 3
     depth = features * len(slots)
-    scratch = block_scratch(counts, rows, features, heads, pair)
     merging = other is not None
+    in_specs, scratch = [whole] * len(operands), []
     if merging:
         operands += list(other) + [w_out]
         in_specs += [whole] * 3 + anywhere(1)
-        scratch += [
+        scratch = [
             pltpu.VMEM(w_out.shape, w_out.dtype),
             pltpu.SemaphoreType.DMA((heads,)),
             pltpu.VMEM((target, heads * size), jnp.bfloat16),
@@ -290,7 +253,7 @@
     else:
         out_shape = [pltpu.VMEM((heads, target, last), jnp.float32) for last in (size, 128, 128)]
     return pl.pallas_call(
-        functools.partial(attend_kernel, counts, merging, width),
+        functools.partial(attend_kernel, placed, len(arrays), merging, width),
         out_shape=out_shape,
         grid_spec=pltpu.PrefetchScalarGridSpec(
             num_scalar_prefetch=1,
@@ -425,13 +388,13 @@
     ).astype(jnp.bfloat16)
 
     own = [prepare(position, enc_rows, enc_gain, 0)]
-    own.append(prepare(position, enc_rows, enc_gain, 1, [queries]))
+    own.append(prepare(position, enc_rows, enc_gain, 1, [queries, row]))
 
     carried = [None, None]
-    slots = [[(half,), (swap(half),)] for half in own]
+    slots = [[[(half, 0, half_rows)], [(swap(half), 0, half_rows)]] for half in own]
     held = [(half, half) for half in own]
     flying = [(hop(half, 1), hop(half, -1)) for half in own]
-    token = queries
+    token = own[1]
     for phase in range(2 * far):
         step, which = phase // 2 + 1, phase % 2
         *arrived, token = lax.optimization_barrier((*flying[phase], token))
@@ -440,11 +403,17 @@
         elif step + 1 == far:
             cut = half_rows // 2
             flying.append((hop(arrived[0][:cut], 1), hop(arrived[1][cut:], -1)))
-        other = [swap(part) for part in arrived]
+        other = swap(jnp.concatenate(arrived, axis=0))
+        length = arrived[0].shape[0]
         if step < far:
-            received = [(part,) for part in arrived + other]
+            received = [[(part, 0, half_rows)] for part in arrived]
+            received += [[(other, at, half_rows)] for at in (0, length)]
         else:
-            received = [tuple(arrived), tuple(other)]
+            rest = half_rows - length
+            received = [
+                [(arrived[0], 0, length), (arrived[1], 0, rest)],
+                [(other, 0, length), (other, length, rest)],
+            ]
         slots.append(received)
         if phase == 0:
             todo, half, begin = slots[0], 0, 0
@@ -463,7 +432,8 @@
     parts = []
     for which, send in enumerate(sends):
         first, *others = fold_blocks(which, keep, send)
-        parts.append([first] + [exchange(term, 4 * (line + 1)) for line, term in enumerate(others)])
+        lines = [*range(1, len(others)), 0]
+        parts.append([first] + [exchange(others[line], 4 * (line + 1)) for line in lines])
     return finish(position, dec_input, parts)
 
 

time: 121 us -> 113 us (0.934)
  Pallas kernels: 47.6 us -> 33.4 us
  waiting for transfers between devices: 27.7 us -> 36.8 us
  starting transfers between devices: 36 us -> 31.4 us
  other arithmetic: 1.8 us -> 3.45 us
    pallas_call x9, Pallas kernels: 45.8 us -> 31.6 us  [the longest x7 22.5 us: sum_step(): pl.pallas_call(functools.partial(sum_kernel, placed, len(arrays), carried...]
    ppermute x16, waiting for transfers between devices: 15.8 us -> 24.6 us  [hop(): return lax.ppermute(values, 'section', pairs)]
    ppermute x27 -> x19, starting transfers between devices: 15.9 us -> 12.2 us  [exchange(): lax.ppermute(values, 'section', [(s, s ^ bits) for s in range(sections)])]
    concatenate x0 -> x8, other arithmetic: none -> 1.58 us  [ring_body(): other = swap(jnp.concatenate(arrived, axis=0))]
    ppermute x27 -> x19, waiting for transfers between devices: 11.9 us -> 12.3 us  [exchange(): lax.ppermute(values, 'section', [(s, s ^ bits) for s in range(sections)])]
  transfers between devices with their start and end apart: 43 -> 35, of which waited for: 13 -> 19; matrix products, arithmetic and copies ran while one was open for 6% -> 7% of each run, Pallas kernels for 31% -> 23%
where the time goes in v3:
time: 113 us; the launch traced here: 112 us
  waiting for transfers between devices  36.8 us (33%)
  Pallas kernels  33.4 us (30%)
  starting transfers between devices  31.4 us (28%)
  matrix products  3.97 us (4%)
  other arithmetic  3.45 us (3%)
  local copies, waits for them, and re-layouts  3.02 us (3%)
    ppermute x16, waiting for transfers between devices, hop(): return lax.ppermute(values, 'section', pairs)  24.6 us
    pallas_call x7, Pallas kernels, sum_step(): pl.pallas_call(functools.partial(sum_kernel, placed, len(arrays), carried...  22.5 us
    ppermute x16, starting transfers between devices, hop(): return lax.ppermute(values, 'section', pairs)  19.2 us
    ppermute x19, waiting for transfers between devices, exchange(): lax.ppermute(values, 'section', [(s, s ^ bits) for s in range(sections)])  12.3 us
    ppermute x19, starting transfers between devices, exchange(): lax.ppermute(values, 'section', [(s, s ^ bits) for s in range(sections)])  12.2 us
    pallas_call x2, Pallas kernels, attend(): pl.pallas_call(functools.partial(attend_kernel, placed, len(arrays), merg...  9.11 us
    dot_general x1, matrix products, ring_body(): jnp.einsum('td,hdk->htk', normed, w_query, preferred_element_type=jnp.flo...  3.97 us
  transfers between devices with their start and end apart: 35, of which 19 were waited for; matrix products, arithmetic and copies ran while one was open for 7% of the time, Pallas kernels for 23%

profile of v3, /device:TPU:0, one launch (start us, length us, event | category | flops | bytes accessed | tf_op | source)
XLA Modules:
  0.0 112.4 jit_solution(15851684616898310403)
XLA Ops:
  0.0 1.3 %copy-done.2 = bf16[1024,384]{1,0:T(8,128)(2,1)S(1)} copy-done((bf16[1024,384]{1,0:T(8,128)(2,1)S(1)}, bf16[1024,384]{1,0:T(8,128)(2,1)}, u32[]{:S(2)}) %copy-start.2) | copy-done | bytes 786456
  1.3 0.7 copy-done.4
  2.4 3.1 %collective-permute-start.14 = (bf16[528,384]{1,0:T(8,128)(2,1)S(1)}, bf16[528,384]{1,0:T(8,128)(2,1)}, u32[]{:S(2)}, u32[]{:S(2)}) collective-permute-start(bf16[528,384]{1,0:T(8,128)(2,1)S(1)} %prepare.3.refs_0_), channel_id=1, source_target_pairs={{0,4},{1,5},{2,0},{3,1},{4,8},{5,9},{6,2},{7,3},{8,12},{9,13},{10,... | collective-permute-start | bytes 1216520 | tf_op jit(solution)/shard_map/ppermute | solution.py:361
  5.5 1.9 %fusion = f32[128]{0:T(128)S(1)} fusion(bf16[128,6144]{1,0:T(8,128)(2,1)} %share_ref.1), kind=kLoop, calls=%fused_computation.2 | loop fusion | flops 2359168 | bytes 1573376 | tf_op jit(solution)/shard_map/reduce_sum | solution.py:21
  7.4 0.7 fusion.17
  8.1 4.0 %fusion.14.refs_0_.refs_6_ = bf16[4,128,128]{2,1,0:T(8,128)(2,1)S(1)} fusion(bf16[4,6144,128]{2,1,0:T(8,128)(2,1)} %param.12, bf16[128,6144]{1,0:T(8,128)(2,1)S(1)} %copy-done.1, f32[6144]{0:T(1024)S(1)} %bitcast.35, f32[128]{0:T(128)S(1)} %add_rsqrt_fusion), kind=kOutput, calls=%fused_computation.11 | convolution fusion | flops 808583168 | bytes 8020480 | tf_op jit(solution)/shard_map/td,hdk->htk/dot_general | solution.py:387
  12.5 2.1 %collective-permute-start = (bf16[528,384]{1,0:T(8,128)(2,1)S(1)}, bf16[528,384]{1,0:T(8,128)(2,1)S(1)}, u32[]{:S(2)}, u32[]{:S(2)}) collective-permute-start(bf16[528,384]{1,0:T(8,128)(2,1)S(1)} %prepare.2.refs_0_), channel_id=1, source_target_pairs={{0,4},{1,5},{2,0},{3,1},{4,8},{5,9},{6,2},{7,3},{8,12},{9,13},{10,... | collective-permute-start | bytes 1216520 | tf_op jit(solution)/shard_map/ppermute | solution.py:361
  14.9 1.4 %collective-permute-done.15.refs_1_ = bf16[528,384]{1,0:T(8,128)(2,1)S(1)} collective-permute-done((bf16[528,384]{1,0:T(8,128)(2,1)S(1)}, bf16[528,384]{1,0:T(8,128)(2,1)S(1)}, u32[]{:S(2)}, u32[]{:S(2)}) %collective-permute-start.15) | collective-permute-done | bytes 405536 | tf_op jit(solution)/shard_map/ppermute | solution.py:361
  16.3 1.1 pad_maximum_fusion.3
  17.6 1.6 %collective-permute-start.16 = (bf16[528,384]{1,0:T(8,128)(2,1)}, bf16[528,384]{1,0:T(8,128)(2,1)S(1)}, u32[]{:S(2)}, u32[]{:S(2)}) collective-permute-start(bf16[528,384]{1,0:T(8,128)(2,1)} %collective-permute-done.14.refs_0_), channel_id=1, source_target_pairs={{0,4},{1,5},{2,0},{3,1},{4,8},{5,9},{6,2},{7,3},{8,12},{9,13},{10,... | collective-permute-start | bytes 1216520 | tf_op jit(solution)/shard_map/ppermute | solution.py:361
  19.1 0.4 collective-permute-start.17
  19.6 2.8 %sum_step.7 = (f32[4,512,256]{2,1,0:T(8,128)S(1)}, f32[16,384]{1,0:T(8,128)S(1)}) custom-call(s32[2]{0:T(128)S(1)} %get-tuple-element.103.index_ref, bf16[528,384]{1,0:T(8,128)(2,1)S(1)} %prepare.3.refs_0_, bf16[528,384]{1,0:T(8,128)(2,1)} %collective-permute-done.2.refs_1_, bf16[4,6144,256]{2,1,0:T(8,128)(2,1)S(1)} %copy-done), custom_call_target="tpu_custom_call" | custom-call | flops 201326592 | bytes 393216 | tf_op jit(solution)/shard_map/sum_step/pallas_call | solution.py:146
  22.4 2.4 %collective-permute-done.refs_2_ = bf16[528,384]{1,0:T(8,128)(2,1)S(1)} collective-permute-done((bf16[528,384]{1,0:T(8,128)(2,1)S(1)}, bf16[528,384]{1,0:T(8,128)(2,1)S(1)}, u32[]{:S(2)}, u32[]{:S(2)}) %collective-permute-start) | collective-permute-done | bytes 405536 | tf_op jit(solution)/shard_map/ppermute | solution.py:361
  24.8 2.0 %collective-permute-done.1.refs_3_ = bf16[528,384]{1,0:T(8,128)(2,1)S(1)} collective-permute-done((bf16[528,384]{1,0:T(8,128)(2,1)S(1)}, bf16[528,384]{1,0:T(8,128)(2,1)S(1)}, u32[]{:S(2)}, u32[]{:S(2)}) %collective-permute-start.1) | collective-permute-done | bytes 405536 | tf_op jit(solution)/shard_map/ppermute | solution.py:361
  26.9 0.5 collective-permute-start.5
  27.5 1.6 %collective-permute-start.3 = (bf16[528,384]{1,0:T(8,128)(2,1)S(1)}, bf16[528,384]{1,0:T(8,128)(2,1)S(1)}, u32[]{:S(2)}, u32[]{:S(2)}) collective-permute-start(bf16[528,384]{1,0:T(8,128)(2,1)S(1)} %collective-permute-done.refs_2_), channel_id=1, source_target_pairs={{0,4},{1,5},{2,0},{3,1},{4,8},{5,9},{6,2},{7,3},{8,12},{9,13},{10,... | collective-permute-start | bytes 1216520 | tf_op jit(solution)/shard_map/ppermute | solution.py:361
  29.1 4.0 %sum_step.11 = (f32[4,512,256]{2,1,0:T(8,128)S(1)}, f32[16,384]{1,0:T(8,128)S(1)}) custom-call(s32[4]{0:T(128)S(1)} %get-tuple-element.99.index_ref, bf16[528,384]{1,0:T(8,128)(2,1)} %collective-permute-done.14.refs_0_, bf16[528,384]{1,0:T(8,128)(2,1)S(1)} %collective-permute-done.15.refs_1_, ...), custom_call_target="tpu_custom_call", output_to_operand_aliasing={{0}: (5, {}), {1}: (6, {})} | custom-call | flops 402653184 | bytes 786432 | tf_op jit(solution)/shard_map/sum_step/pallas_call | solution.py:146
  33.5 1.9 %collective-permute-start.4 = (bf16[528,384]{1,0:T(8,128)(2,1)S(1)}, bf16[528,384]{1,0:T(8,128)(2,1)S(1)}, u32[]{:S(2)}, u32[]{:S(2)}) collective-permute-start(bf16[528,384]{1,0:T(8,128)(2,1)S(1)} %collective-permute-done.1.refs_3_), channel_id=1, source_target_pairs={{0,2},{1,3},{2,6},{3,7},{4,0},{5,1},{6,10},{7,11},{8,4},{9,5},{10,... | collective-permute-start | bytes 1216520 | tf_op jit(solution)/shard_map/ppermute | solution.py:361
  35.6 4.0 %sum_step.8 = (f32[4,512,256]{2,1,0:T(8,128)S(1)}, f32[16,384]{1,0:T(8,128)S(1)}) custom-call(s32[6]{0:T(128)S(1)} %slice_bitcast_fusion.4.index_ref, bf16[528,384]{1,0:T(8,128)(2,1)S(1)} %prepare.2.refs_0_, bf16[528,384]{1,0:T(8,128)(2,1)S(1)} %collective-permute-done.5.refs_1_, bf16[528,384]{1,0:T(8,128)(2,1)S(1)} %collective-permute-done.refs_2_, ...), custom_call_target="tpu_custom_call" | custom-call | flops 603979776 | bytes 1179648 | tf_op jit(solution)/shard_map/sum_step/pallas_call | solution.py:146
  39.5 2.4 %collective-permute-done.3.refs_0_ = bf16[528,384]{1,0:T(8,128)(2,1)S(1)} collective-permute-done((bf16[528,384]{1,0:T(8,128)(2,1)S(1)}, bf16[528,384]{1,0:T(8,128)(2,1)S(1)}, u32[]{:S(2)}, u32[]{:S(2)}) %collective-permute-start.3) | collective-permute-done | bytes 405536 | tf_op jit(solution)/shard_map/ppermute | solution.py:361
  41.9 2.5 %collective-permute-done.4.refs_1_ = bf16[528,384]{1,0:T(8,128)(2,1)S(1)} collective-permute-done((bf16[528,384]{1,0:T(8,128)(2,1)S(1)}, bf16[528,384]{1,0:T(8,128)(2,1)S(1)}, u32[]{:S(2)}, u32[]{:S(2)}) %collective-permute-start.4) | collective-permute-done | bytes 405536 | tf_op jit(solution)/shard_map/ppermute | solution.py:361
  44.6 1.7 %collective-permute-start.19 = (bf16[528,384]{1,0:T(8,128)(2,1)S(1)}, bf16[528,384]{1,0:T(8,128)(2,1)S(1)}, u32[]{:S(2)}, u32[]{:S(2)}) collective-permute-start(bf16[528,384]{1,0:T(8,128)(2,1)S(1)} %collective-permute-done.16.refs_0_), channel_id=1, source_target_pairs={{0,4},{1,5},{2,0},{3,1},{4,8},{5,9},{6,2},{7,3},{8,12},{9,13},{10,... | collective-permute-start | bytes 1216520 | tf_op jit(solution)/shard_map/ppermute | solution.py:361
  46.6 1.6 %collective-permute-start.7 = (bf16[528,384]{1,0:T(8,128)(2,1)S(1)}, bf16[528,384]{1,0:T(8,128)(2,1)S(1)}, u32[]{:S(2)}, u32[]{:S(2)}) collective-permute-start(bf16[528,384]{1,0:T(8,128)(2,1)S(1)} %collective-permute-done.3.refs_0_), channel_id=1, source_target_pairs={{0,4},{1,5},{2,0},{3,1},{4,8},{5,9},{6,2},{7,3},{8,12},{9,13},{10,... | collective-permute-start | bytes 1216520 | tf_op jit(solution)/shard_map/ppermute | solution.py:361
  48.7 2.9 %sum_step.12 = (f32[4,512,256]{2,1,0:T(8,128)S(1)}, f32[16,384]{1,0:T(8,128)S(1)}) custom-call(s32[4]{0:T(128)S(1)} %get-tuple-element.101.index_ref, bf16[528,384]{1,0:T(8,128)(2,1)S(1)} %collective-permute-done.16.refs_0_, bf16[528,384]{1,0:T(8,128)(2,1)S(1)} %collective-permute-done.17.refs_1_, ...), custom_call_target="tpu_custom_call", output_to_operand_aliasing={{0}: (5, {}), {1}: (6, {})} | custom-call | flops 402653184 | bytes 786432 | tf_op jit(solution)/shard_map/sum_step/pallas_call | solution.py:146
  51.6 5.2 %collective-permute-done.19.refs_0_ = bf16[528,384]{1,0:T(8,128)(2,1)S(1)} collective-permute-done((bf16[528,384]{1,0:T(8,128)(2,1)S(1)}, bf16[528,384]{1,0:T(8,128)(2,1)S(1)}, u32[]{:S(2)}, u32[]{:S(2)}) %collective-permute-start.19) | collective-permute-done | bytes 405536 | tf_op jit(solution)/shard_map/ppermute | solution.py:361
  56.8 1.7 %collective-permute-done.20.refs_1_ = bf16[528,384]{1,0:T(8,128)(2,1)S(1)} collective-permute-done((bf16[528,384]{1,0:T(8,128)(2,1)S(1)}, bf16[528,384]{1,0:T(8,128)(2,1)S(1)}, u32[]{:S(2)}, u32[]{:S(2)}) %collective-permute-start.20) | collective-permute-done | bytes 405536 | tf_op jit(solution)/shard_map/ppermute | solution.py:361
  58.7 3.0 %sum_step.9 = (f32[4,512,256]{2,1,0:T(8,128)S(1)}, f32[16,384]{1,0:T(8,128)S(1)}) custom-call(s32[4]{0:T(128)S(1)} %get-tuple-element.101.index_ref, bf16[528,384]{1,0:T(8,128)(2,1)S(1)} %collective-permute-done.3.refs_0_, bf16[528,384]{1,0:T(8,128)(2,1)S(1)} %collective-permute-done.4.refs_1_, ...), custom_call_target="tpu_custom_call", output_to_operand_aliasing={{0}: (5, {}), {1}: (6, {})} | custom-call | flops 402653184 | bytes 786432 | tf_op jit(solution)/shard_map/sum_step/pallas_call | solution.py:146
  61.6 3.4 %collective-permute-done.7.refs_0_ = bf16[528,384]{1,0:T(8,128)(2,1)S(1)} collective-permute-done((bf16[528,384]{1,0:T(8,128)(2,1)S(1)}, bf16[528,384]{1,0:T(8,128)(2,1)S(1)}, u32[]{:S(2)}, u32[]{:S(2)}) %collective-permute-start.7) | collective-permute-done | bytes 405536 | tf_op jit(solution)/shard_map/ppermute | solution.py:361
  65.0 1.4 %collective-permute-done.8.refs_1_ = bf16[528,384]{1,0:T(8,128)(2,1)S(1)} collective-permute-done((bf16[528,384]{1,0:T(8,128)(2,1)S(1)}, bf16[528,384]{1,0:T(8,128)(2,1)S(1)}, u32[]{:S(2)}, u32[]{:S(2)}) %collective-permute-start.8) | collective-permute-done | bytes 405536 | tf_op jit(solution)/shard_map/ppermute | solution.py:361
  67.0 1.7 %collective-permute-start.22 = (bf16[256,384]{1,0:T(8,128)(2,1)S(1)}, bf16[256,384]{1,0:T(8,128)(2,1)S(1)}, u32[]{:S(2)}, u32[]{:S(2)}) collective-permute-start(bf16[256,384]{1,0:T(8,128)(2,1)S(1)} %slice.72), channel_id=1, source_target_pairs={{0,4},{1,5},{2,0},{3,1},{4,8},{5,9},{6,2},{7,3},{8,12},{9,13},{10,... | collective-permute-start | bytes 589832 | tf_op jit(solution)/shard_map/ppermute | solution.py:361
  69.2 1.9 %collective-permute-start.10 = (bf16[256,384]{1,0:T(8,128)(2,1)S(1)}, bf16[256,384]{1,0:T(8,128)(2,1)S(1)}, u32[]{:S(2)}, u32[]{:S(2)}) collective-permute-start(bf16[256,384]{1,0:T(8,128)(2,1)S(1)} %slice.64), channel_id=1, source_target_pairs={{0,4},{1,5},{2,0},{3,1},{4,8},{5,9},{6,2},{7,3},{8,12},{9,13},{10,... | collective-permute-start | bytes 589832 | tf_op jit(solution)/shard_map/ppermute | solution.py:361
  71.1 2.9 %sum_step.13 = (f32[4,512,256]{2,1,0:T(8,128)S(1)}, f32[16,384]{1,0:T(8,128)S(1)}) custom-call(s32[4]{0:T(128)S(1)} %get-tuple-element.100.index_ref, bf16[528,384]{1,0:T(8,128)(2,1)S(1)} %collective-permute-done.19.refs_0_, bf16[528,384]{1,0:T(8,128)(2,1)S(1)} %collective-permute-done.20.refs_1_, ...), custom_call_target="tpu_custom_call", output_to_operand_aliasing={{0}: (5, {}), {1}: (6, {})} | custom-call | flops 402653184 | bytes 786432 | tf_op jit(solution)/shard_map/sum_step/pallas_call | solution.py:146
  74.1 0.8 collective-permute-done.22.refs_0_
  75.0 2.9 %sum_step.10 = (f32[4,512,256]{2,1,0:T(8,128)S(1)}, f32[16,384]{1,0:T(8,128)S(1)}) custom-call(s32[4]{0:T(128)S(1)} %get-tuple-element.100.index_ref, bf16[528,384]{1,0:T(8,128)(2,1)S(1)} %collective-permute-done.7.refs_0_, bf16[528,384]{1,0:T(8,128)(2,1)S(1)} %collective-permute-done.8.refs_1_, ...), custom_call_target="tpu_custom_call", output_to_operand_aliasing={{0}: (5, {}), {1}: (6, {})} | custom-call | flops 402653184 | bytes 786432 | tf_op jit(solution)/shard_map/sum_step/pallas_call | solution.py:146
  78.9 3.4 %attend.2 = (f32[4,128,128]{2,1,0:T(8,128)S(1)}, f32[4,128,128]{2,1,0:T(8,128)S(1)}, f32[4,128,128]{2,1,0:T(8,128)S(1)}) custom-call(s32[2]{0:T(128)S(1)} %get-tuple-element.102.index_ref, bf16[256,384]{1,0:T(8,128)(2,1)S(1)} %collective-permute-done.22.refs_0_, bf16[272,384]{1,0:T(8,128)(2,1)S(1)} %collective-permute-done.23.refs_1_, ...), custom_call_target="tpu_custom_call" | custom-call | flops 201326592 | bytes 393216 | tf_op jit(solution)/shard_map/attend/pallas_call | solution.py:255
  82.3 5.7 %attend.3 = (bf16[8,128,384]{2,1,0:T(8,128)(2,1)S(1)}, f32[8,128,384]{2,1,0:T(8,128)S(1)}) custom-call(s32[18]{0:T(128)S(1)} %slice_bitcast_fusion.6.index_ref, bf16[256,384]{1,0:T(8,128)(2,1)S(1)} %collective-permute-done.10.refs_0_, bf16[272,384]{1,0:T(8,128)(2,1)S(1)} %collective-permute-done.11.refs_1_, ...), custom_call_target="tpu_custom_call" | custom-call | flops 201326592 | bytes 393216 | tf_op jit(solution)/shard_map/attend/pallas_call | solution.py:255
  88.0 0.6 collective-permute-start.26
  88.6 1.9 %collective-permute-done.26.other_ref = bf16[8,128,384]{2,1,0:T(8,128)(2,1)S(1)} collective-permute-done((bf16[8,128,384]{2,1,0:T(8,128)(2,1)S(1)}, bf16[8,128,384]{2,1,0:T(8,128)(2,1)S(1)}, u32[]{:S(2)}, u32[]{:S(2)}) %collective-permute-start.26) | collective-permute-done | bytes 786464 | tf_op jit(solution)/shard_map/ppermute | solution.py:364
  90.7 1.3 %collective-permute-start.31 = (bf16[4,64,384]{2,1,0:T(8,128)(2,1)S(1)}, bf16[4,64,384]{2,1,0:T(8,128)(2,1)S(1)}, u32[]{:S(2)}, u32[]{:S(2)}) collective-permute-start(bf16[4,64,384]{2,1,0:T(8,128)(2,1)S(1)} %get-tuple-element.92), channel_id=1, source_target_pairs={{0,2},{1,3},{2,0},{3,1},{4,6},{5,7},{6,4},{7,5},{8,10},{9,11},{10,... | collective-permute-start | bytes 589832 | tf_op jit(solution)/shard_map/ppermute | solution.py:364
  92.0 0.8 collective-permute-start.27
  92.8 5.7 %collective-permute-done.31.other_ref = bf16[4,64,384]{2,1,0:T(8,128)(2,1)S(1)} collective-permute-done((bf16[4,64,384]{2,1,0:T(8,128)(2,1)S(1)}, bf16[4,64,384]{2,1,0:T(8,128)(2,1)S(1)}, u32[]{:S(2)}, u32[]{:S(2)}) %collective-permute-start.31) | collective-permute-done | bytes 196640 | tf_op jit(solution)/shard_map/ppermute | solution.py:364
  98.5 2.7 %collective-permute-start.32 = (bf16[64,384]{1,0:T(8,128)(2,1)S(1)}, bf16[64,384]{1,0:T(8,128)(2,1)S(1)}, u32[]{:S(2)}, u32[]{:S(2)}) collective-permute-start(bf16[64,384]{1,0:T(8,128)(2,1)S(1)} %get-tuple-element.94), channel_id=1, source_target_pairs={{0,8},{1,9},{2,10},{3,11},{4,12},{5,13},{6,14},{7,15},{8,0},{9,1},... | collective-permute-start | bytes 147464 | tf_op jit(solution)/shard_map/ppermute | solution.py:364
  101.2 1.3 %collective-permute-start.33 = (bf16[64,384]{1,0:T(8,128)(2,1)S(1)}, bf16[64,384]{1,0:T(8,128)(2,1)S(1)}, u32[]{:S(2)}, u32[]{:S(2)}) collective-permute-start(bf16[64,384]{1,0:T(8,128)(2,1)S(1)} %get-tuple-element.95), channel_id=1, source_target_pairs={{0,12},{1,13},{2,14},{3,15},{4,8},{5,9},{6,10},{7,11},{8,4},{9,5},... | collective-permute-start | bytes 147464 | tf_op jit(solution)/shard_map/ppermute | solution.py:364
  102.8 2.9 %collective-permute-start.28 = (bf16[64,384]{1,0:T(8,128)(2,1)S(1)}, bf16[64,384]{1,0:T(8,128)(2,1)S(1)}, u32[]{:S(2)}, u32[]{:S(2)}) collective-permute-start(bf16[64,384]{1,0:T(8,128)(2,1)S(1)} %get-tuple-element.89), channel_id=1, source_target_pairs={{0,8},{1,9},{2,10},{3,11},{4,12},{5,13},{6,14},{7,15},{8,0},{9,1},... | collective-permute-start | bytes 147464 | tf_op jit(solution)/shard_map/ppermute | solution.py:364
  105.7 1.3 %collective-permute-start.29 = (bf16[64,384]{1,0:T(8,128)(2,1)S(1)}, bf16[64,384]{1,0:T(8,128)(2,1)S(1)}, u32[]{:S(2)}, u32[]{:S(2)}) collective-permute-start(bf16[64,384]{1,0:T(8,128)(2,1)S(1)} %get-tuple-element.90), channel_id=1, source_target_pairs={{0,12},{1,13},{2,14},{3,15},{4,8},{5,9},{6,10},{7,11},{8,4},{9,5},... | collective-permute-start | bytes 147464 | tf_op jit(solution)/shard_map/ppermute | solution.py:364
  107.4 0.8 collective-permute-done.28.refs_1_
  108.2 3.5 %collective-permute-done.29.refs_2_ = bf16[64,384]{1,0:T(8,128)(2,1)S(1)} collective-permute-done((bf16[64,384]{1,0:T(8,128)(2,1)S(1)}, bf16[64,384]{1,0:T(8,128)(2,1)S(1)}, u32[]{:S(2)}, u32[]{:S(2)}) %collective-permute-start.29) | collective-permute-done | bytes 49184 | tf_op jit(solution)/shard_map/ppermute | solution.py:364
  111.7 0.7 finish.1
  (76 shorter events, 6.2 us)
Async XLA Ops:
  0.0 8.1 %copy-start.1 = (bf16[128,6144]{1,0:T(8,128)(2,1)S(1)}, bf16[128,6144]{1,0:T(8,128)(2,1)}, u32[]{:S(2)}) copy-start(bf16[128,6144]{1,0:T(8,128)(2,1)} %share_ref.1) | copy-start | bytes 4718596
  0.0 1.3 %copy-start.2 = (bf16[1024,384]{1,0:T(8,128)(2,1)S(1)}, bf16[1024,384]{1,0:T(8,128)(2,1)}, u32[]{:S(2)}) copy-start(bf16[1024,384]{1,0:T(8,128)(2,1)} %rows_ref.3) | copy-start | bytes 2359300
  1.3 0.7 copy-start.4
  2.0 6.1 %copy-start.6 = (f32[1,6144]{1,0:T(1,128)S(1)}, f32[1,6144]{1,0:T(1,128)}, u32[]{:S(2)}) copy-start(f32[1,6144]{1,0:T(1,128)} %param.11) | copy-start | bytes 73732
  2.4 12.5 %collective-permute-start.14 = (bf16[528,384]{1,0:T(8,128)(2,1)S(1)}, bf16[528,384]{1,0:T(8,128)(2,1)}, u32[]{:S(2)}, u32[]{:S(2)}) collective-permute-start(bf16[528,384]{1,0:T(8,128)(2,1)S(1)} %prepare.3.refs_0_), channel_id=1, source_target_pairs={{0,4},{1,5},{2,0},{3,1},{4,8},{5,9},{6,2},{7,3},{8,12},{9,13},{10,... | collective-permute-start | bytes 1216520 | tf_op jit(solution)/shard_map/ppermute | solution.py:361
  5.5 10.8 %collective-permute-start.15 = (bf16[528,384]{1,0:T(8,128)(2,1)S(1)}, bf16[528,384]{1,0:T(8,128)(2,1)S(1)}, u32[]{:S(2)}, u32[]{:S(2)}) collective-permute-start(bf16[528,384]{1,0:T(8,128)(2,1)S(1)} %prepare.3.refs_0_), channel_id=1, source_target_pairs={{0,2},{1,3},{2,6},{3,7},{4,0},{5,1},{6,10},{7,11},{8,4},{9,5},{10,... | collective-permute-start | bytes 1216520 | tf_op jit(solution)/shard_map/ppermute | solution.py:361
  5.5 13.6 %collective-permute-start.2 = (bf16[528,384]{1,0:T(8,128)(2,1)S(1)}, bf16[528,384]{1,0:T(8,128)(2,1)}, u32[]{:S(2)}, u32[]{:S(2)}) collective-permute-start(bf16[528,384]{1,0:T(8,128)(2,1)S(1)} %prepare.3.refs_0_), channel_id=1, source_target_pairs={{0,1},{1,0},{2,3},{3,2},{4,5},{5,4},{6,7},{7,6},{8,9},{9,8},{10,11... | collective-permute-start | bytes 1216520 | tf_op jit(solution)/shard_map/ppermute | solution.py:364
  5.5 6.6 %copy-start.3 = (bf16[1024,384]{1,0:T(8,128)(2,1)S(1)}, bf16[1024,384]{1,0:T(8,128)(2,1)}, u32[]{:S(2)}) copy-start(bf16[1024,384]{1,0:T(8,128)(2,1)} %rows_ref.3) | copy-start | bytes 2359300
  5.5 6.6 %copy-start.5 = (f32[6144]{0:T(1024)S(1)}, f32[6144]{0:T(1024)}, u32[]{:S(2)}) copy-start(f32[6144]{0:T(1024)} %param.9) | copy-start | bytes 73732
  8.1 11.5 %copy-start = (bf16[4,6144,256]{2,1,0:T(8,128)(2,1)S(1)}, bf16[4,6144,256]{2,1,0:T(8,128)(2,1)}, u32[]{:S(2)}) copy-start(bf16[4,6144,256]{2,1,0:T(8,128)(2,1)} %refs_3_.13) | copy-start | bytes 37748740
  12.5 12.3 %collective-permute-start = (bf16[528,384]{1,0:T(8,128)(2,1)S(1)}, bf16[528,384]{1,0:T(8,128)(2,1)S(1)}, u32[]{:S(2)}, u32[]{:S(2)}) collective-permute-start(bf16[528,384]{1,0:T(8,128)(2,1)S(1)} %prepare.2.refs_0_), channel_id=1, source_target_pairs={{0,4},{1,5},{2,0},{3,1},{4,8},{5,9},{6,2},{7,3},{8,12},{9,13},{10,... | collective-permute-start | bytes 1216520 | tf_op jit(solution)/shard_map/ppermute | solution.py:361
  14.6 12.2 %collective-permute-start.1 = (bf16[528,384]{1,0:T(8,128)(2,1)S(1)}, bf16[528,384]{1,0:T(8,128)(2,1)S(1)}, u32[]{:S(2)}, u32[]{:S(2)}) collective-permute-start(bf16[528,384]{1,0:T(8,128)(2,1)S(1)} %prepare.2.refs_0_), channel_id=1, source_target_pairs={{0,2},{1,3},{2,6},{3,7},{4,0},{5,1},{6,10},{7,11},{8,4},{9,5},{10,... | collective-permute-start | bytes 1216520 | tf_op jit(solution)/shard_map/ppermute | solution.py:361
  17.4 10.1 %collective-permute-start.18 = (bf16[1056,384]{1,0:T(8,128)(2,1)S(1)}, bf16[1056,384]{1,0:T(8,128)(2,1)S(1)}, u32[]{:S(2)}, u32[]{:S(2)}) collective-permute-start(bf16[1056,384]{1,0:T(8,128)(2,1)S(1)} %pad_maximum_fusion.3), channel_id=1, source_target_pairs={{0,1},{1,0},{2,3},{3,2},{4,5},{5,4},{6,7},{7,6},{8,9},{9,8},{10,11... | collective-permute-start | bytes 2433032 | tf_op jit(solution)/shard_map/ppermute | solution.py:364
  17.6 15.9 %collective-permute-start.16 = (bf16[528,384]{1,0:T(8,128)(2,1)}, bf16[528,384]{1,0:T(8,128)(2,1)S(1)}, u32[]{:S(2)}, u32[]{:S(2)}) collective-permute-start(bf16[528,384]{1,0:T(8,128)(2,1)} %collective-permute-done.14.refs_0_), channel_id=1, source_target_pairs={{0,4},{1,5},{2,0},{3,1},{4,8},{5,9},{6,2},{7,3},{8,12},{9,13},{10,... | collective-permute-start | bytes 1216520 | tf_op jit(solution)/shard_map/ppermute | solution.py:361
  19.1 16.2 %collective-permute-start.17 = (bf16[528,384]{1,0:T(8,128)(2,1)S(1)}, bf16[528,384]{1,0:T(8,128)(2,1)S(1)}, u32[]{:S(2)}, u32[]{:S(2)}) collective-permute-start(bf16[528,384]{1,0:T(8,128)(2,1)S(1)} %collective-permute-done.15.refs_1_), channel_id=1, source_target_pairs={{0,2},{1,3},{2,6},{3,7},{4,0},{5,1},{6,10},{7,11},{8,4},{9,5},{10,... | collective-permute-start | bytes 1216520 | tf_op jit(solution)/shard_map/ppermute | solution.py:361
  26.9 8.7 %collective-permute-start.6 = (bf16[1056,384]{1,0:T(8,128)(2,1)S(1)}, bf16[1056,384]{1,0:T(8,128)(2,1)S(1)}, u32[]{:S(2)}, u32[]{:S(2)}) collective-permute-start(bf16[1056,384]{1,0:T(8,128)(2,1)S(1)} %pad_maximum_fusion), channel_id=1, source_target_pairs={{0,1},{1,0},{2,3},{3,2},{4,5},{5,4},{6,7},{7,6},{8,9},{9,8},{10,11... | collective-permute-start | bytes 2433032 | tf_op jit(solution)/shard_map/ppermute | solution.py:364
  26.9 8.6 %collective-permute-start.5 = (bf16[528,384]{1,0:T(8,128)(2,1)S(1)}, bf16[528,384]{1,0:T(8,128)(2,1)S(1)}, u32[]{:S(2)}, u32[]{:S(2)}) collective-permute-start(bf16[528,384]{1,0:T(8,128)(2,1)S(1)} %prepare.2.refs_0_), channel_id=1, source_target_pairs={{0,1},{1,0},{2,3},{3,2},{4,5},{5,4},{6,7},{7,6},{8,9},{9,8},{10,11... | collective-permute-start | bytes 1216520 | tf_op jit(solution)/shard_map/ppermute | solution.py:364
  27.5 14.4 %collective-permute-start.3 = (bf16[528,384]{1,0:T(8,128)(2,1)S(1)}, bf16[528,384]{1,0:T(8,128)(2,1)S(1)}, u32[]{:S(2)}, u32[]{:S(2)}) collective-permute-start(bf16[528,384]{1,0:T(8,128)(2,1)S(1)} %collective-permute-done.refs_2_), channel_id=1, source_target_pairs={{0,4},{1,5},{2,0},{3,1},{4,8},{5,9},{6,2},{7,3},{8,12},{9,13},{10,... | collective-permute-start | bytes 1216520 | tf_op jit(solution)/shard_map/ppermute | solution.py:361
  33.5 10.9 %collective-permute-start.4 = (bf16[528,384]{1,0:T(8,128)(2,1)S(1)}, bf16[528,384]{1,0:T(8,128)(2,1)S(1)}, u32[]{:S(2)}, u32[]{:S(2)}) collective-permute-start(bf16[528,384]{1,0:T(8,128)(2,1)S(1)} %collective-permute-done.1.refs_3_), channel_id=1, source_target_pairs={{0,2},{1,3},{2,6},{3,7},{4,0},{5,1},{6,10},{7,11},{8,4},{9,5},{10,... | collective-permute-start | bytes 1216520 | tf_op jit(solution)/shard_map/ppermute | solution.py:361
  35.5 12.8 %collective-permute-start.21 = (bf16[1056,384]{1,0:T(8,128)(2,1)S(1)}, bf16[1056,384]{1,0:T(8,128)(2,1)S(1)}, u32[]{:S(2)}, u32[]{:S(2)}) collective-permute-start(bf16[1056,384]{1,0:T(8,128)(2,1)S(1)} %pad_maximum_fusion.4), channel_id=1, source_target_pairs={{0,1},{1,0},{2,3},{3,2},{4,5},{5,4},{6,7},{7,6},{8,9},{9,8},{10,11... | collective-permute-start | bytes 2433032 | tf_op jit(solution)/shard_map/ppermute | solution.py:364
  44.5 14.2 %collective-permute-start.9 = (bf16[1056,384]{1,0:T(8,128)(2,1)S(1)}, bf16[1056,384]{1,0:T(8,128)(2,1)S(1)}, u32[]{:S(2)}, u32[]{:S(2)}) collective-permute-start(bf16[1056,384]{1,0:T(8,128)(2,1)S(1)} %pad_maximum_fusion.1), channel_id=1, source_target_pairs={{0,1},{1,0},{2,3},{3,2},{4,5},{5,4},{6,7},{7,6},{8,9},{9,8},{10,11... | collective-permute-start | bytes 2433032 | tf_op jit(solution)/shard_map/ppermute | solution.py:364
  44.6 12.2 %collective-permute-start.19 = (bf16[528,384]{1,0:T(8,128)(2,1)S(1)}, bf16[528,384]{1,0:T(8,128)(2,1)S(1)}, u32[]{:S(2)}, u32[]{:S(2)}) collective-permute-start(bf16[528,384]{1,0:T(8,128)(2,1)S(1)} %collective-permute-done.16.refs_0_), channel_id=1, source_target_pairs={{0,4},{1,5},{2,0},{3,1},{4,8},{5,9},{6,2},{7,3},{8,12},{9,13},{10,... | collective-permute-start | bytes 1216520 | tf_op jit(solution)/shard_map/ppermute | solution.py:361
  46.3 12.2 %collective-permute-start.20 = (bf16[528,384]{1,0:T(8,128)(2,1)S(1)}, bf16[528,384]{1,0:T(8,128)(2,1)S(1)}, u32[]{:S(2)}, u32[]{:S(2)}) collective-permute-start(bf16[528,384]{1,0:T(8,128)(2,1)S(1)} %collective-permute-done.17.refs_1_), channel_id=1, source_target_pairs={{0,2},{1,3},{2,6},{3,7},{4,0},{5,1},{6,10},{7,11},{8,4},{9,5},{10,... | collective-permute-start | bytes 1216520 | tf_op jit(solution)/shard_map/ppermute | solution.py:361
  46.6 18.4 %collective-permute-start.7 = (bf16[528,384]{1,0:T(8,128)(2,1)S(1)}, bf16[528,384]{1,0:T(8,128)(2,1)S(1)}, u32[]{:S(2)}, u32[]{:S(2)}) collective-permute-start(bf16[528,384]{1,0:T(8,128)(2,1)S(1)} %collective-permute-done.3.refs_0_), channel_id=1, source_target_pairs={{0,4},{1,5},{2,0},{3,1},{4,8},{5,9},{6,2},{7,3},{8,12},{9,13},{10,... | collective-permute-start | bytes 1216520 | tf_op jit(solution)/shard_map/ppermute | solution.py:361
  48.3 18.1 %collective-permute-start.8 = (bf16[528,384]{1,0:T(8,128)(2,1)S(1)}, bf16[528,384]{1,0:T(8,128)(2,1)S(1)}, u32[]{:S(2)}, u32[]{:S(2)}) collective-permute-start(bf16[528,384]{1,0:T(8,128)(2,1)S(1)} %collective-permute-done.4.refs_1_), channel_id=1, source_target_pairs={{0,2},{1,3},{2,6},{3,7},{4,0},{5,1},{6,10},{7,11},{8,4},{9,5},{10,... | collective-permute-start | bytes 1216520 | tf_op jit(solution)/shard_map/ppermute | solution.py:361
  58.6 10.7 %collective-permute-start.24 = (bf16[1056,384]{1,0:T(8,128)(2,1)S(1)}, bf16[1056,384]{1,0:T(8,128)(2,1)S(1)}, u32[]{:S(2)}, u32[]{:S(2)}) collective-permute-start(bf16[1056,384]{1,0:T(8,128)(2,1)S(1)} %pad_maximum_fusion.5), channel_id=1, source_target_pairs={{0,1},{1,0},{2,3},{3,2},{4,5},{5,4},{6,7},{7,6},{8,9},{9,8},{10,11... | collective-permute-start | bytes 2433032 | tf_op jit(solution)/shard_map/ppermute | solution.py:364
  66.5 8.5 %collective-permute-start.12 = (bf16[1056,384]{1,0:T(8,128)(2,1)S(1)}, bf16[1056,384]{1,0:T(8,128)(2,1)S(1)}, u32[]{:S(2)}, u32[]{:S(2)}) collective-permute-start(bf16[1056,384]{1,0:T(8,128)(2,1)S(1)} %pad_maximum_fusion.2), channel_id=1, source_target_pairs={{0,1},{1,0},{2,3},{3,2},{4,5},{5,4},{6,7},{7,6},{8,9},{9,8},{10,11... | collective-permute-start | bytes 2433032 | tf_op jit(solution)/shard_map/ppermute | solution.py:364
  66.6 8.2 %collective-permute-start.23 = (bf16[272,384]{1,0:T(8,128)(2,1)S(1)}, bf16[272,384]{1,0:T(8,128)(2,1)S(1)}, u32[]{:S(2)}, u32[]{:S(2)}) collective-permute-start(bf16[272,384]{1,0:T(8,128)(2,1)S(1)} %slice.73), channel_id=1, source_target_pairs={{0,2},{1,3},{2,6},{3,7},{4,0},{5,1},{6,10},{7,11},{8,4},{9,5},{10,... | collective-permute-start | bytes 626696 | tf_op jit(solution)/shard_map/ppermute | solution.py:361
  67.0 7.8 %collective-permute-start.22 = (bf16[256,384]{1,0:T(8,128)(2,1)S(1)}, bf16[256,384]{1,0:T(8,128)(2,1)S(1)}, u32[]{:S(2)}, u32[]{:S(2)}) collective-permute-start(bf16[256,384]{1,0:T(8,128)(2,1)S(1)} %slice.72), channel_id=1, source_target_pairs={{0,4},{1,5},{2,0},{3,1},{4,8},{5,9},{6,2},{7,3},{8,12},{9,13},{10,... | collective-permute-start | bytes 589832 | tf_op jit(solution)/shard_map/ppermute | solution.py:361
  68.8 9.9 %collective-permute-start.11 = (bf16[272,384]{1,0:T(8,128)(2,1)S(1)}, bf16[272,384]{1,0:T(8,128)(2,1)S(1)}, u32[]{:S(2)}, u32[]{:S(2)}) collective-permute-start(bf16[272,384]{1,0:T(8,128)(2,1)S(1)} %slice.65), channel_id=1, source_target_pairs={{0,2},{1,3},{2,6},{3,7},{4,0},{5,1},{6,10},{7,11},{8,4},{9,5},{10,... | collective-permute-start | bytes 626696 | tf_op jit(solution)/shard_map/ppermute | solution.py:361
  69.2 9.1 %collective-permute-start.10 = (bf16[256,384]{1,0:T(8,128)(2,1)S(1)}, bf16[256,384]{1,0:T(8,128)(2,1)S(1)}, u32[]{:S(2)}, u32[]{:S(2)}) collective-permute-start(bf16[256,384]{1,0:T(8,128)(2,1)S(1)} %slice.64), channel_id=1, source_target_pairs={{0,4},{1,5},{2,0},{3,1},{4,8},{5,9},{6,2},{7,3},{8,12},{9,13},{10,... | collective-permute-start | bytes 589832 | tf_op jit(solution)/shard_map/ppermute | solution.py:361
  74.9 4.0 %collective-permute-start.25 = (bf16[528,384]{1,0:T(8,128)(2,1)S(1)}, bf16[528,384]{1,0:T(8,128)(2,1)S(1)}, u32[]{:S(2)}, u32[]{:S(2)}) collective-permute-start(bf16[528,384]{1,0:T(8,128)(2,1)S(1)} %pad_maximum_fusion.7), channel_id=1, source_target_pairs={{0,1},{1,0},{2,3},{3,2},{4,5},{5,4},{6,7},{7,6},{8,9},{9,8},{10,11... | collective-permute-start | bytes 1216520 | tf_op jit(solution)/shard_map/ppermute | solution.py:364
  78.7 3.6 %collective-permute-start.13 = (bf16[528,384]{1,0:T(8,128)(2,1)S(1)}, bf16[528,384]{1,0:T(8,128)(2,1)S(1)}, u32[]{:S(2)}, u32[]{:S(2)}) collective-permute-start(bf16[528,384]{1,0:T(8,128)(2,1)S(1)} %pad_maximum_fusion.6), channel_id=1, source_target_pairs={{0,1},{1,0},{2,3},{3,2},{4,5},{5,4},{6,7},{7,6},{8,9},{9,8},{10,11... | collective-permute-start | bytes 1216520 | tf_op jit(solution)/shard_map/ppermute | solution.py:364
  78.9 3.4 %slice-start = ((s8[6291456]{0:T(1024)(128)(4,1)}), s8[4194304]{0:T(1024)(128)(4,1)S(1)}, s32[]{:S(2)}) async-start(s8[6291456]{0:T(1024)(128)(4,1)} %bitcast.31), calls=%async_computation | async-start | bytes 8388608
  78.9 3.4 %slice-start.1 = ((s8[6291456]{0:T(1024)(128)(4,1)}), s8[2097152]{0:T(1024)(128)(4,1)S(1)}, s32[]{:S(2)}) async-start(s8[6291456]{0:T(1024)(128)(4,1)} %bitcast.31), calls=%async_computation.1 | async-start | bytes 4194304
  88.0 2.5 %collective-permute-start.26 = (bf16[8,128,384]{2,1,0:T(8,128)(2,1)S(1)}, bf16[8,128,384]{2,1,0:T(8,128)(2,1)S(1)}, u32[]{:S(2)}, u32[]{:S(2)}) collective-permute-start(bf16[8,128,384]{2,1,0:T(8,128)(2,1)S(1)} %get-tuple-element.85), channel_id=1, source_target_pairs={{0,1},{1,0},{2,3},{3,2},{4,5},{5,4},{6,7},{7,6},{8,9},{9,8},{10,11... | collective-permute-start | bytes 2359304 | tf_op jit(solution)/shard_map/ppermute | solution.py:364
  90.7 7.8 %collective-permute-start.31 = (bf16[4,64,384]{2,1,0:T(8,128)(2,1)S(1)}, bf16[4,64,384]{2,1,0:T(8,128)(2,1)S(1)}, u32[]{:S(2)}, u32[]{:S(2)}) collective-permute-start(bf16[4,64,384]{2,1,0:T(8,128)(2,1)S(1)} %get-tuple-element.92), channel_id=1, source_target_pairs={{0,2},{1,3},{2,0},{3,1},{4,6},{5,7},{6,4},{7,5},{8,10},{9,11},{10,... | collective-permute-start | bytes 589832 | tf_op jit(solution)/shard_map/ppermute | solution.py:364
  92.0 10.7 %collective-permute-start.27 = (bf16[4,64,384]{2,1,0:T(8,128)(2,1)S(1)}, bf16[4,64,384]{2,1,0:T(8,128)(2,1)S(1)}, u32[]{:S(2)}, u32[]{:S(2)}) collective-permute-start(bf16[4,64,384]{2,1,0:T(8,128)(2,1)S(1)} %get-tuple-element.87), channel_id=1, source_target_pairs={{0,2},{1,3},{2,0},{3,1},{4,6},{5,7},{6,4},{7,5},{8,10},{9,11},{10,... | collective-permute-start | bytes 589832 | tf_op jit(solution)/shard_map/ppermute | solution.py:364
  98.5 8.5 %collective-permute-start.32 = (bf16[64,384]{1,0:T(8,128)(2,1)S(1)}, bf16[64,384]{1,0:T(8,128)(2,1)S(1)}, u32[]{:S(2)}, u32[]{:S(2)}) collective-permute-start(bf16[64,384]{1,0:T(8,128)(2,1)S(1)} %get-tuple-element.94), channel_id=1, source_target_pairs={{0,8},{1,9},{2,10},{3,11},{4,12},{5,13},{6,14},{7,15},{8,0},{9,1},... | collective-permute-start | bytes 147464 | tf_op jit(solution)/shard_map/ppermute | solution.py:364
  101.2 6.2 %collective-permute-start.33 = (bf16[64,384]{1,0:T(8,128)(2,1)S(1)}, bf16[64,384]{1,0:T(8,128)(2,1)S(1)}, u32[]{:S(2)}, u32[]{:S(2)}) collective-permute-start(bf16[64,384]{1,0:T(8,128)(2,1)S(1)} %get-tuple-element.95), channel_id=1, source_target_pairs={{0,12},{1,13},{2,14},{3,15},{4,8},{5,9},{6,10},{7,11},{8,4},{9,5},... | collective-permute-start | bytes 147464 | tf_op jit(solution)/shard_map/ppermute | solution.py:364
  102.5 4.9 %collective-permute-start.34 = (bf16[64,384]{1,0:T(8,128)(2,1)S(1)}, bf16[64,384]{1,0:T(8,128)(2,1)S(1)}, u32[]{:S(2)}, u32[]{:S(2)}) collective-permute-start(bf16[64,384]{1,0:T(8,128)(2,1)S(1)} %get-tuple-element.96), channel_id=1, source_target_pairs={{0,4},{1,5},{2,6},{3,7},{4,0},{5,1},{6,2},{7,3},{8,12},{9,13},{10,... | collective-permute-start | bytes 147464 | tf_op jit(solution)/shard_map/ppermute | solution.py:364
  102.8 5.4 %collective-permute-start.28 = (bf16[64,384]{1,0:T(8,128)(2,1)S(1)}, bf16[64,384]{1,0:T(8,128)(2,1)S(1)}, u32[]{:S(2)}, u32[]{:S(2)}) collective-permute-start(bf16[64,384]{1,0:T(8,128)(2,1)S(1)} %get-tuple-element.89), channel_id=1, source_target_pairs={{0,8},{1,9},{2,10},{3,11},{4,12},{5,13},{6,14},{7,15},{8,0},{9,1},... | collective-permute-start | bytes 147464 | tf_op jit(solution)/shard_map/ppermute | solution.py:364
  105.7 6.0 %collective-permute-start.29 = (bf16[64,384]{1,0:T(8,128)(2,1)S(1)}, bf16[64,384]{1,0:T(8,128)(2,1)S(1)}, u32[]{:S(2)}, u32[]{:S(2)}) collective-permute-start(bf16[64,384]{1,0:T(8,128)(2,1)S(1)} %get-tuple-element.90), channel_id=1, source_target_pairs={{0,12},{1,13},{2,14},{3,15},{4,8},{5,9},{6,10},{7,11},{8,4},{9,5},... | collective-permute-start | bytes 147464 | tf_op jit(solution)/shard_map/ppermute | solution.py:364
  107.0 4.6 %collective-permute-start.30 = (bf16[64,384]{1,0:T(8,128)(2,1)S(1)}, bf16[64,384]{1,0:T(8,128)(2,1)S(1)}, u32[]{:S(2)}, u32[]{:S(2)}) collective-permute-start(bf16[64,384]{1,0:T(8,128)(2,1)S(1)} %get-tuple-element.91), channel_id=1, source_target_pairs={{0,4},{1,5},{2,6},{3,7},{4,0},{5,1},{6,2},{7,3},{8,12},{9,13},{10,... | collective-permute-start | bytes 147464 | tf_op jit(solution)/shard_map/ppermute | solution.py:364

commit v4 on v3

--- a/solution.py
+++ b/solution.py
@@ -218,7 +218,7 @@
         copy.wait()
     count, _, cols = mine_ref.shape
     for part, target in enumerate((theirs_ref, mine_ref)):
-        @pl.loop(0, count, unroll=min(count, 4))
+        @pl.loop(0, count, unroll=min(count, 8))
         def _(step):
             block = index_ref[len(slots) + part * count + step]
             columns = pl.ds(pl.multiple_of(block * cols, cols), cols)

time: 113 us -> 112 us (level)
  transfers between devices with their start and end apart: 35 -> 35, of which waited for: 19 -> 19; matrix products, arithmetic and copies ran while one was open for 7% -> 8% of each run, Pallas kernels for 23% -> 24%
where the time goes in v4:
time: 112 us
  waiting for transfers between devices  36.8 us (33%)
  Pallas kernels  33 us (29%)
  starting transfers between devices  31.4 us (28%)
  matrix products  3.97 us (4%)
  other arithmetic  3.45 us (3%)
  local copies, waits for them, and re-layouts  3.02 us (3%)
    ppermute x16, waiting for transfers between devices, hop(): return lax.ppermute(values, 'section', pairs)  24.6 us
    pallas_call x7, Pallas kernels, sum_step(): pl.pallas_call(functools.partial(sum_kernel, placed, len(arrays), carried...  22.5 us
    ppermute x16, starting transfers between devices, hop(): return lax.ppermute(values, 'section', pairs)  19.2 us
    ppermute x19, waiting for transfers between devices, exchange(): lax.ppermute(values, 'section', [(s, s ^ bits) for s in range(sections)])  12.3 us
    ppermute x19, starting transfers between devices, exchange(): lax.ppermute(values, 'section', [(s, s ^ bits) for s in range(sections)])  12.2 us
    pallas_call x2, Pallas kernels, attend(): pl.pallas_call(functools.partial(attend_kernel, placed, len(arrays), merg...  8.73 us
    dot_general x1, matrix products, ring_body(): jnp.einsum('td,hdk->htk', normed, w_query, preferred_element_type=jnp.flo...  3.97 us
  transfers between devices with their start and end apart: 35, of which 19 were waited for; matrix products, arithmetic and copies ran while one was open for 8% of the time, Pallas kernels for 24%

profile of v4, /device:TPU:0, one launch (start us, length us, event | category | flops | bytes accessed | tf_op | source)
XLA Modules:
  0.0 112.0 jit_solution(4538966192281901259)
XLA Ops:
  0.0 1.3 %copy-done.2 = bf16[1024,384]{1,0:T(8,128)(2,1)S(1)} copy-done((bf16[1024,384]{1,0:T(8,128)(2,1)S(1)}, bf16[1024,384]{1,0:T(8,128)(2,1)}, u32[]{:S(2)}) %copy-start.2) | copy-done | bytes 786456
  1.3 0.7 copy-done.4
  2.4 3.1 %collective-permute-start.14 = (bf16[528,384]{1,0:T(8,128)(2,1)S(1)}, bf16[528,384]{1,0:T(8,128)(2,1)}, u32[]{:S(2)}, u32[]{:S(2)}) collective-permute-start(bf16[528,384]{1,0:T(8,128)(2,1)S(1)} %prepare.3.refs_0_), channel_id=1, source_target_pairs={{0,4},{1,5},{2,0},{3,1},{4,8},{5,9},{6,2},{7,3},{8,12},{9,13},{10,... | collective-permute-start | bytes 1216520 | tf_op jit(solution)/shard_map/ppermute | solution.py:361
  5.5 1.9 %fusion = f32[128]{0:T(128)S(1)} fusion(bf16[128,6144]{1,0:T(8,128)(2,1)} %share_ref.1), kind=kLoop, calls=%fused_computation.2 | loop fusion | flops 2359168 | bytes 1573376 | tf_op jit(solution)/shard_map/reduce_sum | solution.py:21
  7.4 0.7 fusion.17
  8.1 4.0 %fusion.14.refs_0_.refs_6_ = bf16[4,128,128]{2,1,0:T(8,128)(2,1)S(1)} fusion(bf16[4,6144,128]{2,1,0:T(8,128)(2,1)} %param.12, bf16[128,6144]{1,0:T(8,128)(2,1)S(1)} %copy-done.1, f32[6144]{0:T(1024)S(1)} %bitcast.35, f32[128]{0:T(128)S(1)} %add_rsqrt_fusion), kind=kOutput, calls=%fused_computation.11 | convolution fusion | flops 808583168 | bytes 8020480 | tf_op jit(solution)/shard_map/td,hdk->htk/dot_general | solution.py:387
  12.5 2.1 %collective-permute-start = (bf16[528,384]{1,0:T(8,128)(2,1)S(1)}, bf16[528,384]{1,0:T(8,128)(2,1)S(1)}, u32[]{:S(2)}, u32[]{:S(2)}) collective-permute-start(bf16[528,384]{1,0:T(8,128)(2,1)S(1)} %prepare.2.refs_0_), channel_id=1, source_target_pairs={{0,4},{1,5},{2,0},{3,1},{4,8},{5,9},{6,2},{7,3},{8,12},{9,13},{10,... | collective-permute-start | bytes 1216520 | tf_op jit(solution)/shard_map/ppermute | solution.py:361
  14.9 1.4 %collective-permute-done.15.refs_1_ = bf16[528,384]{1,0:T(8,128)(2,1)S(1)} collective-permute-done((bf16[528,384]{1,0:T(8,128)(2,1)S(1)}, bf16[528,384]{1,0:T(8,128)(2,1)S(1)}, u32[]{:S(2)}, u32[]{:S(2)}) %collective-permute-start.15) | collective-permute-done | bytes 405536 | tf_op jit(solution)/shard_map/ppermute | solution.py:361
  16.3 1.1 pad_maximum_fusion.3
  17.6 1.6 %collective-permute-start.16 = (bf16[528,384]{1,0:T(8,128)(2,1)}, bf16[528,384]{1,0:T(8,128)(2,1)S(1)}, u32[]{:S(2)}, u32[]{:S(2)}) collective-permute-start(bf16[528,384]{1,0:T(8,128)(2,1)} %collective-permute-done.14.refs_0_), channel_id=1, source_target_pairs={{0,4},{1,5},{2,0},{3,1},{4,8},{5,9},{6,2},{7,3},{8,12},{9,13},{10,... | collective-permute-start | bytes 1216520 | tf_op jit(solution)/shard_map/ppermute | solution.py:361
  19.1 0.4 collective-permute-start.17
  19.6 2.8 %sum_step.7 = (f32[4,512,256]{2,1,0:T(8,128)S(1)}, f32[16,384]{1,0:T(8,128)S(1)}) custom-call(s32[2]{0:T(128)S(1)} %get-tuple-element.103.index_ref, bf16[528,384]{1,0:T(8,128)(2,1)S(1)} %prepare.3.refs_0_, bf16[528,384]{1,0:T(8,128)(2,1)} %collective-permute-done.2.refs_1_, bf16[4,6144,256]{2,1,0:T(8,128)(2,1)S(1)} %copy-done), custom_call_target="tpu_custom_call" | custom-call | flops 201326592 | bytes 393216 | tf_op jit(solution)/shard_map/sum_step/pallas_call | solution.py:146
  22.4 2.4 %collective-permute-done.refs_2_ = bf16[528,384]{1,0:T(8,128)(2,1)S(1)} collective-permute-done((bf16[528,384]{1,0:T(8,128)(2,1)S(1)}, bf16[528,384]{1,0:T(8,128)(2,1)S(1)}, u32[]{:S(2)}, u32[]{:S(2)}) %collective-permute-start) | collective-permute-done | bytes 405536 | tf_op jit(solution)/shard_map/ppermute | solution.py:361
  24.8 2.0 %collective-permute-done.1.refs_3_ = bf16[528,384]{1,0:T(8,128)(2,1)S(1)} collective-permute-done((bf16[528,384]{1,0:T(8,128)(2,1)S(1)}, bf16[528,384]{1,0:T(8,128)(2,1)S(1)}, u32[]{:S(2)}, u32[]{:S(2)}) %collective-permute-start.1) | collective-permute-done | bytes 405536 | tf_op jit(solution)/shard_map/ppermute | solution.py:361
  26.9 0.5 collective-permute-start.5
  27.5 1.6 %collective-permute-start.3 = (bf16[528,384]{1,0:T(8,128)(2,1)S(1)}, bf16[528,384]{1,0:T(8,128)(2,1)S(1)}, u32[]{:S(2)}, u32[]{:S(2)}) collective-permute-start(bf16[528,384]{1,0:T(8,128)(2,1)S(1)} %collective-permute-done.refs_2_), channel_id=1, source_target_pairs={{0,4},{1,5},{2,0},{3,1},{4,8},{5,9},{6,2},{7,3},{8,12},{9,13},{10,... | collective-permute-start | bytes 1216520 | tf_op jit(solution)/shard_map/ppermute | solution.py:361
  29.1 4.0 %sum_step.11 = (f32[4,512,256]{2,1,0:T(8,128)S(1)}, f32[16,384]{1,0:T(8,128)S(1)}) custom-call(s32[4]{0:T(128)S(1)} %get-tuple-element.99.index_ref, bf16[528,384]{1,0:T(8,128)(2,1)} %collective-permute-done.14.refs_0_, bf16[528,384]{1,0:T(8,128)(2,1)S(1)} %collective-permute-done.15.refs_1_, ...), custom_call_target="tpu_custom_call", output_to_operand_aliasing={{0}: (5, {}), {1}: (6, {})} | custom-call | flops 402653184 | bytes 786432 | tf_op jit(solution)/shard_map/sum_step/pallas_call | solution.py:146
  33.5 1.9 %collective-permute-start.4 = (bf16[528,384]{1,0:T(8,128)(2,1)S(1)}, bf16[528,384]{1,0:T(8,128)(2,1)S(1)}, u32[]{:S(2)}, u32[]{:S(2)}) collective-permute-start(bf16[528,384]{1,0:T(8,128)(2,1)S(1)} %collective-permute-done.1.refs_3_), channel_id=1, source_target_pairs={{0,2},{1,3},{2,6},{3,7},{4,0},{5,1},{6,10},{7,11},{8,4},{9,5},{10,... | collective-permute-start | bytes 1216520 | tf_op jit(solution)/shard_map/ppermute | solution.py:361
  35.6 4.0 %sum_step.8 = (f32[4,512,256]{2,1,0:T(8,128)S(1)}, f32[16,384]{1,0:T(8,128)S(1)}) custom-call(s32[6]{0:T(128)S(1)} %slice_bitcast_fusion.4.index_ref, bf16[528,384]{1,0:T(8,128)(2,1)S(1)} %prepare.2.refs_0_, bf16[528,384]{1,0:T(8,128)(2,1)S(1)} %collective-permute-done.5.refs_1_, bf16[528,384]{1,0:T(8,128)(2,1)S(1)} %collective-permute-done.refs_2_, ...), custom_call_target="tpu_custom_call" | custom-call | flops 603979776 | bytes 1179648 | tf_op jit(solution)/shard_map/sum_step/pallas_call | solution.py:146
  39.5 2.4 %collective-permute-done.3.refs_0_ = bf16[528,384]{1,0:T(8,128)(2,1)S(1)} collective-permute-done((bf16[528,384]{1,0:T(8,128)(2,1)S(1)}, bf16[528,384]{1,0:T(8,128)(2,1)S(1)}, u32[]{:S(2)}, u32[]{:S(2)}) %collective-permute-start.3) | collective-permute-done | bytes 405536 | tf_op jit(solution)/shard_map/ppermute | solution.py:361
  41.9 2.5 %collective-permute-done.4.refs_1_ = bf16[528,384]{1,0:T(8,128)(2,1)S(1)} collective-permute-done((bf16[528,384]{1,0:T(8,128)(2,1)S(1)}, bf16[528,384]{1,0:T(8,128)(2,1)S(1)}, u32[]{:S(2)}, u32[]{:S(2)}) %collective-permute-start.4) | collective-permute-done | bytes 405536 | tf_op jit(solution)/shard_map/ppermute | solution.py:361
  44.6 1.7 %collective-permute-start.19 = (bf16[528,384]{1,0:T(8,128)(2,1)S(1)}, bf16[528,384]{1,0:T(8,128)(2,1)S(1)}, u32[]{:S(2)}, u32[]{:S(2)}) collective-permute-start(bf16[528,384]{1,0:T(8,128)(2,1)S(1)} %collective-permute-done.16.refs_0_), channel_id=1, source_target_pairs={{0,4},{1,5},{2,0},{3,1},{4,8},{5,9},{6,2},{7,3},{8,12},{9,13},{10,... | collective-permute-start | bytes 1216520 | tf_op jit(solution)/shard_map/ppermute | solution.py:361
  46.6 1.6 %collective-permute-start.7 = (bf16[528,384]{1,0:T(8,128)(2,1)S(1)}, bf16[528,384]{1,0:T(8,128)(2,1)S(1)}, u32[]{:S(2)}, u32[]{:S(2)}) collective-permute-start(bf16[528,384]{1,0:T(8,128)(2,1)S(1)} %collective-permute-done.3.refs_0_), channel_id=1, source_target_pairs={{0,4},{1,5},{2,0},{3,1},{4,8},{5,9},{6,2},{7,3},{8,12},{9,13},{10,... | collective-permute-start | bytes 1216520 | tf_op jit(solution)/shard_map/ppermute | solution.py:361
  48.7 2.9 %sum_step.12 = (f32[4,512,256]{2,1,0:T(8,128)S(1)}, f32[16,384]{1,0:T(8,128)S(1)}) custom-call(s32[4]{0:T(128)S(1)} %get-tuple-element.101.index_ref, bf16[528,384]{1,0:T(8,128)(2,1)S(1)} %collective-permute-done.16.refs_0_, bf16[528,384]{1,0:T(8,128)(2,1)S(1)} %collective-permute-done.17.refs_1_, ...), custom_call_target="tpu_custom_call", output_to_operand_aliasing={{0}: (5, {}), {1}: (6, {})} | custom-call | flops 402653184 | bytes 786432 | tf_op jit(solution)/shard_map/sum_step/pallas_call | solution.py:146
  51.6 5.2 %collective-permute-done.19.refs_0_ = bf16[528,384]{1,0:T(8,128)(2,1)S(1)} collective-permute-done((bf16[528,384]{1,0:T(8,128)(2,1)S(1)}, bf16[528,384]{1,0:T(8,128)(2,1)S(1)}, u32[]{:S(2)}, u32[]{:S(2)}) %collective-permute-start.19) | collective-permute-done | bytes 405536 | tf_op jit(solution)/shard_map/ppermute | solution.py:361
  56.8 1.7 %collective-permute-done.20.refs_1_ = bf16[528,384]{1,0:T(8,128)(2,1)S(1)} collective-permute-done((bf16[528,384]{1,0:T(8,128)(2,1)S(1)}, bf16[528,384]{1,0:T(8,128)(2,1)S(1)}, u32[]{:S(2)}, u32[]{:S(2)}) %collective-permute-start.20) | collective-permute-done | bytes 405536 | tf_op jit(solution)/shard_map/ppermute | solution.py:361
  58.7 3.0 %sum_step.9 = (f32[4,512,256]{2,1,0:T(8,128)S(1)}, f32[16,384]{1,0:T(8,128)S(1)}) custom-call(s32[4]{0:T(128)S(1)} %get-tuple-element.101.index_ref, bf16[528,384]{1,0:T(8,128)(2,1)S(1)} %collective-permute-done.3.refs_0_, bf16[528,384]{1,0:T(8,128)(2,1)S(1)} %collective-permute-done.4.refs_1_, ...), custom_call_target="tpu_custom_call", output_to_operand_aliasing={{0}: (5, {}), {1}: (6, {})} | custom-call | flops 402653184 | bytes 786432 | tf_op jit(solution)/shard_map/sum_step/pallas_call | solution.py:146
  61.6 3.4 %collective-permute-done.7.refs_0_ = bf16[528,384]{1,0:T(8,128)(2,1)S(1)} collective-permute-done((bf16[528,384]{1,0:T(8,128)(2,1)S(1)}, bf16[528,384]{1,0:T(8,128)(2,1)S(1)}, u32[]{:S(2)}, u32[]{:S(2)}) %collective-permute-start.7) | collective-permute-done | bytes 405536 | tf_op jit(solution)/shard_map/ppermute | solution.py:361
  65.0 1.4 %collective-permute-done.8.refs_1_ = bf16[528,384]{1,0:T(8,128)(2,1)S(1)} collective-permute-done((bf16[528,384]{1,0:T(8,128)(2,1)S(1)}, bf16[528,384]{1,0:T(8,128)(2,1)S(1)}, u32[]{:S(2)}, u32[]{:S(2)}) %collective-permute-start.8) | collective-permute-done | bytes 405536 | tf_op jit(solution)/shard_map/ppermute | solution.py:361
  67.0 1.7 %collective-permute-start.22 = (bf16[256,384]{1,0:T(8,128)(2,1)S(1)}, bf16[256,384]{1,0:T(8,128)(2,1)S(1)}, u32[]{:S(2)}, u32[]{:S(2)}) collective-permute-start(bf16[256,384]{1,0:T(8,128)(2,1)S(1)} %slice.72), channel_id=1, source_target_pairs={{0,4},{1,5},{2,0},{3,1},{4,8},{5,9},{6,2},{7,3},{8,12},{9,13},{10,... | collective-permute-start | bytes 589832 | tf_op jit(solution)/shard_map/ppermute | solution.py:361
  69.2 1.9 %collective-permute-start.10 = (bf16[256,384]{1,0:T(8,128)(2,1)S(1)}, bf16[256,384]{1,0:T(8,128)(2,1)S(1)}, u32[]{:S(2)}, u32[]{:S(2)}) collective-permute-start(bf16[256,384]{1,0:T(8,128)(2,1)S(1)} %slice.64), channel_id=1, source_target_pairs={{0,4},{1,5},{2,0},{3,1},{4,8},{5,9},{6,2},{7,3},{8,12},{9,13},{10,... | collective-permute-start | bytes 589832 | tf_op jit(solution)/shard_map/ppermute | solution.py:361
  71.1 2.9 %sum_step.13 = (f32[4,512,256]{2,1,0:T(8,128)S(1)}, f32[16,384]{1,0:T(8,128)S(1)}) custom-call(s32[4]{0:T(128)S(1)} %get-tuple-element.100.index_ref, bf16[528,384]{1,0:T(8,128)(2,1)S(1)} %collective-permute-done.19.refs_0_, bf16[528,384]{1,0:T(8,128)(2,1)S(1)} %collective-permute-done.20.refs_1_, ...), custom_call_target="tpu_custom_call", output_to_operand_aliasing={{0}: (5, {}), {1}: (6, {})} | custom-call | flops 402653184 | bytes 786432 | tf_op jit(solution)/shard_map/sum_step/pallas_call | solution.py:146
  74.1 0.8 collective-permute-done.22.refs_0_
  75.0 2.9 %sum_step.10 = (f32[4,512,256]{2,1,0:T(8,128)S(1)}, f32[16,384]{1,0:T(8,128)S(1)}) custom-call(s32[4]{0:T(128)S(1)} %get-tuple-element.100.index_ref, bf16[528,384]{1,0:T(8,128)(2,1)S(1)} %collective-permute-done.7.refs_0_, bf16[528,384]{1,0:T(8,128)(2,1)S(1)} %collective-permute-done.8.refs_1_, ...), custom_call_target="tpu_custom_call", output_to_operand_aliasing={{0}: (5, {}), {1}: (6, {})} | custom-call | flops 402653184 | bytes 786432 | tf_op jit(solution)/shard_map/sum_step/pallas_call | solution.py:146
  78.9 3.4 %attend.2 = (f32[4,128,128]{2,1,0:T(8,128)S(1)}, f32[4,128,128]{2,1,0:T(8,128)S(1)}, f32[4,128,128]{2,1,0:T(8,128)S(1)}) custom-call(s32[2]{0:T(128)S(1)} %get-tuple-element.102.index_ref, bf16[256,384]{1,0:T(8,128)(2,1)S(1)} %collective-permute-done.22.refs_0_, bf16[272,384]{1,0:T(8,128)(2,1)S(1)} %collective-permute-done.23.refs_1_, ...), custom_call_target="tpu_custom_call" | custom-call | flops 201326592 | bytes 393216 | tf_op jit(solution)/shard_map/attend/pallas_call | solution.py:255
  82.3 5.3 %attend.3 = (bf16[8,128,384]{2,1,0:T(8,128)(2,1)S(1)}, f32[8,128,384]{2,1,0:T(8,128)S(1)}) custom-call(s32[18]{0:T(128)S(1)} %slice_bitcast_fusion.6.index_ref, bf16[256,384]{1,0:T(8,128)(2,1)S(1)} %collective-permute-done.10.refs_0_, bf16[272,384]{1,0:T(8,128)(2,1)S(1)} %collective-permute-done.11.refs_1_, ...), custom_call_target="tpu_custom_call" | custom-call | flops 201326592 | bytes 393216 | tf_op jit(solution)/shard_map/attend/pallas_call | solution.py:255
  87.7 0.6 collective-permute-start.26
  88.2 1.9 %collective-permute-done.26.other_ref = bf16[8,128,384]{2,1,0:T(8,128)(2,1)S(1)} collective-permute-done((bf16[8,128,384]{2,1,0:T(8,128)(2,1)S(1)}, bf16[8,128,384]{2,1,0:T(8,128)(2,1)S(1)}, u32[]{:S(2)}, u32[]{:S(2)}) %collective-permute-start.26) | collective-permute-done | bytes 786464 | tf_op jit(solution)/shard_map/ppermute | solution.py:364
  90.3 1.3 %collective-permute-start.31 = (bf16[4,64,384]{2,1,0:T(8,128)(2,1)S(1)}, bf16[4,64,384]{2,1,0:T(8,128)(2,1)S(1)}, u32[]{:S(2)}, u32[]{:S(2)}) collective-permute-start(bf16[4,64,384]{2,1,0:T(8,128)(2,1)S(1)} %get-tuple-element.92), channel_id=1, source_target_pairs={{0,2},{1,3},{2,0},{3,1},{4,6},{5,7},{6,4},{7,5},{8,10},{9,11},{10,... | collective-permute-start | bytes 589832 | tf_op jit(solution)/shard_map/ppermute | solution.py:364
  91.6 0.8 collective-permute-start.27
  92.4 5.7 %collective-permute-done.31.other_ref = bf16[4,64,384]{2,1,0:T(8,128)(2,1)S(1)} collective-permute-done((bf16[4,64,384]{2,1,0:T(8,128)(2,1)S(1)}, bf16[4,64,384]{2,1,0:T(8,128)(2,1)S(1)}, u32[]{:S(2)}, u32[]{:S(2)}) %collective-permute-start.31) | collective-permute-done | bytes 196640 | tf_op jit(solution)/shard_map/ppermute | solution.py:364
  98.1 2.7 %collective-permute-start.32 = (bf16[64,384]{1,0:T(8,128)(2,1)S(1)}, bf16[64,384]{1,0:T(8,128)(2,1)S(1)}, u32[]{:S(2)}, u32[]{:S(2)}) collective-permute-start(bf16[64,384]{1,0:T(8,128)(2,1)S(1)} %get-tuple-element.94), channel_id=1, source_target_pairs={{0,8},{1,9},{2,10},{3,11},{4,12},{5,13},{6,14},{7,15},{8,0},{9,1},... | collective-permute-start | bytes 147464 | tf_op jit(solution)/shard_map/ppermute | solution.py:364
  100.8 1.3 %collective-permute-start.33 = (bf16[64,384]{1,0:T(8,128)(2,1)S(1)}, bf16[64,384]{1,0:T(8,128)(2,1)S(1)}, u32[]{:S(2)}, u32[]{:S(2)}) collective-permute-start(bf16[64,384]{1,0:T(8,128)(2,1)S(1)} %get-tuple-element.95), channel_id=1, source_target_pairs={{0,12},{1,13},{2,14},{3,15},{4,8},{5,9},{6,10},{7,11},{8,4},{9,5},... | collective-permute-start | bytes 147464 | tf_op jit(solution)/shard_map/ppermute | solution.py:364
  102.4 2.9 %collective-permute-start.28 = (bf16[64,384]{1,0:T(8,128)(2,1)S(1)}, bf16[64,384]{1,0:T(8,128)(2,1)S(1)}, u32[]{:S(2)}, u32[]{:S(2)}) collective-permute-start(bf16[64,384]{1,0:T(8,128)(2,1)S(1)} %get-tuple-element.89), channel_id=1, source_target_pairs={{0,8},{1,9},{2,10},{3,11},{4,12},{5,13},{6,14},{7,15},{8,0},{9,1},... | collective-permute-start | bytes 147464 | tf_op jit(solution)/shard_map/ppermute | solution.py:364
  105.3 1.3 %collective-permute-start.29 = (bf16[64,384]{1,0:T(8,128)(2,1)S(1)}, bf16[64,384]{1,0:T(8,128)(2,1)S(1)}, u32[]{:S(2)}, u32[]{:S(2)}) collective-permute-start(bf16[64,384]{1,0:T(8,128)(2,1)S(1)} %get-tuple-element.90), channel_id=1, source_target_pairs={{0,12},{1,13},{2,14},{3,15},{4,8},{5,9},{6,10},{7,11},{8,4},{9,5},... | collective-permute-start | bytes 147464 | tf_op jit(solution)/shard_map/ppermute | solution.py:364
  107.0 0.8 collective-permute-done.28.refs_1_
  107.8 3.5 %collective-permute-done.29.refs_2_ = bf16[64,384]{1,0:T(8,128)(2,1)S(1)} collective-permute-done((bf16[64,384]{1,0:T(8,128)(2,1)S(1)}, bf16[64,384]{1,0:T(8,128)(2,1)S(1)}, u32[]{:S(2)}, u32[]{:S(2)}) %collective-permute-start.29) | collective-permute-done | bytes 49184 | tf_op jit(solution)/shard_map/ppermute | solution.py:364
  111.3 0.7 finish.1
  (76 shorter events, 6.2 us)
Async XLA Ops:
  0.0 8.1 %copy-start.1 = (bf16[128,6144]{1,0:T(8,128)(2,1)S(1)}, bf16[128,6144]{1,0:T(8,128)(2,1)}, u32[]{:S(2)}) copy-start(bf16[128,6144]{1,0:T(8,128)(2,1)} %share_ref.1) | copy-start | bytes 4718596
  0.0 1.3 %copy-start.2 = (bf16[1024,384]{1,0:T(8,128)(2,1)S(1)}, bf16[1024,384]{1,0:T(8,128)(2,1)}, u32[]{:S(2)}) copy-start(bf16[1024,384]{1,0:T(8,128)(2,1)} %rows_ref.3) | copy-start | bytes 2359300
  1.3 0.7 copy-start.4
  2.0 6.1 %copy-start.6 = (f32[1,6144]{1,0:T(1,128)S(1)}, f32[1,6144]{1,0:T(1,128)}, u32[]{:S(2)}) copy-start(f32[1,6144]{1,0:T(1,128)} %param.11) | copy-start | bytes 73732
  2.4 12.5 %collective-permute-start.14 = (bf16[528,384]{1,0:T(8,128)(2,1)S(1)}, bf16[528,384]{1,0:T(8,128)(2,1)}, u32[]{:S(2)}, u32[]{:S(2)}) collective-permute-start(bf16[528,384]{1,0:T(8,128)(2,1)S(1)} %prepare.3.refs_0_), channel_id=1, source_target_pairs={{0,4},{1,5},{2,0},{3,1},{4,8},{5,9},{6,2},{7,3},{8,12},{9,13},{10,... | collective-permute-start | bytes 1216520 | tf_op jit(solution)/shard_map/ppermute | solution.py:361
  5.5 10.8 %collective-permute-start.15 = (bf16[528,384]{1,0:T(8,128)(2,1)S(1)}, bf16[528,384]{1,0:T(8,128)(2,1)S(1)}, u32[]{:S(2)}, u32[]{:S(2)}) collective-permute-start(bf16[528,384]{1,0:T(8,128)(2,1)S(1)} %prepare.3.refs_0_), channel_id=1, source_target_pairs={{0,2},{1,3},{2,6},{3,7},{4,0},{5,1},{6,10},{7,11},{8,4},{9,5},{10,... | collective-permute-start | bytes 1216520 | tf_op jit(solution)/shard_map/ppermute | solution.py:361
  5.5 13.6 %collective-permute-start.2 = (bf16[528,384]{1,0:T(8,128)(2,1)S(1)}, bf16[528,384]{1,0:T(8,128)(2,1)}, u32[]{:S(2)}, u32[]{:S(2)}) collective-permute-start(bf16[528,384]{1,0:T(8,128)(2,1)S(1)} %prepare.3.refs_0_), channel_id=1, source_target_pairs={{0,1},{1,0},{2,3},{3,2},{4,5},{5,4},{6,7},{7,6},{8,9},{9,8},{10,11... | collective-permute-start | bytes 1216520 | tf_op jit(solution)/shard_map/ppermute | solution.py:364
  5.5 6.6 %copy-start.3 = (bf16[1024,384]{1,0:T(8,128)(2,1)S(1)}, bf16[1024,384]{1,0:T(8,128)(2,1)}, u32[]{:S(2)}) copy-start(bf16[1024,384]{1,0:T(8,128)(2,1)} %rows_ref.3) | copy-start | bytes 2359300
  5.5 6.6 %copy-start.5 = (f32[6144]{0:T(1024)S(1)}, f32[6144]{0:T(1024)}, u32[]{:S(2)}) copy-start(f32[6144]{0:T(1024)} %param.9) | copy-start | bytes 73732
  8.1 11.5 %copy-start = (bf16[4,6144,256]{2,1,0:T(8,128)(2,1)S(1)}, bf16[4,6144,256]{2,1,0:T(8,128)(2,1)}, u32[]{:S(2)}) copy-start(bf16[4,6144,256]{2,1,0:T(8,128)(2,1)} %refs_3_.13) | copy-start | bytes 37748740
  12.5 12.3 %collective-permute-start = (bf16[528,384]{1,0:T(8,128)(2,1)S(1)}, bf16[528,384]{1,0:T(8,128)(2,1)S(1)}, u32[]{:S(2)}, u32[]{:S(2)}) collective-permute-start(bf16[528,384]{1,0:T(8,128)(2,1)S(1)} %prepare.2.refs_0_), channel_id=1, source_target_pairs={{0,4},{1,5},{2,0},{3,1},{4,8},{5,9},{6,2},{7,3},{8,12},{9,13},{10,... | collective-permute-start | bytes 1216520 | tf_op jit(solution)/shard_map/ppermute | solution.py:361
  14.6 12.2 %collective-permute-start.1 = (bf16[528,384]{1,0:T(8,128)(2,1)S(1)}, bf16[528,384]{1,0:T(8,128)(2,1)S(1)}, u32[]{:S(2)}, u32[]{:S(2)}) collective-permute-start(bf16[528,384]{1,0:T(8,128)(2,1)S(1)} %prepare.2.refs_0_), channel_id=1, source_target_pairs={{0,2},{1,3},{2,6},{3,7},{4,0},{5,1},{6,10},{7,11},{8,4},{9,5},{10,... | collective-permute-start | bytes 1216520 | tf_op jit(solution)/shard_map/ppermute | solution.py:361
  17.4 10.1 %collective-permute-start.18 = (bf16[1056,384]{1,0:T(8,128)(2,1)S(1)}, bf16[1056,384]{1,0:T(8,128)(2,1)S(1)}, u32[]{:S(2)}, u32[]{:S(2)}) collective-permute-start(bf16[1056,384]{1,0:T(8,128)(2,1)S(1)} %pad_maximum_fusion.3), channel_id=1, source_target_pairs={{0,1},{1,0},{2,3},{3,2},{4,5},{5,4},{6,7},{7,6},{8,9},{9,8},{10,11... | collective-permute-start | bytes 2433032 | tf_op jit(solution)/shard_map/ppermute | solution.py:364
  17.6 15.9 %collective-permute-start.16 = (bf16[528,384]{1,0:T(8,128)(2,1)}, bf16[528,384]{1,0:T(8,128)(2,1)S(1)}, u32[]{:S(2)}, u32[]{:S(2)}) collective-permute-start(bf16[528,384]{1,0:T(8,128)(2,1)} %collective-permute-done.14.refs_0_), channel_id=1, source_target_pairs={{0,4},{1,5},{2,0},{3,1},{4,8},{5,9},{6,2},{7,3},{8,12},{9,13},{10,... | collective-permute-start | bytes 1216520 | tf_op jit(solution)/shard_map/ppermute | solution.py:361
  19.1 16.2 %collective-permute-start.17 = (bf16[528,384]{1,0:T(8,128)(2,1)S(1)}, bf16[528,384]{1,0:T(8,128)(2,1)S(1)}, u32[]{:S(2)}, u32[]{:S(2)}) collective-permute-start(bf16[528,384]{1,0:T(8,128)(2,1)S(1)} %collective-permute-done.15.refs_1_), channel_id=1, source_target_pairs={{0,2},{1,3},{2,6},{3,7},{4,0},{5,1},{6,10},{7,11},{8,4},{9,5},{10,... | collective-permute-start | bytes 1216520 | tf_op jit(solution)/shard_map/ppermute | solution.py:361
  26.9 8.7 %collective-permute-start.6 = (bf16[1056,384]{1,0:T(8,128)(2,1)S(1)}, bf16[1056,384]{1,0:T(8,128)(2,1)S(1)}, u32[]{:S(2)}, u32[]{:S(2)}) collective-permute-start(bf16[1056,384]{1,0:T(8,128)(2,1)S(1)} %pad_maximum_fusion), channel_id=1, source_target_pairs={{0,1},{1,0},{2,3},{3,2},{4,5},{5,4},{6,7},{7,6},{8,9},{9,8},{10,11... | collective-permute-start | bytes 2433032 | tf_op jit(solution)/shard_map/ppermute | solution.py:364
  26.9 8.6 %collective-permute-start.5 = (bf16[528,384]{1,0:T(8,128)(2,1)S(1)}, bf16[528,384]{1,0:T(8,128)(2,1)S(1)}, u32[]{:S(2)}, u32[]{:S(2)}) collective-permute-start(bf16[528,384]{1,0:T(8,128)(2,1)S(1)} %prepare.2.refs_0_), channel_id=1, source_target_pairs={{0,1},{1,0},{2,3},{3,2},{4,5},{5,4},{6,7},{7,6},{8,9},{9,8},{10,11... | collective-permute-start | bytes 1216520 | tf_op jit(solution)/shard_map/ppermute | solution.py:364
  27.5 14.4 %collective-permute-start.3 = (bf16[528,384]{1,0:T(8,128)(2,1)S(1)}, bf16[528,384]{1,0:T(8,128)(2,1)S(1)}, u32[]{:S(2)}, u32[]{:S(2)}) collective-permute-start(bf16[528,384]{1,0:T(8,128)(2,1)S(1)} %collective-permute-done.refs_2_), channel_id=1, source_target_pairs={{0,4},{1,5},{2,0},{3,1},{4,8},{5,9},{6,2},{7,3},{8,12},{9,13},{10,... | collective-permute-start | bytes 1216520 | tf_op jit(solution)/shard_map/ppermute | solution.py:361
  33.5 10.9 %collective-permute-start.4 = (bf16[528,384]{1,0:T(8,128)(2,1)S(1)}, bf16[528,384]{1,0:T(8,128)(2,1)S(1)}, u32[]{:S(2)}, u32[]{:S(2)}) collective-permute-start(bf16[528,384]{1,0:T(8,128)(2,1)S(1)} %collective-permute-done.1.refs_3_), channel_id=1, source_target_pairs={{0,2},{1,3},{2,6},{3,7},{4,0},{5,1},{6,10},{7,11},{8,4},{9,5},{10,... | collective-permute-start | bytes 1216520 | tf_op jit(solution)/shard_map/ppermute | solution.py:361
  35.5 12.8 %collective-permute-start.21 = (bf16[1056,384]{1,0:T(8,128)(2,1)S(1)}, bf16[1056,384]{1,0:T(8,128)(2,1)S(1)}, u32[]{:S(2)}, u32[]{:S(2)}) collective-permute-start(bf16[1056,384]{1,0:T(8,128)(2,1)S(1)} %pad_maximum_fusion.4), channel_id=1, source_target_pairs={{0,1},{1,0},{2,3},{3,2},{4,5},{5,4},{6,7},{7,6},{8,9},{9,8},{10,11... | collective-permute-start | bytes 2433032 | tf_op jit(solution)/shard_map/ppermute | solution.py:364
  44.5 14.2 %collective-permute-start.9 = (bf16[1056,384]{1,0:T(8,128)(2,1)S(1)}, bf16[1056,384]{1,0:T(8,128)(2,1)S(1)}, u32[]{:S(2)}, u32[]{:S(2)}) collective-permute-start(bf16[1056,384]{1,0:T(8,128)(2,1)S(1)} %pad_maximum_fusion.1), channel_id=1, source_target_pairs={{0,1},{1,0},{2,3},{3,2},{4,5},{5,4},{6,7},{7,6},{8,9},{9,8},{10,11... | collective-permute-start | bytes 2433032 | tf_op jit(solution)/shard_map/ppermute | solution.py:364
  44.6 12.2 %collective-permute-start.19 = (bf16[528,384]{1,0:T(8,128)(2,1)S(1)}, bf16[528,384]{1,0:T(8,128)(2,1)S(1)}, u32[]{:S(2)}, u32[]{:S(2)}) collective-permute-start(bf16[528,384]{1,0:T(8,128)(2,1)S(1)} %collective-permute-done.16.refs_0_), channel_id=1, source_target_pairs={{0,4},{1,5},{2,0},{3,1},{4,8},{5,9},{6,2},{7,3},{8,12},{9,13},{10,... | collective-permute-start | bytes 1216520 | tf_op jit(solution)/shard_map/ppermute | solution.py:361
  46.3 12.2 %collective-permute-start.20 = (bf16[528,384]{1,0:T(8,128)(2,1)S(1)}, bf16[528,384]{1,0:T(8,128)(2,1)S(1)}, u32[]{:S(2)}, u32[]{:S(2)}) collective-permute-start(bf16[528,384]{1,0:T(8,128)(2,1)S(1)} %collective-permute-done.17.refs_1_), channel_id=1, source_target_pairs={{0,2},{1,3},{2,6},{3,7},{4,0},{5,1},{6,10},{7,11},{8,4},{9,5},{10,... | collective-permute-start | bytes 1216520 | tf_op jit(solution)/shard_map/ppermute | solution.py:361
  46.6 18.4 %collective-permute-start.7 = (bf16[528,384]{1,0:T(8,128)(2,1)S(1)}, bf16[528,384]{1,0:T(8,128)(2,1)S(1)}, u32[]{:S(2)}, u32[]{:S(2)}) collective-permute-start(bf16[528,384]{1,0:T(8,128)(2,1)S(1)} %collective-permute-done.3.refs_0_), channel_id=1, source_target_pairs={{0,4},{1,5},{2,0},{3,1},{4,8},{5,9},{6,2},{7,3},{8,12},{9,13},{10,... | collective-permute-start | bytes 1216520 | tf_op jit(solution)/shard_map/ppermute | solution.py:361
  48.3 18.1 %collective-permute-start.8 = (bf16[528,384]{1,0:T(8,128)(2,1)S(1)}, bf16[528,384]{1,0:T(8,128)(2,1)S(1)}, u32[]{:S(2)}, u32[]{:S(2)}) collective-permute-start(bf16[528,384]{1,0:T(8,128)(2,1)S(1)} %collective-permute-done.4.refs_1_), channel_id=1, source_target_pairs={{0,2},{1,3},{2,6},{3,7},{4,0},{5,1},{6,10},{7,11},{8,4},{9,5},{10,... | collective-permute-start | bytes 1216520 | tf_op jit(solution)/shard_map/ppermute | solution.py:361
  58.6 10.7 %collective-permute-start.24 = (bf16[1056,384]{1,0:T(8,128)(2,1)S(1)}, bf16[1056,384]{1,0:T(8,128)(2,1)S(1)}, u32[]{:S(2)}, u32[]{:S(2)}) collective-permute-start(bf16[1056,384]{1,0:T(8,128)(2,1)S(1)} %pad_maximum_fusion.5), channel_id=1, source_target_pairs={{0,1},{1,0},{2,3},{3,2},{4,5},{5,4},{6,7},{7,6},{8,9},{9,8},{10,11... | collective-permute-start | bytes 2433032 | tf_op jit(solution)/shard_map/ppermute | solution.py:364
  66.5 8.5 %collective-permute-start.12 = (bf16[1056,384]{1,0:T(8,128)(2,1)S(1)}, bf16[1056,384]{1,0:T(8,128)(2,1)S(1)}, u32[]{:S(2)}, u32[]{:S(2)}) collective-permute-start(bf16[1056,384]{1,0:T(8,128)(2,1)S(1)} %pad_maximum_fusion.2), channel_id=1, source_target_pairs={{0,1},{1,0},{2,3},{3,2},{4,5},{5,4},{6,7},{7,6},{8,9},{9,8},{10,11... | collective-permute-start | bytes 2433032 | tf_op jit(solution)/shard_map/ppermute | solution.py:364
  66.6 8.2 %collective-permute-start.23 = (bf16[272,384]{1,0:T(8,128)(2,1)S(1)}, bf16[272,384]{1,0:T(8,128)(2,1)S(1)}, u32[]{:S(2)}, u32[]{:S(2)}) collective-permute-start(bf16[272,384]{1,0:T(8,128)(2,1)S(1)} %slice.73), channel_id=1, source_target_pairs={{0,2},{1,3},{2,6},{3,7},{4,0},{5,1},{6,10},{7,11},{8,4},{9,5},{10,... | collective-permute-start | bytes 626696 | tf_op jit(solution)/shard_map/ppermute | solution.py:361
  67.0 7.8 %collective-permute-start.22 = (bf16[256,384]{1,0:T(8,128)(2,1)S(1)}, bf16[256,384]{1,0:T(8,128)(2,1)S(1)}, u32[]{:S(2)}, u32[]{:S(2)}) collective-permute-start(bf16[256,384]{1,0:T(8,128)(2,1)S(1)} %slice.72), channel_id=1, source_target_pairs={{0,4},{1,5},{2,0},{3,1},{4,8},{5,9},{6,2},{7,3},{8,12},{9,13},{10,... | collective-permute-start | bytes 589832 | tf_op jit(solution)/shard_map/ppermute | solution.py:361
  68.8 9.9 %collective-permute-start.11 = (bf16[272,384]{1,0:T(8,128)(2,1)S(1)}, bf16[272,384]{1,0:T(8,128)(2,1)S(1)}, u32[]{:S(2)}, u32[]{:S(2)}) collective-permute-start(bf16[272,384]{1,0:T(8,128)(2,1)S(1)} %slice.65), channel_id=1, source_target_pairs={{0,2},{1,3},{2,6},{3,7},{4,0},{5,1},{6,10},{7,11},{8,4},{9,5},{10,... | collective-permute-start | bytes 626696 | tf_op jit(solution)/shard_map/ppermute | solution.py:361
  69.2 9.1 %collective-permute-start.10 = (bf16[256,384]{1,0:T(8,128)(2,1)S(1)}, bf16[256,384]{1,0:T(8,128)(2,1)S(1)}, u32[]{:S(2)}, u32[]{:S(2)}) collective-permute-start(bf16[256,384]{1,0:T(8,128)(2,1)S(1)} %slice.64), channel_id=1, source_target_pairs={{0,4},{1,5},{2,0},{3,1},{4,8},{5,9},{6,2},{7,3},{8,12},{9,13},{10,... | collective-permute-start | bytes 589832 | tf_op jit(solution)/shard_map/ppermute | solution.py:361
  74.9 4.0 %collective-permute-start.25 = (bf16[528,384]{1,0:T(8,128)(2,1)S(1)}, bf16[528,384]{1,0:T(8,128)(2,1)S(1)}, u32[]{:S(2)}, u32[]{:S(2)}) collective-permute-start(bf16[528,384]{1,0:T(8,128)(2,1)S(1)} %pad_maximum_fusion.7), channel_id=1, source_target_pairs={{0,1},{1,0},{2,3},{3,2},{4,5},{5,4},{6,7},{7,6},{8,9},{9,8},{10,11... | collective-permute-start | bytes 1216520 | tf_op jit(solution)/shard_map/ppermute | solution.py:364
  78.7 3.6 %collective-permute-start.13 = (bf16[528,384]{1,0:T(8,128)(2,1)S(1)}, bf16[528,384]{1,0:T(8,128)(2,1)S(1)}, u32[]{:S(2)}, u32[]{:S(2)}) collective-permute-start(bf16[528,384]{1,0:T(8,128)(2,1)S(1)} %pad_maximum_fusion.6), channel_id=1, source_target_pairs={{0,1},{1,0},{2,3},{3,2},{4,5},{5,4},{6,7},{7,6},{8,9},{9,8},{10,11... | collective-permute-start | bytes 1216520 | tf_op jit(solution)/shard_map/ppermute | solution.py:364
  78.9 3.4 %slice-start = ((s8[6291456]{0:T(1024)(128)(4,1)}), s8[4194304]{0:T(1024)(128)(4,1)S(1)}, s32[]{:S(2)}) async-start(s8[6291456]{0:T(1024)(128)(4,1)} %bitcast.31), calls=%async_computation | async-start | bytes 8388608
  78.9 3.4 %slice-start.1 = ((s8[6291456]{0:T(1024)(128)(4,1)}), s8[2097152]{0:T(1024)(128)(4,1)S(1)}, s32[]{:S(2)}) async-start(s8[6291456]{0:T(1024)(128)(4,1)} %bitcast.31), calls=%async_computation.1 | async-start | bytes 4194304
  87.7 2.5 %collective-permute-start.26 = (bf16[8,128,384]{2,1,0:T(8,128)(2,1)S(1)}, bf16[8,128,384]{2,1,0:T(8,128)(2,1)S(1)}, u32[]{:S(2)}, u32[]{:S(2)}) collective-permute-start(bf16[8,128,384]{2,1,0:T(8,128)(2,1)S(1)} %get-tuple-element.85), channel_id=1, source_target_pairs={{0,1},{1,0},{2,3},{3,2},{4,5},{5,4},{6,7},{7,6},{8,9},{9,8},{10,11... | collective-permute-start | bytes 2359304 | tf_op jit(solution)/shard_map/ppermute | solution.py:364
  90.3 7.8 %collective-permute-start.31 = (bf16[4,64,384]{2,1,0:T(8,128)(2,1)S(1)}, bf16[4,64,384]{2,1,0:T(8,128)(2,1)S(1)}, u32[]{:S(2)}, u32[]{:S(2)}) collective-permute-start(bf16[4,64,384]{2,1,0:T(8,128)(2,1)S(1)} %get-tuple-element.92), channel_id=1, source_target_pairs={{0,2},{1,3},{2,0},{3,1},{4,6},{5,7},{6,4},{7,5},{8,10},{9,11},{10,... | collective-permute-start | bytes 589832 | tf_op jit(solution)/shard_map/ppermute | solution.py:364
  91.6 10.8 %collective-permute-start.27 = (bf16[4,64,384]{2,1,0:T(8,128)(2,1)S(1)}, bf16[4,64,384]{2,1,0:T(8,128)(2,1)S(1)}, u32[]{:S(2)}, u32[]{:S(2)}) collective-permute-start(bf16[4,64,384]{2,1,0:T(8,128)(2,1)S(1)} %get-tuple-element.87), channel_id=1, source_target_pairs={{0,2},{1,3},{2,0},{3,1},{4,6},{5,7},{6,4},{7,5},{8,10},{9,11},{10,... | collective-permute-start | bytes 589832 | tf_op jit(solution)/shard_map/ppermute | solution.py:364
  98.1 8.5 %collective-permute-start.32 = (bf16[64,384]{1,0:T(8,128)(2,1)S(1)}, bf16[64,384]{1,0:T(8,128)(2,1)S(1)}, u32[]{:S(2)}, u32[]{:S(2)}) collective-permute-start(bf16[64,384]{1,0:T(8,128)(2,1)S(1)} %get-tuple-element.94), channel_id=1, source_target_pairs={{0,8},{1,9},{2,10},{3,11},{4,12},{5,13},{6,14},{7,15},{8,0},{9,1},... | collective-permute-start | bytes 147464 | tf_op jit(solution)/shard_map/ppermute | solution.py:364
  100.8 6.2 %collective-permute-start.33 = (bf16[64,384]{1,0:T(8,128)(2,1)S(1)}, bf16[64,384]{1,0:T(8,128)(2,1)S(1)}, u32[]{:S(2)}, u32[]{:S(2)}) collective-permute-start(bf16[64,384]{1,0:T(8,128)(2,1)S(1)} %get-tuple-element.95), channel_id=1, source_target_pairs={{0,12},{1,13},{2,14},{3,15},{4,8},{5,9},{6,10},{7,11},{8,4},{9,5},... | collective-permute-start | bytes 147464 | tf_op jit(solution)/shard_map/ppermute | solution.py:364
  102.1 4.9 %collective-permute-start.34 = (bf16[64,384]{1,0:T(8,128)(2,1)S(1)}, bf16[64,384]{1,0:T(8,128)(2,1)S(1)}, u32[]{:S(2)}, u32[]{:S(2)}) collective-permute-start(bf16[64,384]{1,0:T(8,128)(2,1)S(1)} %get-tuple-element.96), channel_id=1, source_target_pairs={{0,4},{1,5},{2,6},{3,7},{4,0},{5,1},{6,2},{7,3},{8,12},{9,13},{10,... | collective-permute-start | bytes 147464 | tf_op jit(solution)/shard_map/ppermute | solution.py:364
  102.4 5.4 %collective-permute-start.28 = (bf16[64,384]{1,0:T(8,128)(2,1)S(1)}, bf16[64,384]{1,0:T(8,128)(2,1)S(1)}, u32[]{:S(2)}, u32[]{:S(2)}) collective-permute-start(bf16[64,384]{1,0:T(8,128)(2,1)S(1)} %get-tuple-element.89), channel_id=1, source_target_pairs={{0,8},{1,9},{2,10},{3,11},{4,12},{5,13},{6,14},{7,15},{8,0},{9,1},... | collective-permute-start | bytes 147464 | tf_op jit(solution)/shard_map/ppermute | solution.py:364
  105.3 6.0 %collective-permute-start.29 = (bf16[64,384]{1,0:T(8,128)(2,1)S(1)}, bf16[64,384]{1,0:T(8,128)(2,1)S(1)}, u32[]{:S(2)}, u32[]{:S(2)}) collective-permute-start(bf16[64,384]{1,0:T(8,128)(2,1)S(1)} %get-tuple-element.90), channel_id=1, source_target_pairs={{0,12},{1,13},{2,14},{3,15},{4,8},{5,9},{6,10},{7,11},{8,4},{9,5},... | collective-permute-start | bytes 147464 | tf_op jit(solution)/shard_map/ppermute | solution.py:364
  106.7 4.6 %collective-permute-start.30 = (bf16[64,384]{1,0:T(8,128)(2,1)S(1)}, bf16[64,384]{1,0:T(8,128)(2,1)S(1)}, u32[]{:S(2)}, u32[]{:S(2)}) collective-permute-start(bf16[64,384]{1,0:T(8,128)(2,1)S(1)} %get-tuple-element.91), channel_id=1, source_target_pairs={{0,4},{1,5},{2,6},{3,7},{4,0},{5,1},{6,2},{7,3},{8,12},{9,13},{10,... | collective-permute-start | bytes 147464 | tf_op jit(solution)/shard_map/ppermute | solution.py:364
